TPU v7x, 32 devices: a whole 2x2x4 slice. The times are simulated.
32 devices in a mesh: attn: 4 (over z), expert: 8 (over y, x, core).
Axes of the slice: x: 2, y: 2, z: 4, core: 2. Of those that a mesh axis runs over, the one named last changes fastest.
Arguments:
- stream_in: bfloat16 [256, 4096], P(('attn', 'expert')), may hold values from -48 to 48
- norm_gain: bfloat16 [4096], replicated, may hold values from 0.5 to 1.5
- expert_ids: int32 [256, 8], P(('attn', 'expert')), may hold values from 0 to 31, as said below
- route_weights: float32 [256, 8], P(('attn', 'expert')), may hold values from 0.1 to 1
- w_gate: bfloat16 [32, 1536, 4096], P('expert', 'attn'), may hold values from -0.09375 to 0.09375
- w_up: bfloat16 [32, 1536, 4096], P('expert', 'attn'), may hold values from -0.09375 to 0.09375
- w_down: bfloat16 [32, 1536, 4096], P('expert', 'attn'), may hold values from -0.15625 to 0.15625
Outputs:
- expert_mix: float32 [256, 4096], P(('attn', 'expert'))
Inputs may be any that keep to these rules, and one draw needn't show every extreme that they name: `expert_ids`: each row names 8 different experts; the tokens of one device name no expert more than 4 times, and one expert is named exactly 4 times by the tokens of every device.
All inputs are finite; a program needn't handle non-finite values.
Results may differ from a plain program's by a relative error of at most 0.014.
Values may be sent and summed in bfloat16 or wider, within the bound.
No kernel may reach another device: no remote copies, remote signals or barrier semaphores. Data moves between devices by JAX's collectives and lax.ppermute only.
A program may use at most 128 MiB of HBM per device.

v0:
```python
import jax
import jax.numpy as jnp
from jax import lax
from jax.sharding import PartitionSpec as P


def local(stream_in, norm_gain, expert_ids, route_weights, w_gate, w_up, w_down):
    row_count, feature_count = stream_in.shape
    top_count = expert_ids.shape[1]
    held_count = w_gate.shape[0]
    attn_size = lax.axis_size("attn")
    expert_size = lax.axis_size("expert")
    device_count = attn_size * expert_size
    expert_total = held_count * expert_size
    slot_count = 2 * row_count * top_count // expert_total
    stream = stream_in.astype(jnp.float32)
    inverse = lax.rsqrt(jnp.mean(stream * stream, axis=-1, keepdims=True) + 1e-06)
    normed = (stream * inverse * norm_gain.astype(jnp.float32)).astype(jnp.bfloat16)
    hit = expert_ids[:, :, None] == jnp.arange(expert_total, dtype=jnp.int32)[None, None, :]
    named = jnp.any(hit, axis=1).astype(jnp.int32)
    earlier = jnp.cumsum(named, axis=0) - named
    weight = jnp.sum(jnp.where(hit, route_weights[:, :, None], 0.0), axis=1)
    slot_range = jnp.arange(slot_count, dtype=jnp.int32)
    select = ((named[:, :, None] == 1) & (earlier[:, :, None] == slot_range[None, None, :])).astype(
        jnp.float32
    )
    select_flat = select.reshape(row_count, expert_total * slot_count)
    packed = jnp.einsum(
        "rk,rd->kd", select_flat.astype(jnp.bfloat16), normed, preferred_element_type=jnp.float32
    )
    packed = packed.astype(jnp.bfloat16).reshape(expert_size, held_count, slot_count, feature_count)
    copies = jnp.broadcast_to(packed[None], (attn_size,) + packed.shape)
    copies = copies.reshape(device_count, held_count, slot_count, feature_count)
    block = lax.all_to_all(copies, ("attn", "expert"), split_axis=0, concat_axis=0, tiled=True)
    gate = jnp.einsum("sjmd,jfd->sjmf", block, w_gate, preferred_element_type=jnp.float32)
    up = jnp.einsum("sjmd,jfd->sjmf", block, w_up, preferred_element_type=jnp.float32)
    hidden = (jax.nn.silu(gate) * up).astype(jnp.bfloat16)
    partial_out = jnp.einsum(
        "sjmf,jfd->sjmd", hidden, w_down, preferred_element_type=jnp.float32
    ).astype(jnp.bfloat16)
    returned = lax.all_to_all(
        partial_out, ("attn", "expert"), split_axis=0, concat_axis=0, tiled=True
    )
    returned = returned.reshape(attn_size, expert_total * slot_count, feature_count)
    results = jnp.sum(returned.astype(jnp.float32), axis=0)
    mixer = (select * weight[:, :, None]).reshape(row_count, expert_total * slot_count)
    return jnp.dot(
        mixer, results, precision=lax.Precision.HIGHEST, preferred_element_type=jnp.float32
    )


def solution(mesh):
    return jax.shard_map(
        local,
        mesh=mesh,
        in_specs=(
            P(("attn", "expert"), None),
            P(),
            P(("attn", "expert"), None),
            P(("attn", "expert"), None),
            P("expert", "attn", None),
            P("expert", "attn", None),
            P("expert", "attn", None),
        ),
        out_specs=P(("attn", "expert"), None),
        check_vma=False,
    )
```

profile of v0, /device:TPU:0, one launch (start us, length us, event | category | flops | bytes accessed | tf_op | source)
XLA Modules:
  0.0 251.3 jit_solution(12864610528381276522)
XLA Ops:
  0.0 0.8 fusion.53
  0.8 0.1 copy.15
  0.9 0.1 copy.14
  1.0 0.1 eq.53
  1.1 0.7 convert_element_type.52
  1.8 1.0 fusion.44
  2.9 0.1 compare_and_fusion
  2.9 1.3 convolution_convert_fusion
  4.3 0.4 broadcast_in_dim.18
  4.7 2.1 broadcast_in_dim.19
  6.8 100.8 %all_to_all.10 = bf16[32,4,4,4096]{3,2,1,0:T(4,128)(2,1)S(1)} all-to-all(bf16[32,4,4,4096]{3,2,1,0:T(4,128)(2,1)S(1)} %bitcast.46), channel_id=1, replica_groups=mesh['attn'=4,'expert'=8] {'attn','expert'}, dimensions={0} | all-to-all | bytes 8388608 | tf_op jit(solution)/shard_map/all_to_all | solution.py:34
  107.6 0.0 copy-start
  107.6 2.0 copy-done
  109.5 9.3 %fusion.14 = f32[32,4,4,384]{3,0,2,1:T(8,128)S(1)} fusion(bf16[4,384,4096]{2,1,0:T(8,128)(2,1)} %param.11, bf16[32,4,4,4096]{3,2,1,0:T(4,128)(2,1)S(1)} %all_to_all.10), kind=kOutput, calls=%fused_computation.11 | convolution fusion | flops 1610612736 | bytes 17563648 | tf_op jit(solution)/shard_map/sjmd,jfd->sjmf/dot_general | solution.py:35
  118.8 14.1 %fusion.9 = bf16[32,4,4,4096]{3,0,2,1:T(8,128)(2,1)} fusion(bf16[4,384,4096]{2,1,0:T(8,128)(2,1)} %param.13, bf16[4,384,4096]{2,1,0:T(8,128)(2,1)} %param.12, bf16[32,4,4,4096]{3,2,1,0:T(4,128)(2,1)} %copy-done, f32[32,4,4,384]{3,0,2,1:T(8,128)S(1)} %fusion.14), kind=kOutput, calls=%fused_computation.7 | convolution fusion | flops 3224502272 | bytes 34340864 | tf_op jit(solution)/shard_map/sjmf,jfd->sjmd/dot_general | solution.py:38
  132.9 7.4 %copy.19 = bf16[32,4,4,4096]{3,2,1,0:T(4,128)(2,1)} copy(bf16[32,4,4,4096]{3,0,2,1:T(8,128)(2,1)} %fusion.9) | data formatting | bytes 8388608 | tf_op jit(solution)/shard_map/convert_element_type | solution.py:40
  140.3 0.0 copy-start.1
  140.3 0.0 copy-start.2
  140.3 3.8 %all-to-all-start.1 = ((bf16[32,4,4,4096]{3,2,1,0:T(4,128)(2,1)}), bf16[32,4,4,4096]{3,2,1,0:T(4,128)(2,1)}, u32[]{:S(2)}, u32[]{:S(2)}) async-start(bf16[32,4,4,4096]{3,2,1,0:T(4,128)(2,1)} %copy.19), calls=%async_computation.1 | async-start | bytes 8388608 | tf_op jit(solution)/shard_map/all_to_all | solution.py:41
  144.1 0.0 copy-done.1
  144.2 0.0 copy-done.2
  144.2 0.1 select_reduce_fusion
  144.3 0.1 copy.16
  144.3 93.7 %all-to-all-done.1 = bf16[32,4,4,4096]{3,2,1,0:T(4,128)(2,1)} async-done(((bf16[32,4,4,4096]{3,2,1,0:T(4,128)(2,1)}), bf16[32,4,4,4096]{3,2,1,0:T(4,128)(2,1)}, u32[]{:S(2)}, u32[]{:S(2)}) %all-to-all-start.1) | async-done | bytes 4194336 | tf_op jit(solution)/shard_map/all_to_all | solution.py:41
  238.0 7.3 %reshape.45 = f32[4,128,4096]{2,1,0:T(8,128)} reshape(bf16[32,4,4,4096]{3,2,1,0:T(4,128)(2,1)} %all-to-all-done.1) | data formatting | bytes 12582912 | tf_op jit(solution)/shard_map/convert_element_type | solution.py:45
  245.3 4.2 %reduce_sum.29 = f32[128,4096]{1,0:T(8,128)S(1)} reduce(f32[4,128,4096]{2,1,0:T(8,128)} %reshape.45, f32[]{:T(128)} %constant.15.clone.1), dimensions={0}, to_apply=%region_4.5 | reduce | flops 1572864 | bytes 10485764 | tf_op jit(solution)/shard_map/reduce_sum | solution.py:45
  249.5 1.8 fusion.50
  (8 shorter events, 0.1 us)
Async XLA Ops:
  107.6 2.0 copy-start
  140.3 3.9 %copy-start.1 = (s32[8,8]{1,0:T(8,128)S(1)}, s32[8,8]{1,0:T(8,128)}, u32[]{:S(2)}) copy-start(s32[8,8]{1,0:T(8,128)} %param.9) | copy-start | bytes 772
  140.3 3.9 %copy-start.2 = (f32[8,8]{1,0:T(8,128)S(1)}, f32[8,8]{1,0:T(8,128)}, u32[]{:S(2)}) copy-start(f32[8,8]{1,0:T(8,128)} %param.10) | copy-start | bytes 772
  140.3 97.7 %all-to-all-start.1 = ((bf16[32,4,4,4096]{3,2,1,0:T(4,128)(2,1)}), bf16[32,4,4,4096]{3,2,1,0:T(4,128)(2,1)}, u32[]{:S(2)}, u32[]{:S(2)}) async-start(bf16[32,4,4,4096]{3,2,1,0:T(4,128)(2,1)} %copy.19), calls=%async_computation.1 | async-start | bytes 8388608 | tf_op jit(solution)/shard_map/all_to_all | solution.py:41
where the time goes:
time: 252 us; the launch traced here: 251 us
  blocking collectives  101 us (40%)
  waiting for transfers between devices  93.7 us (37%)
  matrix products  26.4 us (10%)
  local copies, waits for them, and re-layouts  19.6 us (8%)
  other arithmetic  6.88 us (3%)
  starting transfers between devices  3.84 us (2%)
    all_to_all x1, blocking collectives, local(): lax.all_to_all(copies, ('attn', 'expert'), split_axis=0, concat_axis=0, t...  101 us
    all_to_all x1, waiting for transfers between devices, local(): lax.all_to_all(partial_out, ('attn', 'expert'), split_axis=0, concat_axis...  93.7 us
    dot_general x1, matrix products, local(): jnp.einsum('sjmf,jfd->sjmd', hidden, w_down, preferred_element_type=jnp.f...  14.1 us
    dot_general x1, matrix products, local(): jnp.einsum('sjmd,jfd->sjmf', block, w_gate, preferred_element_type=jnp.fl...  9.27 us
    convert_element_type x1, local copies, waits for them, and re-layouts, local(): partial_out = jnp.einsum('sjmf,jfd->sjmd', hidden, w_down, preferred_elem...  7.39 us
    convert_element_type x1, local copies, waits for them, and re-layouts, local(): results = jnp.sum(returned.astype(jnp.float32), axis=0)  7.26 us
  transfers between devices with their start and end apart: 1, of which 1 were waited for; matrix products, arithmetic and copies ran while one was open for 0% of the time, Pallas kernels for 0%

commit v1 on v0

v1 whole, which is shorter than its diff:
```python
import jax
import jax.numpy as jnp
from jax import lax
from jax.experimental import pallas as pl
from jax.experimental.pallas import tpu as pltpu
from jax.sharding import PartitionSpec as P

LANES = 128
F32 = jnp.float32
BF16 = jnp.bfloat16
MIB = 1 << 20


def whole(shape):
    return pl.BlockSpec(shape, lambda *_: (0,) * len(shape))


def swap(value, axis, distance):
    size = lax.axis_size(axis)
    return lax.ppermute(value, axis, [(i, i ^ distance) for i in range(size)])


def pack_kernel(stream_ref, gain_ref, ids_ref, weights_ref, out_ref, *, experts, features):
    stream = stream_ref[...].astype(F32)
    inverse = lax.rsqrt(jnp.mean(stream * stream, axis=-1, keepdims=True) + 1e-06)
    normed = stream * inverse * gain_ref[...].astype(F32)
    out_ref[:, :features] = normed.astype(BF16)
    rows = stream.shape[0]
    width = out_ref.shape[1] - features
    column = lax.broadcasted_iota(jnp.int32, (rows, width), 1)
    dense = jnp.zeros((rows, width), F32)
    for k in range(ids_ref.shape[1]):
        expert = ids_ref[:, k : k + 1]
        weight = weights_ref[:, k : k + 1]
        high = weight.astype(BF16).astype(F32)
        middle = (weight - high).astype(BF16).astype(F32)
        low = weight - high - middle
        dense = dense + jnp.where(column == expert, high, 0.0)
        dense = dense + jnp.where(column == expert + experts, middle, 0.0)
        dense = dense + jnp.where(column == expert + 2 * experts, low, 0.0)
    out_ref[:, features:] = dense.astype(BF16)


def hidden_kernel(*refs, pieces, features):
    piece_refs = refs[:pieces]
    gate_ref, up_ref, spread_ref, act_ref, rows_ref = refs[pieces:]
    step = pl.program_id(0)
    count = piece_refs[0].shape[0]

    @pl.when(step == 0)
    def _():
        for i, ref in enumerate(piece_refs):
            rows_ref[i * count : (i + 1) * count, :] = ref[...]

    rows = rows_ref[:, :features]
    matrix = jnp.concatenate([gate_ref[...], up_ref[...]], axis=0)
    both = lax.dot_general(rows, matrix, (((1,), (1,)), ((), ())), preferred_element_type=F32)
    weight = jnp.dot(rows_ref[:, features:], spread_ref[...], preferred_element_type=F32)
    block = gate_ref.shape[0]
    gate, up = both[:, :block], both[:, block:]
    act_ref[...] = (gate / (1.0 + jnp.exp(-gate)) * up * weight).astype(BF16)


def down_kernel(act_ref, down_ref, keep_ref, send_ref):
    out = jnp.dot(act_ref[...], down_ref[...], preferred_element_type=F32)
    half = keep_ref.shape[0]
    keep_ref[...] = out[:half]
    send_ref[...] = out[half:].astype(BF16)


def local(stream_in, norm_gain, expert_ids, route_weights, w_gate, w_up, w_down):
    row_count, features = stream_in.shape
    held, slice_size, _ = w_gate.shape
    attn_size = lax.axis_size("attn")
    expert_size = lax.axis_size("expert")
    experts = held * expert_size
    planes = expert_size // 2
    width = -(-3 * experts // LANES) * LANES
    hidden = held * slice_size

    packed = pl.pallas_call(
        lambda *refs: pack_kernel(*refs, experts=experts, features=features),
        out_shape=jax.ShapeDtypeStruct((row_count, features + width), BF16),
    )(stream_in, norm_gain.reshape(1, features), expert_ids, route_weights)

    column = jnp.concatenate([packed] + [swap(packed, "attn", d) for d in range(1, attn_size)], axis=0)
    pieces = [column] + [swap(column, "expert", 2 * d) for d in range(1, planes)]
    pieces = pieces + [swap(piece, "expert", 1) for piece in pieces]
    tokens = len(pieces) * column.shape[0]

    first = lax.axis_index("expert") * held
    lane = jnp.arange(width, dtype=jnp.int32)[:, None]
    owner = first + jnp.arange(hidden, dtype=jnp.int32)[None, :] // slice_size
    spread = ((lane % experts == owner) & (lane < 3 * experts)).astype(BF16)

    block = LANES
    act = pl.pallas_call(
        lambda *refs: hidden_kernel(*refs, pieces=len(pieces), features=features),
        out_shape=jax.ShapeDtypeStruct((tokens, hidden), BF16),
        grid=(hidden // block,),
        in_specs=[whole(column.shape)] * len(pieces)
        + [
            pl.BlockSpec((block, features), lambda j: (j, 0)),
            pl.BlockSpec((block, features), lambda j: (j, 0)),
            pl.BlockSpec((width, block), lambda j: (0, j)),
        ],
        out_specs=pl.BlockSpec((tokens, block), lambda j: (0, j)),
        scratch_shapes=[pltpu.VMEM((tokens, features + width), BF16)],
        compiler_params=pltpu.CompilerParams(vmem_limit_bytes=56 * MIB),
    )(*pieces, w_gate.reshape(hidden, features), w_up.reshape(hidden, features), spread)

    chunk = 512
    keep, send = pl.pallas_call(
        down_kernel,
        out_shape=(
            jax.ShapeDtypeStruct((tokens // 2, features), F32),
            jax.ShapeDtypeStruct((tokens // 2, features), BF16),
        ),
        grid=(features // chunk,),
        in_specs=[
            whole((tokens, hidden)),
            pl.BlockSpec((hidden, chunk), lambda j: (0, j)),
        ],
        out_specs=[
            pl.BlockSpec((tokens // 2, chunk), lambda j: (0, j)),
            pl.BlockSpec((tokens // 2, chunk), lambda j: (0, j)),
        ],
        compiler_params=pltpu.CompilerParams(vmem_limit_bytes=56 * MIB),
    )(act, w_down.reshape(hidden, features))

    total = keep + swap(send, "expert", 1).astype(F32)
    total = total.reshape(planes, attn_size * row_count, features)
    parts = [swap(total[d].astype(BF16), "expert", 2 * d) for d in range(1, planes)]
    total = sum([part.astype(F32) for part in parts], total[0])
    total = total.reshape(attn_size, row_count, features)
    parts = [swap(total[d].astype(BF16), "attn", d) for d in range(1, attn_size)]
    return sum([part.astype(F32) for part in parts], total[0])


def solution(mesh):
    return jax.shard_map(
        local,
        mesh=mesh,
        in_specs=(
            P(("attn", "expert"), None),
            P(),
            P(("attn", "expert"), None),
            P(("attn", "expert"), None),
            P("expert", "attn", None),
            P("expert", "attn", None),
            P("expert", "attn", None),
        ),
        out_specs=P(("attn", "expert"), None),
        check_vma=False,
    )
```

time: 252 us -> 90.9 us (0.36)
  blocking collectives: 101 us -> 0 us
  waiting for transfers between devices: 93.7 us -> 37.4 us
  Pallas kernels: 0 us -> 29.3 us
  matrix products: 26.4 us -> 0 us
  local copies, waits for them, and re-layouts: 19.6 us -> 2.07 us
  starting transfers between devices: 3.84 us -> 16.7 us
    all_to_all x1 -> x0, blocking collectives: 101 us -> none  [local(): lax.all_to_all(copies, ('attn', 'expert'), split_axis=0, concat_axis=0, t...]
    all_to_all x1 -> x0, waiting for transfers between devices: 93.7 us -> none  [local(): lax.all_to_all(partial_out, ('attn', 'expert'), split_axis=0, concat_axis...]
    ppermute x0 -> x17, waiting for transfers between devices: none -> 37.4 us  [swap(): return lax.ppermute(value, axis, [(i, i ^ distance) for i in range(size)])]
    pallas_call x0 -> x3, Pallas kernels: none -> 29.3 us  [the longest x1 17.4 us: local(): pl.pallas_call(lambda *refs: hidden_kernel(*refs, pieces=len(pieces), fea...]
    dot_general x4 -> x0, matrix products: 26.4 us -> none  [the longest x1 14.1 us: local(): jnp.einsum('sjmf,jfd->sjmd', hidden, w_down, preferred_element_type=jnp.f...]
    ppermute x0 -> x17, starting transfers between devices: none -> 16.7 us  [swap(): return lax.ppermute(value, axis, [(i, i ^ distance) for i in range(size)])]
    convert_element_type x2 -> x0, local copies, waits for them, and re-layouts: 14.7 us -> none  [the longest x1 7.39 us: local(): partial_out = jnp.einsum('sjmf,jfd->sjmd', hidden, w_down, preferred_elem...]
    reduce_sum x3 -> x0, other arithmetic: 5.26 us -> none  [the longest x1 4.18 us: local(): results = jnp.sum(returned.astype(jnp.float32), axis=0)]
  transfers between devices with their start and end apart: 1 -> 17, of which waited for: 1 -> 14; matrix products, arithmetic and copies ran while one was open for 0% -> 1% of each run, Pallas kernels for 0% -> 0%
where the time goes in v1:
time: 90.9 us; the launch traced here: 90.2 us
  waiting for transfers between devices  37.4 us (41%)
  Pallas kernels  29.3 us (32%)
  starting transfers between devices  16.7 us (18%)
  other arithmetic  4.63 us (5%)
  local copies, waits for them, and re-layouts  2.07 us (2%)
    ppermute x17, waiting for transfers between devices, swap(): return lax.ppermute(value, axis, [(i, i ^ distance) for i in range(size)])  37.4 us
    pallas_call x1, Pallas kernels, local(): pl.pallas_call(lambda *refs: hidden_kernel(*refs, pieces=len(pieces), fea...  17.4 us
    ppermute x17, starting transfers between devices, swap(): return lax.ppermute(value, axis, [(i, i ^ distance) for i in range(size)])  16.7 us
    pallas_call x1, Pallas kernels, local(): pl.pallas_call(down_kernel, out_shape=(jax.ShapeDtypeStruct((tokens // 2,...  10.3 us
    another operation x2, other arithmetic  2.06 us
  transfers between devices with their start and end apart: 17, of which 14 were waited for; matrix products, arithmetic and copies ran while one was open for 1% of the time, Pallas kernels for 0%

profile of v1, /device:TPU:0, one launch (start us, length us, event | category | flops | bytes accessed | tf_op | source)
XLA Modules:
  0.0 90.2 jit_solution(14020597017464499885)
XLA Ops:
  0.0 1.3 %reshape.75.refs_1_ = bf16[1,4096]{1,0:T(2,128)(2,1)} reshape(bf16[4096]{0:T(1024)(128)(2,1)} %param.8) | data formatting | bytes 16384 | tf_op jit(solution)/shard_map/reshape | solution.py:84
  1.3 1.6 %shard_map.73 = bf16[8,4224]{1,0:T(8,128)(2,1)} custom-call(bf16[8,4096]{1,0:T(8,128)(2,1)} %refs_0_.1, bf16[1,4096]{1,0:T(2,128)(2,1)} %reshape.75.refs_1_, s32[8,8]{1,0:T(8,128)} %refs_2_.1, f32[8,8]{1,0:T(8,128)} %refs_3_.1), custom_call_target="tpu_custom_call" | custom-call | tf_op jit(solution)/shard_map/pallas_call | solution.py:81
  2.9 5.0 %collective-permute-start.2 = (bf16[8,4224]{1,0:T(8,128)(2,1)}, bf16[8,4224]{1,0:T(8,128)(2,1)S(1)}, u32[]{:S(2)}, u32[]{:S(2)}) collective-permute-start(bf16[8,4224]{1,0:T(8,128)(2,1)} %shard_map.73), channel_id=1, source_target_pairs={{0,24},{8,16},{16,8},{24,0},{1,25},{9,17},{17,9},{25,1},{2,26},{10... | collective-permute-start | bytes 202760 | tf_op jit(solution)/shard_map/ppermute | solution.py:20
  8.0 0.0 collective-permute-start.1
  8.0 0.6 collective-permute-start
  8.6 2.3 %collective-permute-done.2 = bf16[8,4224]{1,0:T(8,128)(2,1)S(1)} collective-permute-done((bf16[8,4224]{1,0:T(8,128)(2,1)}, bf16[8,4224]{1,0:T(8,128)(2,1)S(1)}, u32[]{:S(2)}, u32[]{:S(2)}) %collective-permute-start.2) | collective-permute-done | bytes 67616 | tf_op jit(solution)/shard_map/ppermute | solution.py:20
  10.8 3.1 %collective-permute-done.1 = bf16[8,4224]{1,0:T(8,128)(2,1)S(1)} collective-permute-done((bf16[8,4224]{1,0:T(8,128)(2,1)}, bf16[8,4224]{1,0:T(8,128)(2,1)S(1)}, u32[]{:S(2)}, u32[]{:S(2)}) %collective-permute-start.1) | collective-permute-done | bytes 67616 | tf_op jit(solution)/shard_map/ppermute | solution.py:20
  14.0 0.0 collective-permute-done
  14.0 0.9 %pad_maximum_fusion.refs_0_ = bf16[32,4224]{1,0:T(8,128)(2,1)S(1)} fusion(bf16[8,4224]{1,0:T(8,128)(2,1)S(1)} %collective-permute-done.2, bf16[8,4224]{1,0:T(8,128)(2,1)S(1)} %collective-permute-done.1, bf16[8,4224]{1,0:T(8,128)(2,1)S(1)} %collective-permute-done, bf16[8,4224]{1,0:T(8,128)(2,1)} %shard_map.73), kind=kLoop, calls=%fused_computation.5 | loop fusion | flops 1081344 | bytes 540672 | tf_op jit(solution)/shard_map/concatenate | solution.py:86
  14.9 0.0 copy-start
  14.9 2.5 %collective-permute-start.5 = (bf16[32,4224]{1,0:T(8,128)(2,1)S(1)}, bf16[32,4224]{1,0:T(8,128)(2,1)S(1)}, u32[]{:S(2)}, u32[]{:S(2)}) collective-permute-start(bf16[32,4224]{1,0:T(8,128)(2,1)S(1)} %pad_maximum_fusion.refs_0_), channel_id=1, source_target_pairs={{0,6},{1,7},{2,4},{3,5},{4,2},{5,3},{6,0},{7,1},{8,14},{9,15},{10,... | collective-permute-start | bytes 811016 | tf_op jit(solution)/shard_map/ppermute | solution.py:20
  17.4 0.5 collective-permute-start.4
  17.9 0.5 collective-permute-start.3
  18.4 0.1 collective-permute-start.6
  18.5 6.8 %collective-permute-done.5.refs_3_ = bf16[32,4224]{1,0:T(8,128)(2,1)S(1)} collective-permute-done((bf16[32,4224]{1,0:T(8,128)(2,1)S(1)}, bf16[32,4224]{1,0:T(8,128)(2,1)S(1)}, u32[]{:S(2)}, u32[]{:S(2)}) %collective-permute-start.5) | collective-permute-done | bytes 270368 | tf_op jit(solution)/shard_map/ppermute | solution.py:20
  25.3 0.0 copy-start.1
  25.3 0.0 collective-permute-start.9
  25.3 4.4 %collective-permute-done.4.refs_2_ = bf16[32,4224]{1,0:T(8,128)(2,1)S(1)} collective-permute-done((bf16[32,4224]{1,0:T(8,128)(2,1)S(1)}, bf16[32,4224]{1,0:T(8,128)(2,1)S(1)}, u32[]{:S(2)}, u32[]{:S(2)}) %collective-permute-start.4) | collective-permute-done | bytes 270368 | tf_op jit(solution)/shard_map/ppermute | solution.py:20
  29.7 0.0 copy-start.2
  29.7 0.0 collective-permute-start.8
  29.7 0.3 collective-permute-done.3.refs_1_
  30.0 0.0 copy-start.3
  30.0 0.2 collective-permute-start.7
  30.2 1.0 %and_convert_fusion.refs_10_ = bf16[128,1536]{1,0:T(8,128)(2,1)} fusion(s32[1536]{0:T(1024)S(1)} %fusion.4, s32[128]{0:T(128)S(1)} %and_select_fusion, pred[128]{0:T(512)(128)(4,1)S(1)} %iota_compare_fusion), kind=kLoop, calls=%fused_computation.1 | loop fusion | flops 589824 | bytes 400000 | tf_op jit(solution)/shard_map/convert_element_type | solution.py:94
  31.1 0.0 collective-permute-done.6.refs_4_
  31.2 0.0 copy-start.4
  31.2 0.0 collective-permute-done.9.refs_7_
  31.2 0.0 copy-start.5
  31.2 0.1 collective-permute-done.8.refs_6_
  31.2 0.0 copy-start.6
  31.2 0.4 collective-permute-done.7.refs_5_
  31.6 0.0 copy-start.7
  31.6 0.0 copy-done
  31.6 0.0 copy-done.1
  31.6 0.0 copy-done.2
  31.6 0.0 copy-done.3
  31.6 0.2 copy-done.4
  31.9 0.1 copy-done.5
  32.0 0.1 copy-done.6
  32.1 0.2 copy-done.7
  32.3 17.4 %shard_map.74.act_ref = bf16[256,1536]{1,0:T(8,128)(2,1)} custom-call(bf16[32,4224]{1,0:T(8,128)(2,1)} %copy-done, bf16[32,4224]{1,0:T(8,128)(2,1)} %copy-done.3, bf16[32,4224]{1,0:T(8,128)(2,1)} %copy-done.2, bf16[32,4224]{1,0:T(8,128)(2,1)} %copy-done.1, bf16[32,4224]{1,0:T(8,128)(2,1)} %copy-done.4, bf16[32,4224]{1,0:T(8,128)(2,1)} %copy-done.7, ...), custom_call_target="tpu_custom_call" | custom-call | tf_op jit(solution)/shard_map/pallas_call | solution.py:97
  49.7 10.3 %shard_map.75 = (f32[128,4096]{1,0:T(8,128)}, bf16[128,4096]{1,0:T(8,128)(2,1)}) custom-call(bf16[256,1536]{1,0:T(8,128)(2,1)} %shard_map.74.act_ref, bf16[1536,4096]{1,0:T(8,128)(2,1)} %bitcast.5), custom_call_target="tpu_custom_call" | custom-call | tf_op jit(solution)/shard_map/pallas_call | solution.py:113
  60.0 0.1 collective-permute-start.10
  60.1 2.7 %collective-permute-done.10 = bf16[128,4096]{1,0:T(8,128)(2,1)S(1)} collective-permute-done((bf16[128,4096]{1,0:T(8,128)(2,1)}, bf16[128,4096]{1,0:T(8,128)(2,1)S(1)}, u32[]{:S(2)}, u32[]{:S(2)}) %collective-permute-start.10) | collective-permute-done | bytes 1048608 | tf_op jit(solution)/shard_map/ppermute | solution.py:20
  62.9 1.9 %fusion.10 = (bf16[128,4096]{1,0:T(8,128)(2,1)S(1)}, f32[128,4096]{1,0:T(8,128)S(1)}) fusion(f32[128,4096]{1,0:T(8,128)} %get-tuple-element.7, bf16[128,4096]{1,0:T(8,128)(2,1)S(1)} %collective-permute-done.10), kind=kLoop, calls=%fused_computation.20 | loop fusion | flops 1572864 | bytes 6291456 | tf_op jit(solution)/shard_map/convert.5
  64.8 0.1 fusion.11
  64.8 1.7 %collective-permute-start.11 = (bf16[32,4096]{1,0:T(8,128)(2,1)S(1)}, bf16[32,4096]{1,0:T(8,128)(2,1)S(1)}, u32[]{:S(2)}, u32[]{:S(2)}) collective-permute-start(bf16[32,4096]{1,0:T(8,128)(2,1)S(1)} %get-tuple-element.13), channel_id=1, source_target_pairs={{0,2},{1,3},{2,0},{3,1},{4,6},{5,7},{6,4},{7,5},{8,10},{9,11},{10,... | collective-permute-start | bytes 786440 | tf_op jit(solution)/shard_map/ppermute | solution.py:20
  66.6 1.5 %collective-permute-start.13 = (bf16[32,4096]{1,0:T(8,128)(2,1)S(1)}, bf16[32,4096]{1,0:T(8,128)(2,1)S(1)}, u32[]{:S(2)}, u32[]{:S(2)}) collective-permute-start(bf16[32,4096]{1,0:T(8,128)(2,1)S(1)} %get-tuple-element.14), channel_id=1, source_target_pairs={{0,6},{1,7},{2,4},{3,5},{4,2},{5,3},{6,0},{7,1},{8,14},{9,15},{10,... | collective-permute-start | bytes 786440 | tf_op jit(solution)/shard_map/ppermute | solution.py:20
  68.1 0.3 collective-permute-start.12
  68.4 5.7 %collective-permute-done.11 = bf16[32,4096]{1,0:T(8,128)(2,1)S(1)} collective-permute-done((bf16[32,4096]{1,0:T(8,128)(2,1)S(1)}, bf16[32,4096]{1,0:T(8,128)(2,1)S(1)}, u32[]{:S(2)}, u32[]{:S(2)}) %collective-permute-start.11) | collective-permute-done | bytes 262176 | tf_op jit(solution)/shard_map/ppermute | solution.py:20
  74.1 6.1 %collective-permute-done.13 = bf16[32,4096]{1,0:T(8,128)(2,1)S(1)} collective-permute-done((bf16[32,4096]{1,0:T(8,128)(2,1)S(1)}, bf16[32,4096]{1,0:T(8,128)(2,1)S(1)}, u32[]{:S(2)}, u32[]{:S(2)}) %collective-permute-start.13) | collective-permute-done | bytes 262176 | tf_op jit(solution)/shard_map/ppermute | solution.py:20
  80.1 1.4 %collective-permute-done.12 = bf16[32,4096]{1,0:T(8,128)(2,1)S(1)} collective-permute-done((bf16[32,4096]{1,0:T(8,128)(2,1)S(1)}, bf16[32,4096]{1,0:T(8,128)(2,1)S(1)}, u32[]{:S(2)}, u32[]{:S(2)}) %collective-permute-start.12) | collective-permute-done | bytes 262176 | tf_op jit(solution)/shard_map/ppermute | solution.py:20
  81.5 0.1 fusion.8
  81.7 0.1 collective-permute-start.14
  81.7 1.5 %collective-permute-start.16 = (bf16[8,4096]{1,0:T(8,128)(2,1)S(1)}, bf16[8,4096]{1,0:T(8,128)(2,1)S(1)}, u32[]{:S(2)}, u32[]{:S(2)}) collective-permute-start(bf16[8,4096]{1,0:T(8,128)(2,1)S(1)} %get-tuple-element.17), channel_id=1, source_target_pairs={{0,24},{8,16},{16,8},{24,0},{1,25},{9,17},{17,9},{25,1},{2,26},{10... | collective-permute-start | bytes 196616 | tf_op jit(solution)/shard_map/ppermute | solution.py:20
  83.2 2.0 %collective-permute-start.15 = (bf16[8,4096]{1,0:T(8,128)(2,1)S(1)}, bf16[8,4096]{1,0:T(8,128)(2,1)S(1)}, u32[]{:S(2)}, u32[]{:S(2)}) collective-permute-start(bf16[8,4096]{1,0:T(8,128)(2,1)S(1)} %get-tuple-element.18), channel_id=1, source_target_pairs={{0,16},{8,24},{16,0},{24,8},{1,17},{9,25},{17,1},{25,9},{2,18},{10... | collective-permute-start | bytes 196616 | tf_op jit(solution)/shard_map/ppermute | solution.py:20
  85.2 1.2 %collective-permute-done.14 = bf16[8,4096]{1,0:T(8,128)(2,1)S(1)} collective-permute-done((bf16[8,4096]{1,0:T(8,128)(2,1)S(1)}, bf16[8,4096]{1,0:T(8,128)(2,1)S(1)}, u32[]{:S(2)}, u32[]{:S(2)}) %collective-permute-start.14) | collective-permute-done | bytes 65568 | tf_op jit(solution)/shard_map/ppermute | solution.py:20
  86.4 1.6 %collective-permute-done.16 = bf16[8,4096]{1,0:T(8,128)(2,1)S(1)} collective-permute-done((bf16[8,4096]{1,0:T(8,128)(2,1)S(1)}, bf16[8,4096]{1,0:T(8,128)(2,1)S(1)}, u32[]{:S(2)}, u32[]{:S(2)}) %collective-permute-start.16) | collective-permute-done | bytes 65568 | tf_op jit(solution)/shard_map/ppermute | solution.py:20
  88.0 1.6 %collective-permute-done.15 = bf16[8,4096]{1,0:T(8,128)(2,1)S(1)} collective-permute-done((bf16[8,4096]{1,0:T(8,128)(2,1)S(1)}, bf16[8,4096]{1,0:T(8,128)(2,1)S(1)}, u32[]{:S(2)}, u32[]{:S(2)}) %collective-permute-start.15) | collective-permute-done | bytes 65568 | tf_op jit(solution)/shard_map/ppermute | solution.py:20
  89.6 0.7 fusion.3
  (4 shorter events, 0.0 us)
Async XLA Ops:
  2.9 7.9 %collective-permute-start.2 = (bf16[8,4224]{1,0:T(8,128)(2,1)}, bf16[8,4224]{1,0:T(8,128)(2,1)S(1)}, u32[]{:S(2)}, u32[]{:S(2)}) collective-permute-start(bf16[8,4224]{1,0:T(8,128)(2,1)} %shard_map.73), channel_id=1, source_target_pairs={{0,24},{8,16},{16,8},{24,0},{1,25},{9,17},{17,9},{25,1},{2,26},{10... | collective-permute-start | bytes 202760 | tf_op jit(solution)/shard_map/ppermute | solution.py:20
  8.0 6.0 %collective-permute-start.1 = (bf16[8,4224]{1,0:T(8,128)(2,1)}, bf16[8,4224]{1,0:T(8,128)(2,1)S(1)}, u32[]{:S(2)}, u32[]{:S(2)}) collective-permute-start(bf16[8,4224]{1,0:T(8,128)(2,1)} %shard_map.73), channel_id=1, source_target_pairs={{0,16},{8,24},{16,0},{24,8},{1,17},{9,25},{17,1},{25,9},{2,18},{10... | collective-permute-start | bytes 202760 | tf_op jit(solution)/shard_map/ppermute | solution.py:20
  8.0 6.0 %collective-permute-start = (bf16[8,4224]{1,0:T(8,128)(2,1)}, bf16[8,4224]{1,0:T(8,128)(2,1)S(1)}, u32[]{:S(2)}, u32[]{:S(2)}) collective-permute-start(bf16[8,4224]{1,0:T(8,128)(2,1)} %shard_map.73), channel_id=1, source_target_pairs={{0,8},{8,0},{16,24},{24,16},{1,9},{9,1},{17,25},{25,17},{2,10},{10... | collective-permute-start | bytes 202760 | tf_op jit(solution)/shard_map/ppermute | solution.py:20
  14.9 16.8 %copy-start = (bf16[32,4224]{1,0:T(8,128)(2,1)}, bf16[32,4224]{1,0:T(8,128)(2,1)S(1)}, u32[]{:S(2)}) copy-start(bf16[32,4224]{1,0:T(8,128)(2,1)S(1)} %pad_maximum_fusion.refs_0_) | copy-start | bytes 811012
  14.9 10.4 %collective-permute-start.5 = (bf16[32,4224]{1,0:T(8,128)(2,1)S(1)}, bf16[32,4224]{1,0:T(8,128)(2,1)S(1)}, u32[]{:S(2)}, u32[]{:S(2)}) collective-permute-start(bf16[32,4224]{1,0:T(8,128)(2,1)S(1)} %pad_maximum_fusion.refs_0_), channel_id=1, source_target_pairs={{0,6},{1,7},{2,4},{3,5},{4,2},{5,3},{6,0},{7,1},{8,14},{9,15},{10,... | collective-permute-start | bytes 811016 | tf_op jit(solution)/shard_map/ppermute | solution.py:20
  17.4 12.3 %collective-permute-start.4 = (bf16[32,4224]{1,0:T(8,128)(2,1)S(1)}, bf16[32,4224]{1,0:T(8,128)(2,1)S(1)}, u32[]{:S(2)}, u32[]{:S(2)}) collective-permute-start(bf16[32,4224]{1,0:T(8,128)(2,1)S(1)} %pad_maximum_fusion.refs_0_), channel_id=1, source_target_pairs={{0,4},{1,5},{2,6},{3,7},{4,0},{5,1},{6,2},{7,3},{8,12},{9,13},{10,... | collective-permute-start | bytes 811016 | tf_op jit(solution)/shard_map/ppermute | solution.py:20
  17.9 12.1 %collective-permute-start.3 = (bf16[32,4224]{1,0:T(8,128)(2,1)S(1)}, bf16[32,4224]{1,0:T(8,128)(2,1)S(1)}, u32[]{:S(2)}, u32[]{:S(2)}) collective-permute-start(bf16[32,4224]{1,0:T(8,128)(2,1)S(1)} %pad_maximum_fusion.refs_0_), channel_id=1, source_target_pairs={{0,2},{1,3},{2,0},{3,1},{4,6},{5,7},{6,4},{7,5},{8,10},{9,11},{10,... | collective-permute-start | bytes 811016 | tf_op jit(solution)/shard_map/ppermute | solution.py:20
  18.4 12.7 %collective-permute-start.6 = (bf16[32,4224]{1,0:T(8,128)(2,1)S(1)}, bf16[32,4224]{1,0:T(8,128)(2,1)S(1)}, u32[]{:S(2)}, u32[]{:S(2)}) collective-permute-start(bf16[32,4224]{1,0:T(8,128)(2,1)S(1)} %pad_maximum_fusion.refs_0_), channel_id=1, source_target_pairs={{0,1},{1,0},{2,3},{3,2},{4,5},{5,4},{6,7},{7,6},{8,9},{9,8},{10,11... | collective-permute-start | bytes 811016 | tf_op jit(solution)/shard_map/ppermute | solution.py:20
  25.3 6.3 %copy-start.1 = (bf16[32,4224]{1,0:T(8,128)(2,1)}, bf16[32,4224]{1,0:T(8,128)(2,1)S(1)}, u32[]{:S(2)}) copy-start(bf16[32,4224]{1,0:T(8,128)(2,1)S(1)} %collective-permute-done.5.refs_3_) | copy-start | bytes 811012
  25.3 5.9 %collective-permute-start.9 = (bf16[32,4224]{1,0:T(8,128)(2,1)S(1)}, bf16[32,4224]{1,0:T(8,128)(2,1)S(1)}, u32[]{:S(2)}, u32[]{:S(2)}) collective-permute-start(bf16[32,4224]{1,0:T(8,128)(2,1)S(1)} %collective-permute-done.5.refs_3_), channel_id=1, source_target_pairs={{0,1},{1,0},{2,3},{3,2},{4,5},{5,4},{6,7},{7,6},{8,9},{9,8},{10,11... | collective-permute-start | bytes 811016 | tf_op jit(solution)/shard_map/ppermute | solution.py:20
  29.7 1.9 %copy-start.2 = (bf16[32,4224]{1,0:T(8,128)(2,1)}, bf16[32,4224]{1,0:T(8,128)(2,1)S(1)}, u32[]{:S(2)}) copy-start(bf16[32,4224]{1,0:T(8,128)(2,1)S(1)} %collective-permute-done.4.refs_2_) | copy-start | bytes 811012
  29.7 1.5 %collective-permute-start.8 = (bf16[32,4224]{1,0:T(8,128)(2,1)S(1)}, bf16[32,4224]{1,0:T(8,128)(2,1)S(1)}, u32[]{:S(2)}, u32[]{:S(2)}) collective-permute-start(bf16[32,4224]{1,0:T(8,128)(2,1)S(1)} %collective-permute-done.4.refs_2_), channel_id=1, source_target_pairs={{0,1},{1,0},{2,3},{3,2},{4,5},{5,4},{6,7},{7,6},{8,9},{9,8},{10,11... | collective-permute-start | bytes 811016 | tf_op jit(solution)/shard_map/ppermute | solution.py:20
  30.0 1.7 %copy-start.3 = (bf16[32,4224]{1,0:T(8,128)(2,1)}, bf16[32,4224]{1,0:T(8,128)(2,1)S(1)}, u32[]{:S(2)}) copy-start(bf16[32,4224]{1,0:T(8,128)(2,1)S(1)} %collective-permute-done.3.refs_1_) | copy-start | bytes 811012
  30.0 1.6 %collective-permute-start.7 = (bf16[32,4224]{1,0:T(8,128)(2,1)S(1)}, bf16[32,4224]{1,0:T(8,128)(2,1)S(1)}, u32[]{:S(2)}, u32[]{:S(2)}) collective-permute-start(bf16[32,4224]{1,0:T(8,128)(2,1)S(1)} %collective-permute-done.3.refs_1_), channel_id=1, source_target_pairs={{0,1},{1,0},{2,3},{3,2},{4,5},{5,4},{6,7},{7,6},{8,9},{9,8},{10,11... | collective-permute-start | bytes 811016 | tf_op jit(solution)/shard_map/ppermute | solution.py:20
  31.2 0.7 copy-start.4
  31.2 0.8 copy-start.5
  31.2 0.8 copy-start.6
  31.6 0.7 copy-start.7
  60.0 2.9 %collective-permute-start.10 = (bf16[128,4096]{1,0:T(8,128)(2,1)}, bf16[128,4096]{1,0:T(8,128)(2,1)S(1)}, u32[]{:S(2)}, u32[]{:S(2)}) collective-permute-start(bf16[128,4096]{1,0:T(8,128)(2,1)} %get-tuple-element.8), channel_id=1, source_target_pairs={{0,1},{1,0},{2,3},{3,2},{4,5},{5,4},{6,7},{7,6},{8,9},{9,8},{10,11... | collective-permute-start | bytes 3145736 | tf_op jit(solution)/shard_map/ppermute | solution.py:20
  64.8 9.2 %collective-permute-start.11 = (bf16[32,4096]{1,0:T(8,128)(2,1)S(1)}, bf16[32,4096]{1,0:T(8,128)(2,1)S(1)}, u32[]{:S(2)}, u32[]{:S(2)}) collective-permute-start(bf16[32,4096]{1,0:T(8,128)(2,1)S(1)} %get-tuple-element.13), channel_id=1, source_target_pairs={{0,2},{1,3},{2,0},{3,1},{4,6},{5,7},{6,4},{7,5},{8,10},{9,11},{10,... | collective-permute-start | bytes 786440 | tf_op jit(solution)/shard_map/ppermute | solution.py:20
  66.6 13.6 %collective-permute-start.13 = (bf16[32,4096]{1,0:T(8,128)(2,1)S(1)}, bf16[32,4096]{1,0:T(8,128)(2,1)S(1)}, u32[]{:S(2)}, u32[]{:S(2)}) collective-permute-start(bf16[32,4096]{1,0:T(8,128)(2,1)S(1)} %get-tuple-element.14), channel_id=1, source_target_pairs={{0,6},{1,7},{2,4},{3,5},{4,2},{5,3},{6,0},{7,1},{8,14},{9,15},{10,... | collective-permute-start | bytes 786440 | tf_op jit(solution)/shard_map/ppermute | solution.py:20
  68.1 13.4 %collective-permute-start.12 = (bf16[32,4096]{1,0:T(8,128)(2,1)S(1)}, bf16[32,4096]{1,0:T(8,128)(2,1)S(1)}, u32[]{:S(2)}, u32[]{:S(2)}) collective-permute-start(bf16[32,4096]{1,0:T(8,128)(2,1)S(1)} %get-tuple-element.15), channel_id=1, source_target_pairs={{0,4},{1,5},{2,6},{3,7},{4,0},{5,1},{6,2},{7,3},{8,12},{9,13},{10,... | collective-permute-start | bytes 786440 | tf_op jit(solution)/shard_map/ppermute | solution.py:20
  81.7 4.7 %collective-permute-start.14 = (bf16[8,4096]{1,0:T(8,128)(2,1)S(1)}, bf16[8,4096]{1,0:T(8,128)(2,1)S(1)}, u32[]{:S(2)}, u32[]{:S(2)}) collective-permute-start(bf16[8,4096]{1,0:T(8,128)(2,1)S(1)} %get-tuple-element.16), channel_id=1, source_target_pairs={{0,8},{8,0},{16,24},{24,16},{1,9},{9,1},{17,25},{25,17},{2,10},{10... | collective-permute-start | bytes 196616 | tf_op jit(solution)/shard_map/ppermute | solution.py:20
  81.7 6.2 %collective-permute-start.16 = (bf16[8,4096]{1,0:T(8,128)(2,1)S(1)}, bf16[8,4096]{1,0:T(8,128)(2,1)S(1)}, u32[]{:S(2)}, u32[]{:S(2)}) collective-permute-start(bf16[8,4096]{1,0:T(8,128)(2,1)S(1)} %get-tuple-element.17), channel_id=1, source_target_pairs={{0,24},{8,16},{16,8},{24,0},{1,25},{9,17},{17,9},{25,1},{2,26},{10... | collective-permute-start | bytes 196616 | tf_op jit(solution)/shard_map/ppermute | solution.py:20
  83.2 6.3 %collective-permute-start.15 = (bf16[8,4096]{1,0:T(8,128)(2,1)S(1)}, bf16[8,4096]{1,0:T(8,128)(2,1)S(1)}, u32[]{:S(2)}, u32[]{:S(2)}) collective-permute-start(bf16[8,4096]{1,0:T(8,128)(2,1)S(1)} %get-tuple-element.18), channel_id=1, source_target_pairs={{0,16},{8,24},{16,0},{24,8},{1,17},{9,25},{17,1},{25,9},{2,18},{10... | collective-permute-start | bytes 196616 | tf_op jit(solution)/shard_map/ppermute | solution.py:20

commit v2 on v0

v2 whole, which is shorter than its diff:
```python
import jax
import jax.numpy as jnp
from jax import lax
from jax.experimental import pallas as pl
from jax.experimental.pallas import tpu as pltpu
from jax.sharding import PartitionSpec as P

LANES = 128
F32 = jnp.float32
BF16 = jnp.bfloat16
MIB = 1 << 20
HALVES = 2
IN_VMEM = pl.BlockSpec(memory_space=pltpu.VMEM)
IN_HBM = pl.BlockSpec(memory_space=pltpu.HBM)
ANYWHERE = pl.BlockSpec(memory_space=pl.ANY)


def near(value):
    return pltpu.with_memory_space_constraint(value, pltpu.VMEM)


def far(value):
    return pltpu.with_memory_space_constraint(value, pltpu.HBM)


def swap(value, axis, to):
    return lax.ppermute(value, axis, [(i, to(i)) for i in range(lax.axis_size(axis))])


def partner(step, steps):
    return lambda i: i ^ (2 << (step if i % 2 == 0 else steps - 1 - step))


def pack_kernel(stream_ref, gain_ref, ids_ref, weights_ref, own_ref, *half_refs, experts):
    stream = stream_ref[...].astype(F32)
    inverse = lax.rsqrt(jnp.mean(stream * stream, axis=-1, keepdims=True) + 1e-06)
    rows, features = stream.shape
    for i in range(features // LANES):
        here = slice(i * LANES, (i + 1) * LANES)
        own_ref[:, here] = (stream[:, here] * inverse * gain_ref[i : i + 1, :].astype(F32)).astype(BF16)
    width = own_ref.shape[1] - features
    column = lax.broadcasted_iota(jnp.int32, (rows, width), 1)
    dense = jnp.zeros((rows, width), F32)
    for k in range(ids_ref.shape[1]):
        expert = ids_ref[:, k : k + 1]
        weight = weights_ref[:, k : k + 1]
        high = weight.astype(BF16).astype(F32)
        middle = (weight - high).astype(BF16).astype(F32)
        low = weight - high - middle
        dense = dense + jnp.where(column == expert, high, 0.0)
        dense = dense + jnp.where(column == expert + experts, middle, 0.0)
        dense = dense + jnp.where(column == expert + 2 * experts, low, 0.0)
    own_ref[:, features:] = dense.astype(BF16)
    at = 0
    for ref in half_refs:
        ref[...] = jnp.zeros_like(ref)
        ref[:rows, :] = own_ref[:, at : at + ref.shape[1]]
        at += ref.shape[1]


def load_kernel(*refs, sources, cuts):
    source_refs, out_refs, sems = refs[:sources], refs[-1 - len(cuts) : -1], refs[-1]
    copies = []
    for i, (source, at, size) in enumerate(cuts):
        copies.append(pltpu.make_async_copy(source_refs[source].at[:, pl.ds(at, size)], out_refs[i], sems.at[i]))
    for copy in copies:
        copy.start()
    for copy in copies:
        copy.wait()


def load(arrays, cuts, after):
    size = sum(arrays[s].shape[0] * n * 2 for s, _, n in cuts)
    out = pl.pallas_call(
        lambda *refs: load_kernel(*refs, sources=len(arrays), cuts=cuts),
        out_shape=[pltpu.VMEM((arrays[s].shape[0], n), BF16) for s, _, n in cuts],
        in_specs=[IN_HBM] * len(arrays) + [ANYWHERE],
        out_specs=[IN_VMEM] * len(cuts),
        scratch_shapes=[pltpu.SemaphoreType.DMA((len(cuts),))],
        compiler_params=pltpu.CompilerParams(vmem_limit_bytes=MIB),
        cost_estimate=pl.CostEstimate(flops=0, bytes_accessed=size, transcendentals=0),
    )(*[far(a) for a in arrays], after)
    return [near(value) for value in out]


def dot_rows(rows, matrix):
    return lax.dot_general(rows, matrix, (((1,), (1,)), ((), ())), preferred_element_type=F32)


def first_kernel(*refs, pieces, block, part, experts):
    piece_refs = refs[:pieces]
    gate_ref, up_ref, down_hbm, gate_out, up_out, spread_ref, down_ref, rows_ref, sem = refs[pieces:]
    fetch = pltpu.make_async_copy(down_hbm.at[:, pl.ds(0, part)], down_ref, sem)
    fetch.start()
    count = piece_refs[0].shape[0]
    for i, ref in enumerate(piece_refs):
        rows_ref[i * count : (i + 1) * count, :] = ref[...]
    for j in range(gate_ref.shape[0] // block):
        here = slice(j * block, (j + 1) * block)
        both = dot_rows(rows_ref[...], jnp.concatenate([gate_ref[here], up_ref[here]], axis=0))
        gate_out[:, here] = both[:, :block]
        up_out[:, here] = both[:, block:]
    held = experts // lax.axis_size("expert")
    lane = lax.broadcasted_iota(jnp.int32, spread_ref.shape, 0)
    unit = lax.broadcasted_iota(jnp.int32, spread_ref.shape, 1)
    low = (lax.axis_index("expert") * held + jnp.zeros((1, 1), jnp.int32)) + unit // (spread_ref.shape[1] // held)
    hit = (lane == low) | (lane == low + experts) | (lane == low + 2 * experts)
    spread_ref[...] = jnp.where(hit, 1.0, 0.0).astype(BF16)
    fetch.wait()


def second_kernel(*refs, pieces, block, part):
    piece_refs = refs[:pieces]
    gate_ref, up_ref, gate_in, up_in, spread_ref, down_hbm, act_ref, down_ref, rows_ref, sem = refs[pieces:]
    fetch = pltpu.make_async_copy(down_hbm.at[:, pl.ds(part, part)], down_ref, sem)
    fetch.start()
    count = piece_refs[0].shape[0]
    for i, ref in enumerate(piece_refs):
        rows_ref[i * count : (i + 1) * count, :] = ref[...]
    for j in range(gate_ref.shape[0] // block):
        here = slice(j * block, (j + 1) * block)
        both = dot_rows(rows_ref[:, :part], jnp.concatenate([gate_ref[here], up_ref[here]], axis=0))
        weight = jnp.dot(rows_ref[:, part:], spread_ref[:, here], preferred_element_type=F32)
        gate = gate_in[:, here] + both[:, :block]
        up = up_in[:, here] + both[:, block:]
        act_ref[:, here] = (gate / (1.0 + jnp.exp(-gate)) * up * weight).astype(BF16)
    fetch.wait()


def down_kernel(act_ref, down_ref, keep_ref, send_ref, *, chunk):
    half = keep_ref.shape[0]
    for j in range(keep_ref.shape[1] // chunk):
        here = slice(j * chunk, (j + 1) * chunk)
        out = jnp.dot(act_ref[...], down_ref[:, here], preferred_element_type=F32)
        keep_ref[:, here] = out[:half]
        send_ref[:, here] = out[half:].astype(BF16)


def params(mib):
    return pltpu.CompilerParams(vmem_limit_bytes=mib * MIB)


def cost(flops, size):
    return pl.CostEstimate(flops=flops, bytes_accessed=size, transcendentals=0)


def local(stream_in, norm_gain, expert_ids, route_weights, w_gate, w_up, w_down):
    row_count, features = stream_in.shape
    held, slice_size, _ = w_gate.shape
    attn_size = lax.axis_size("attn")
    expert_size = lax.axis_size("expert")
    experts = held * expert_size
    width = -(-3 * experts // LANES) * LANES
    hidden = held * slice_size
    part = features // HALVES
    tokens = row_count * attn_size * expert_size
    half = tokens // 2
    steps = (expert_size // 2).bit_length() - 1
    beside = lambda i: i ^ 1

    w_gate = w_gate.reshape(hidden, features)
    w_up = w_up.reshape(hidden, features)
    w_down = w_down.reshape(hidden, features)

    own, *columns = pl.pallas_call(
        lambda *refs: pack_kernel(*refs, experts=experts),
        out_shape=[
            pltpu.VMEM((row_count, features + width), BF16),
            pltpu.VMEM((row_count * attn_size, part), BF16),
            pltpu.VMEM((row_count * attn_size, part + width), BF16),
        ],
    )(stream_in, norm_gain.reshape(features // LANES, LANES), expert_ids, route_weights)

    received = [swap(own, "attn", lambda i, d=d: (i + d) % attn_size) for d in range(1, attn_size)]
    gate_1, up_1 = load([w_gate, w_up], [(0, 0, part), (1, 0, part)], own)
    *received, gate_1, up_1 = lax.optimization_barrier((*received, gate_1, up_1))
    for d, value in enumerate(received, 1):
        at = d * row_count
        columns[0] = columns[0].at[at : at + row_count].set(value[:, :part])
        columns[1] = columns[1].at[at : at + row_count].set(value[:, part:])

    (gate_2,) = load([w_gate], [(0, part, part)], columns[1])
    def beside_all(pieces):
        return pieces + [swap(piece, "expert", beside) for piece in pieces]

    first_column, second_column = columns
    for step in range(steps - 1):
        other = swap(first_column, "expert", partner(step, steps))
        if step == 0:
            other, gate_2 = lax.optimization_barrier((other, gate_2))
        first_column = jnp.concatenate([first_column, other], axis=0)
        other = swap(second_column, "expert", partner(step, steps))
        second_column = jnp.concatenate([second_column, other], axis=0)
    (up_2,) = load([w_up], [(0, part, part)], first_column)
    other = swap(first_column, "expert", partner(steps - 1, steps))
    other, up_2 = lax.optimization_barrier((other, up_2))
    first_pieces = beside_all([first_column, other])
    other = swap(second_column, "expert", partner(steps - 1, steps))
    pieces = len(first_pieces)

    gate, up, spread, down_1 = pl.pallas_call(
        lambda *refs: first_kernel(*refs, pieces=pieces, block=LANES, part=part, experts=experts),
        out_shape=[pltpu.VMEM((tokens, hidden), F32)] * 2
        + [pltpu.VMEM((width, hidden), BF16), pltpu.VMEM((hidden, part), BF16)],
        in_specs=[IN_VMEM] * (pieces + 2) + [IN_HBM],
        out_specs=[IN_VMEM] * 4,
        scratch_shapes=[pltpu.VMEM((tokens, part), BF16), pltpu.SemaphoreType.DMA],
        compiler_params=params(6),
        cost_estimate=cost(4 * tokens * hidden * part, 4 * hidden * part),
    )(*first_pieces, near(gate_1), near(up_1), far(w_down))
    other, gate, up = lax.optimization_barrier((other, gate, up))
    second_pieces = beside_all([second_column, other])
    act, down_2 = pl.pallas_call(
        lambda *refs: second_kernel(*refs, pieces=pieces, block=LANES, part=part),
        out_shape=[pltpu.VMEM((tokens, hidden), BF16), pltpu.VMEM((hidden, part), BF16)],
        in_specs=[IN_VMEM] * (pieces + 5) + [IN_HBM],
        out_specs=[IN_VMEM] * 2,
        scratch_shapes=[pltpu.VMEM((tokens, part + width), BF16), pltpu.SemaphoreType.DMA],
        compiler_params=params(6),
        cost_estimate=cost(4 * tokens * hidden * part, 4 * hidden * part),
    )(*second_pieces, near(gate_2), near(up_2), near(gate), near(up), near(spread), far(w_down))

    outs = []
    for down in (down_1, down_2):
        keep, send = pl.pallas_call(
            lambda *refs: down_kernel(*refs, chunk=512),
            out_shape=[
                pltpu.VMEM((half, part), F32),
                pltpu.VMEM((half, part), BF16),
            ],
            in_specs=[IN_VMEM] * 2,
            out_specs=[IN_VMEM] * 2,
            compiler_params=params(12),
            cost_estimate=cost(2 * tokens * hidden * part, 2 * hidden * part),
        )(near(act), near(down))
        total = keep + swap(send, "expert", beside).astype(F32)
        for step in reversed(range(steps)):
            count = total.shape[0] // 2
            back = swap(total[count:].astype(BF16), "expert", partner(step, steps))
            total = total[:count] + back.astype(F32)
        outs.append(total)
    total = jnp.concatenate(outs, axis=1).reshape(attn_size, row_count, features)
    back = [
        swap(total[d].astype(BF16), "attn", lambda i, d=d: (i - d) % attn_size) for d in range(1, attn_size)
    ]
    return sum([value.astype(F32) for value in back], total[0])


def solution(mesh):
    return jax.shard_map(
        local,
        mesh=mesh,
        in_specs=(
            P(("attn", "expert"), None),
            P(),
            P(("attn", "expert"), None),
            P(("attn", "expert"), None),
            P("expert", "attn", None),
            P("expert", "attn", None),
            P("expert", "attn", None),
        ),
        out_specs=P(("attn", "expert"), None),
        check_vma=False,
    )
```

time: 252 us -> 65.5 us (0.26)
  blocking collectives: 101 us -> 0 us
  waiting for transfers between devices: 93.7 us -> 18.3 us
  matrix products: 26.4 us -> 0 us
  Pallas kernels: 0 us -> 22.7 us
  local copies, waits for them, and re-layouts: 19.6 us -> 0.15 us
  starting transfers between devices: 3.84 us -> 22.8 us
  other arithmetic: 6.88 us -> 1.11 us
    all_to_all x1 -> x0, blocking collectives: 101 us -> none  [local(): lax.all_to_all(copies, ('attn', 'expert'), split_axis=0, concat_axis=0, t...]
    all_to_all x1 -> x0, waiting for transfers between devices: 93.7 us -> none  [local(): lax.all_to_all(partial_out, ('attn', 'expert'), split_axis=0, concat_axis...]
    dot_general x4 -> x0, matrix products: 26.4 us -> none  [the longest x1 14.1 us: local(): jnp.einsum('sjmf,jfd->sjmd', hidden, w_down, preferred_element_type=jnp.f...]
    ppermute x0 -> x20, starting transfers between devices: none -> 22.8 us  [swap(): lax.ppermute(value, axis, [(i, to(i)) for i in range(lax.axis_size(axis))])]
    pallas_call x0 -> x8, Pallas kernels: none -> 22.7 us  [the longest x3 10.2 us: load(): pl.pallas_call(lambda *refs: load_kernel(*refs, sources=len(arrays), cuts...]
    ppermute x0 -> x20, waiting for transfers between devices: none -> 18.3 us  [swap(): lax.ppermute(value, axis, [(i, to(i)) for i in range(lax.axis_size(axis))])]
    convert_element_type x2 -> x0, local copies, waits for them, and re-layouts: 14.7 us -> none  [the longest x1 7.39 us: local(): partial_out = jnp.einsum('sjmf,jfd->sjmd', hidden, w_down, preferred_elem...]
    reduce_sum x3 -> x0, other arithmetic: 5.26 us -> none  [the longest x1 4.18 us: local(): results = jnp.sum(returned.astype(jnp.float32), axis=0)]
  transfers between devices with their start and end apart: 1 -> 20, of which waited for: 1 -> 11; matrix products, arithmetic and copies ran while one was open for 0% -> 1% of each run, Pallas kernels for 0% -> 24%
where the time goes in v2:
time: 65.5 us; the launch traced here: 65.2 us
  starting transfers between devices  22.8 us (35%)
  Pallas kernels  22.7 us (35%)
  waiting for transfers between devices  18.3 us (28%)
  other arithmetic  1.11 us (2%)
    ppermute x20, starting transfers between devices, swap(): lax.ppermute(value, axis, [(i, to(i)) for i in range(lax.axis_size(axis))])  22.8 us
    ppermute x20, waiting for transfers between devices, swap(): lax.ppermute(value, axis, [(i, to(i)) for i in range(lax.axis_size(axis))])  18.3 us
    pallas_call x3, Pallas kernels, load(): pl.pallas_call(lambda *refs: load_kernel(*refs, sources=len(arrays), cuts...  10.2 us
    pallas_call x1, Pallas kernels, local(): pl.pallas_call(lambda *refs: second_kernel(*refs, pieces=pieces, block=LA...  3.95 us
    pallas_call x1, Pallas kernels, local(): pl.pallas_call(lambda *refs: first_kernel(*refs, pieces=pieces, block=LAN...  3.91 us
    pallas_call x2, Pallas kernels, local(): pl.pallas_call(lambda *refs: down_kernel(*refs, chunk=512), out_shape=[pl...  3.57 us
  transfers between devices with their start and end apart: 20, of which 11 were waited for; matrix products, arithmetic and copies ran while one was open for 1% of the time, Pallas kernels for 24%

profile of v2, /device:TPU:0, one launch (start us, length us, event | category | flops | bytes accessed | tf_op | source)
XLA Modules:
  0.0 65.2 jit_solution(2282869635130042139)
XLA Ops:
  0.0 1.0 %shard_map.73 = (bf16[8,4224]{1,0:T(8,128)(2,1)S(1)}, bf16[32,2048]{1,0:T(8,128)(2,1)S(1)}, bf16[32,2176]{1,0:T(8,128)(2,1)S(1)}) custom-call(bf16[8,4096]{1,0:T(8,128)(2,1)} %refs_0_.1, bf16[32,128]{1,0:T(8,128)(2,1)} %bitcast.10, s32[8,8]{1,0:T(8,128)} %refs_2_.1, f32[8,8]{1,0:T(8,128)} %refs_3_.1), custom_call_target="tpu_custom_call" | custom-call | tf_op jit(solution)/shard_map/pallas_call | solution.py:165
  1.0 3.1 %collective-permute-start = (bf16[8,4224]{1,0:T(8,128)(2,1)S(1)}, bf16[8,4224]{1,0:T(8,128)(2,1)S(1)}, u32[]{:S(2)}, u32[]{:S(2)}) collective-permute-start(bf16[8,4224]{1,0:T(8,128)(2,1)S(1)} %get-tuple-element.105.refs_2_), channel_id=1, source_target_pairs={{0,8},{8,16},{16,24},{24,0},{1,9},{9,17},{17,25},{25,1},{2,10},{10... | collective-permute-start | bytes 202760 | tf_op jit(solution)/shard_map/ppermute | solution.py:27
  4.1 2.6 %collective-permute-start.1 = (bf16[8,4224]{1,0:T(8,128)(2,1)S(1)}, bf16[8,4224]{1,0:T(8,128)(2,1)S(1)}, u32[]{:S(2)}, u32[]{:S(2)}) collective-permute-start(bf16[8,4224]{1,0:T(8,128)(2,1)S(1)} %get-tuple-element.105.refs_2_), channel_id=1, source_target_pairs={{0,16},{8,24},{16,0},{24,8},{1,17},{9,25},{17,1},{25,9},{2,18},{10... | collective-permute-start | bytes 202760 | tf_op jit(solution)/shard_map/ppermute | solution.py:27
  6.7 1.3 %collective-permute-start.2 = (bf16[8,4224]{1,0:T(8,128)(2,1)S(1)}, bf16[8,4224]{1,0:T(8,128)(2,1)S(1)}, u32[]{:S(2)}, u32[]{:S(2)}) collective-permute-start(bf16[8,4224]{1,0:T(8,128)(2,1)S(1)} %get-tuple-element.105.refs_2_), channel_id=1, source_target_pairs={{0,24},{8,0},{16,8},{24,16},{1,25},{9,1},{17,9},{25,17},{2,26},{10... | collective-permute-start | bytes 202760 | tf_op jit(solution)/shard_map/ppermute | solution.py:27
  8.0 4.6 %shard_map.74 = (bf16[1536,2048]{1,0:T(8,128)(2,1)S(1)}, bf16[1536,2048]{1,0:T(8,128)(2,1)S(1)}) custom-call(bf16[1536,4096]{1,0:T(8,128)(2,1)} %bitcast.6, bf16[1536,4096]{1,0:T(8,128)(2,1)} %bitcast.8, bf16[8,4224]{1,0:T(8,128)(2,1)S(1)} %get-tuple-element.105.refs_2_), custom_call_target="tpu_custom_call" | custom-call | bytes 12582912 | tf_op jit(solution)/shard_map/pallas_call | solution.py:74
  12.7 0.0 collective-permute-done
  12.7 0.0 collective-permute-done.1
  12.7 0.0 collective-permute-done.2
  12.8 1.6 %collective-permute-start.5 = (bf16[32,2048]{1,0:T(8,128)(2,1)S(1)}, bf16[32,2048]{1,0:T(8,128)(2,1)S(1)}, u32[]{:S(2)}, u32[]{:S(2)}) collective-permute-start(bf16[32,2048]{1,0:T(8,128)(2,1)S(1)} %slice_dynamic-update-slice_fusion.3), channel_id=1, source_target_pairs={{0,2},{1,5},{2,0},{3,7},{4,6},{5,1},{6,4},{7,3},{8,10},{9,13},{10,... | collective-permute-start | bytes 393224 | tf_op jit(solution)/shard_map/ppermute | solution.py:27
  14.3 2.8 %shard_map.75.refs_4_ = bf16[1536,2048]{1,0:T(8,128)(2,1)S(1)} custom-call(bf16[1536,4096]{1,0:T(8,128)(2,1)} %bitcast.7, bf16[32,2176]{1,0:T(8,128)(2,1)S(1)} %slice_dynamic-update-slice_fusion.refs_1_), custom_call_target="tpu_custom_call" | custom-call | bytes 6291456 | tf_op jit(solution)/shard_map/pallas_call | solution.py:74
  17.1 0.7 %collective-permute-done.5 = bf16[32,2048]{1,0:T(8,128)(2,1)S(1)} collective-permute-done((bf16[32,2048]{1,0:T(8,128)(2,1)S(1)}, bf16[32,2048]{1,0:T(8,128)(2,1)S(1)}, u32[]{:S(2)}, u32[]{:S(2)}) %collective-permute-start.5) | collective-permute-done | bytes 131104 | tf_op jit(solution)/shard_map/ppermute | solution.py:27
  17.8 1.6 %collective-permute-start.6 = (bf16[64,2048]{1,0:T(8,128)(2,1)S(1)}, bf16[64,2048]{1,0:T(8,128)(2,1)S(1)}, u32[]{:S(2)}, u32[]{:S(2)}) collective-permute-start(bf16[64,2048]{1,0:T(8,128)(2,1)S(1)} %pad_maximum_fusion.2.refs_1_.refs_0_), channel_id=1, source_target_pairs={{0,4},{1,3},{2,6},{3,1},{4,0},{5,7},{6,2},{7,5},{8,12},{9,11},{10,... | collective-permute-start | bytes 786440 | tf_op jit(solution)/shard_map/ppermute | solution.py:27
  19.4 1.5 %collective-permute-start.3 = (bf16[32,2176]{1,0:T(8,128)(2,1)S(1)}, bf16[32,2176]{1,0:T(8,128)(2,1)S(1)}, u32[]{:S(2)}, u32[]{:S(2)}) collective-permute-start(bf16[32,2176]{1,0:T(8,128)(2,1)S(1)} %slice_dynamic-update-slice_fusion.refs_1_), channel_id=1, source_target_pairs={{0,2},{1,5},{2,0},{3,7},{4,6},{5,1},{6,4},{7,3},{8,10},{9,13},{10,... | collective-permute-start | bytes 417800 | tf_op jit(solution)/shard_map/ppermute | solution.py:27
  20.9 2.8 %shard_map.76.refs_5_ = bf16[1536,2048]{1,0:T(8,128)(2,1)S(1)} custom-call(bf16[1536,4096]{1,0:T(8,128)(2,1)} %bitcast.9, bf16[64,2048]{1,0:T(8,128)(2,1)S(1)} %pad_maximum_fusion.2.refs_1_.refs_0_), custom_call_target="tpu_custom_call" | custom-call | bytes 6291456 | tf_op jit(solution)/shard_map/pallas_call | solution.py:74
  23.7 0.1 collective-permute-start.7
  23.8 0.5 collective-permute-done.6.refs_1_
  24.3 0.0 collective-permute-start.8
  24.3 0.2 collective-permute-done.3
  24.5 1.4 %collective-permute-start.4 = (bf16[64,2176]{1,0:T(8,128)(2,1)S(1)}, bf16[64,2176]{1,0:T(8,128)(2,1)S(1)}, u32[]{:S(2)}, u32[]{:S(2)}) collective-permute-start(bf16[64,2176]{1,0:T(8,128)(2,1)S(1)} %pad_maximum_fusion.1.refs_0_), channel_id=1, source_target_pairs={{0,4},{1,3},{2,6},{3,1},{4,0},{5,7},{6,2},{7,5},{8,12},{9,11},{10,... | collective-permute-start | bytes 835592 | tf_op jit(solution)/shard_map/ppermute | solution.py:27
  25.9 0.2 collective-permute-start.9
  26.1 0.0 collective-permute-done.7.refs_2_
  26.1 0.0 collective-permute-done.8.refs_3_
  26.1 3.9 %shard_map.77 = (f32[256,1536]{1,0:T(8,128)S(1)}, f32[256,1536]{1,0:T(8,128)S(1)}, bf16[128,1536]{1,0:T(8,128)(2,1)S(1)}, bf16[1536,2048]{1,0:T(8,128)(2,1)S(1)}) custom-call(bf16[64,2048]{1,0:T(8,128)(2,1)S(1)} %pad_maximum_fusion.2.refs_1_.refs_0_, bf16[64,2048]{1,0:T(8,128)(2,1)S(1)} %collective-permute-done.6.refs_1_, ...), custom_call_target="tpu_custom_call" | custom-call | flops 3221225472 | bytes 12582912 | tf_op jit(solution)/shard_map/pallas_call | solution.py:201
  30.0 1.1 %collective-permute-done.4.refs_1_ = bf16[64,2176]{1,0:T(8,128)(2,1)S(1)} collective-permute-done((bf16[64,2176]{1,0:T(8,128)(2,1)S(1)}, bf16[64,2176]{1,0:T(8,128)(2,1)S(1)}, u32[]{:S(2)}, u32[]{:S(2)}) %collective-permute-start.4) | collective-permute-done | bytes 278560 | tf_op jit(solution)/shard_map/ppermute | solution.py:27
  31.1 0.0 collective-permute-start.10
  31.1 0.0 collective-permute-done.9.refs_2_
  31.1 1.6 %collective-permute-done.10.refs_3_ = bf16[64,2176]{1,0:T(8,128)(2,1)S(1)} collective-permute-done((bf16[64,2176]{1,0:T(8,128)(2,1)S(1)}, bf16[64,2176]{1,0:T(8,128)(2,1)S(1)}, u32[]{:S(2)}, u32[]{:S(2)}) %collective-permute-start.10) | collective-permute-done | bytes 278560 | tf_op jit(solution)/shard_map/ppermute | solution.py:27
  32.7 4.0 %shard_map.78 = (bf16[256,1536]{1,0:T(8,128)(2,1)S(1)}, bf16[1536,2048]{1,0:T(8,128)(2,1)S(1)}) custom-call(bf16[64,2176]{1,0:T(8,128)(2,1)S(1)} %pad_maximum_fusion.1.refs_0_, bf16[64,2176]{1,0:T(8,128)(2,1)S(1)} %collective-permute-done.4.refs_1_, bf16[64,2176]{1,0:T(8,128)(2,1)S(1)} %collective-permute-done.9.refs_2_, ...), custom_call_target="tpu_custom_call" | custom-call | flops 3221225472 | bytes 12582912 | tf_op jit(solution)/shard_map/pallas_call | solution.py:213
  36.6 1.8 %shard_map.80 = (f32[128,2048]{1,0:T(8,128)S(1)}, bf16[128,2048]{1,0:T(8,128)(2,1)S(1)}) custom-call(bf16[256,1536]{1,0:T(8,128)(2,1)S(1)} %get-tuple-element.124.refs_0_, bf16[1536,2048]{1,0:T(8,128)(2,1)S(1)} %get-tuple-element.128.refs_1_), custom_call_target="tpu_custom_call" | custom-call | flops 1610612736 | bytes 6291456 | tf_op jit(solution)/shard_map/pallas_call | solution.py:225
  38.4 0.2 collective-permute-start.14
  38.6 1.8 %shard_map.79 = (f32[128,2048]{1,0:T(8,128)S(1)}, bf16[128,2048]{1,0:T(8,128)(2,1)S(1)}) custom-call(bf16[256,1536]{1,0:T(8,128)(2,1)S(1)} %get-tuple-element.124.refs_0_, bf16[1536,2048]{1,0:T(8,128)(2,1)S(1)} %get-tuple-element.125.refs_1_), custom_call_target="tpu_custom_call" | custom-call | flops 1610612736 | bytes 6291456 | tf_op jit(solution)/shard_map/pallas_call | solution.py:225
  40.4 0.4 collective-permute-start.11
  40.8 0.0 collective-permute-done.14
  40.8 0.1 convert_add_fusion
  41.0 1.4 %collective-permute-start.15 = (bf16[64,2048]{1,0:T(8,128)(2,1)S(1)}, bf16[64,2048]{1,0:T(8,128)(2,1)S(1)}, u32[]{:S(2)}, u32[]{:S(2)}) collective-permute-start(bf16[64,2048]{1,0:T(8,128)(2,1)S(1)} %slice.224), channel_id=1, source_target_pairs={{0,4},{1,3},{2,6},{3,1},{4,0},{5,7},{6,2},{7,5},{8,12},{9,11},{10,... | collective-permute-start | bytes 786440 | tf_op jit(solution)/shard_map/ppermute | solution.py:27
  42.4 0.0 collective-permute-done.11
  42.4 0.1 convert_add_fusion.1
  42.5 1.4 %collective-permute-start.12 = (bf16[64,2048]{1,0:T(8,128)(2,1)S(1)}, bf16[64,2048]{1,0:T(8,128)(2,1)S(1)}, u32[]{:S(2)}, u32[]{:S(2)}) collective-permute-start(bf16[64,2048]{1,0:T(8,128)(2,1)S(1)} %slice.225), channel_id=1, source_target_pairs={{0,4},{1,3},{2,6},{3,1},{4,0},{5,7},{6,2},{7,5},{8,12},{9,11},{10,... | collective-permute-start | bytes 786440 | tf_op jit(solution)/shard_map/ppermute | solution.py:27
  43.9 3.5 %collective-permute-done.15 = bf16[64,2048]{1,0:T(8,128)(2,1)S(1)} collective-permute-done((bf16[64,2048]{1,0:T(8,128)(2,1)S(1)}, bf16[64,2048]{1,0:T(8,128)(2,1)S(1)}, u32[]{:S(2)}, u32[]{:S(2)}) %collective-permute-start.15) | collective-permute-done | bytes 262176 | tf_op jit(solution)/shard_map/ppermute | solution.py:27
  47.5 1.6 %collective-permute-start.16 = (bf16[32,2048]{1,0:T(8,128)(2,1)S(1)}, bf16[32,2048]{1,0:T(8,128)(2,1)S(1)}, u32[]{:S(2)}, u32[]{:S(2)}) collective-permute-start(bf16[32,2048]{1,0:T(8,128)(2,1)S(1)} %slice.226), channel_id=1, source_target_pairs={{0,2},{1,5},{2,0},{3,7},{4,6},{5,1},{6,4},{7,3},{8,10},{9,13},{10,... | collective-permute-start | bytes 393224 | tf_op jit(solution)/shard_map/ppermute | solution.py:27
  49.1 1.9 %collective-permute-done.12 = bf16[64,2048]{1,0:T(8,128)(2,1)S(1)} collective-permute-done((bf16[64,2048]{1,0:T(8,128)(2,1)S(1)}, bf16[64,2048]{1,0:T(8,128)(2,1)S(1)}, u32[]{:S(2)}, u32[]{:S(2)}) %collective-permute-start.12) | collective-permute-done | bytes 262176 | tf_op jit(solution)/shard_map/ppermute | solution.py:27
  51.0 0.1 slice_add_fusion.1
  51.1 1.6 %collective-permute-start.13 = (bf16[32,2048]{1,0:T(8,128)(2,1)S(1)}, bf16[32,2048]{1,0:T(8,128)(2,1)S(1)}, u32[]{:S(2)}, u32[]{:S(2)}) collective-permute-start(bf16[32,2048]{1,0:T(8,128)(2,1)S(1)} %slice.227), channel_id=1, source_target_pairs={{0,2},{1,5},{2,0},{3,7},{4,6},{5,1},{6,4},{7,3},{8,10},{9,13},{10,... | collective-permute-start | bytes 393224 | tf_op jit(solution)/shard_map/ppermute | solution.py:27
  52.6 0.0 collective-permute-done.16
  52.7 3.4 %collective-permute-done.13 = bf16[32,2048]{1,0:T(8,128)(2,1)S(1)} collective-permute-done((bf16[32,2048]{1,0:T(8,128)(2,1)S(1)}, bf16[32,2048]{1,0:T(8,128)(2,1)S(1)}, u32[]{:S(2)}, u32[]{:S(2)}) %collective-permute-start.13) | collective-permute-done | bytes 131104 | tf_op jit(solution)/shard_map/ppermute | solution.py:27
  56.2 2.3 %collective-permute-start.17 = (bf16[8,4096]{1,0:T(8,128)(2,1)S(1)}, bf16[8,4096]{1,0:T(8,128)(2,1)S(1)}, u32[]{:S(2)}, u32[]{:S(2)}) collective-permute-start(bf16[8,4096]{1,0:T(8,128)(2,1)S(1)} %get-tuple-element.131), channel_id=1, source_target_pairs={{0,24},{8,0},{16,8},{24,16},{1,25},{9,1},{17,9},{25,17},{2,26},{10... | collective-permute-start | bytes 196616 | tf_op jit(solution)/shard_map/ppermute | solution.py:27
  58.5 0.0 collective-permute-start.18
  58.5 0.6 collective-permute-start.19
  59.1 1.9 %collective-permute-done.17 = bf16[8,4096]{1,0:T(8,128)(2,1)S(1)} collective-permute-done((bf16[8,4096]{1,0:T(8,128)(2,1)S(1)}, bf16[8,4096]{1,0:T(8,128)(2,1)S(1)}, u32[]{:S(2)}, u32[]{:S(2)}) %collective-permute-start.17) | collective-permute-done | bytes 65568 | tf_op jit(solution)/shard_map/ppermute | solution.py:27
  61.1 2.6 %collective-permute-done.18 = bf16[8,4096]{1,0:T(8,128)(2,1)S(1)} collective-permute-done((bf16[8,4096]{1,0:T(8,128)(2,1)S(1)}, bf16[8,4096]{1,0:T(8,128)(2,1)S(1)}, u32[]{:S(2)}, u32[]{:S(2)}) %collective-permute-start.18) | collective-permute-done | bytes 65568 | tf_op jit(solution)/shard_map/ppermute | solution.py:27
  63.7 0.9 %collective-permute-done.19 = bf16[8,4096]{1,0:T(8,128)(2,1)S(1)} collective-permute-done((bf16[8,4096]{1,0:T(8,128)(2,1)S(1)}, bf16[8,4096]{1,0:T(8,128)(2,1)S(1)}, u32[]{:S(2)}, u32[]{:S(2)}) %collective-permute-start.19) | collective-permute-done | bytes 65568 | tf_op jit(solution)/shard_map/ppermute | solution.py:27
  64.6 0.7 %fusion.4 = f32[8,4096]{1,0:T(8,128)} fusion(f32[32,2048]{1,0:T(8,128)S(1)} %slice_add_fusion.3, f32[32,2048]{1,0:T(8,128)S(1)} %slice_add_fusion.2, bf16[8,4096]{1,0:T(8,128)(2,1)S(1)} %collective-permute-done.19, bf16[8,4096]{1,0:T(8,128)(2,1)S(1)} %collective-permute-done.18, bf16[8,4096]{1,0:T(8,128)(2,1)S(1)} %collective-permute-done.17), kind=kLoop, calls=%fused_computation.19 | loop fusion | flops 229376 | bytes 851968 | tf_op jit(solution)/shard_map/add | solution.py:246
  (17 shorter events, 0.3 us)
Async XLA Ops:
  1.0 11.6 %collective-permute-start = (bf16[8,4224]{1,0:T(8,128)(2,1)S(1)}, bf16[8,4224]{1,0:T(8,128)(2,1)S(1)}, u32[]{:S(2)}, u32[]{:S(2)}) collective-permute-start(bf16[8,4224]{1,0:T(8,128)(2,1)S(1)} %get-tuple-element.105.refs_2_), channel_id=1, source_target_pairs={{0,8},{8,16},{16,24},{24,0},{1,9},{9,17},{17,25},{25,1},{2,10},{10... | collective-permute-start | bytes 202760 | tf_op jit(solution)/shard_map/ppermute | solution.py:27
  4.1 8.6 %collective-permute-start.1 = (bf16[8,4224]{1,0:T(8,128)(2,1)S(1)}, bf16[8,4224]{1,0:T(8,128)(2,1)S(1)}, u32[]{:S(2)}, u32[]{:S(2)}) collective-permute-start(bf16[8,4224]{1,0:T(8,128)(2,1)S(1)} %get-tuple-element.105.refs_2_), channel_id=1, source_target_pairs={{0,16},{8,24},{16,0},{24,8},{1,17},{9,25},{17,1},{25,9},{2,18},{10... | collective-permute-start | bytes 202760 | tf_op jit(solution)/shard_map/ppermute | solution.py:27
  6.7 6.0 %collective-permute-start.2 = (bf16[8,4224]{1,0:T(8,128)(2,1)S(1)}, bf16[8,4224]{1,0:T(8,128)(2,1)S(1)}, u32[]{:S(2)}, u32[]{:S(2)}) collective-permute-start(bf16[8,4224]{1,0:T(8,128)(2,1)S(1)} %get-tuple-element.105.refs_2_), channel_id=1, source_target_pairs={{0,24},{8,0},{16,8},{24,16},{1,25},{9,1},{17,9},{25,17},{2,26},{10... | collective-permute-start | bytes 202760 | tf_op jit(solution)/shard_map/ppermute | solution.py:27
  12.8 5.0 %collective-permute-start.5 = (bf16[32,2048]{1,0:T(8,128)(2,1)S(1)}, bf16[32,2048]{1,0:T(8,128)(2,1)S(1)}, u32[]{:S(2)}, u32[]{:S(2)}) collective-permute-start(bf16[32,2048]{1,0:T(8,128)(2,1)S(1)} %slice_dynamic-update-slice_fusion.3), channel_id=1, source_target_pairs={{0,2},{1,5},{2,0},{3,7},{4,6},{5,1},{6,4},{7,3},{8,10},{9,13},{10,... | collective-permute-start | bytes 393224 | tf_op jit(solution)/shard_map/ppermute | solution.py:27
  17.8 6.4 %collective-permute-start.6 = (bf16[64,2048]{1,0:T(8,128)(2,1)S(1)}, bf16[64,2048]{1,0:T(8,128)(2,1)S(1)}, u32[]{:S(2)}, u32[]{:S(2)}) collective-permute-start(bf16[64,2048]{1,0:T(8,128)(2,1)S(1)} %pad_maximum_fusion.2.refs_1_.refs_0_), channel_id=1, source_target_pairs={{0,4},{1,3},{2,6},{3,1},{4,0},{5,7},{6,2},{7,5},{8,12},{9,11},{10,... | collective-permute-start | bytes 786440 | tf_op jit(solution)/shard_map/ppermute | solution.py:27
  19.4 5.1 %collective-permute-start.3 = (bf16[32,2176]{1,0:T(8,128)(2,1)S(1)}, bf16[32,2176]{1,0:T(8,128)(2,1)S(1)}, u32[]{:S(2)}, u32[]{:S(2)}) collective-permute-start(bf16[32,2176]{1,0:T(8,128)(2,1)S(1)} %slice_dynamic-update-slice_fusion.refs_1_), channel_id=1, source_target_pairs={{0,2},{1,5},{2,0},{3,7},{4,6},{5,1},{6,4},{7,3},{8,10},{9,13},{10,... | collective-permute-start | bytes 417800 | tf_op jit(solution)/shard_map/ppermute | solution.py:27
  23.7 2.4 %collective-permute-start.7 = (bf16[64,2048]{1,0:T(8,128)(2,1)S(1)}, bf16[64,2048]{1,0:T(8,128)(2,1)S(1)}, u32[]{:S(2)}, u32[]{:S(2)}) collective-permute-start(bf16[64,2048]{1,0:T(8,128)(2,1)S(1)} %pad_maximum_fusion.2.refs_1_.refs_0_), channel_id=1, source_target_pairs={{0,1},{1,0},{2,3},{3,2},{4,5},{5,4},{6,7},{7,6},{8,9},{9,8},{10,11... | collective-permute-start | bytes 786440 | tf_op jit(solution)/shard_map/ppermute | solution.py:27
  24.3 1.8 %collective-permute-start.8 = (bf16[64,2048]{1,0:T(8,128)(2,1)S(1)}, bf16[64,2048]{1,0:T(8,128)(2,1)S(1)}, u32[]{:S(2)}, u32[]{:S(2)}) collective-permute-start(bf16[64,2048]{1,0:T(8,128)(2,1)S(1)} %collective-permute-done.6.refs_1_), channel_id=1, source_target_pairs={{0,1},{1,0},{2,3},{3,2},{4,5},{5,4},{6,7},{7,6},{8,9},{9,8},{10,11... | collective-permute-start | bytes 786440 | tf_op jit(solution)/shard_map/ppermute | solution.py:27
  24.5 6.6 %collective-permute-start.4 = (bf16[64,2176]{1,0:T(8,128)(2,1)S(1)}, bf16[64,2176]{1,0:T(8,128)(2,1)S(1)}, u32[]{:S(2)}, u32[]{:S(2)}) collective-permute-start(bf16[64,2176]{1,0:T(8,128)(2,1)S(1)} %pad_maximum_fusion.1.refs_0_), channel_id=1, source_target_pairs={{0,4},{1,3},{2,6},{3,1},{4,0},{5,7},{6,2},{7,5},{8,12},{9,11},{10,... | collective-permute-start | bytes 835592 | tf_op jit(solution)/shard_map/ppermute | solution.py:27
  25.9 5.2 %collective-permute-start.9 = (bf16[64,2176]{1,0:T(8,128)(2,1)S(1)}, bf16[64,2176]{1,0:T(8,128)(2,1)S(1)}, u32[]{:S(2)}, u32[]{:S(2)}) collective-permute-start(bf16[64,2176]{1,0:T(8,128)(2,1)S(1)} %pad_maximum_fusion.1.refs_0_), channel_id=1, source_target_pairs={{0,1},{1,0},{2,3},{3,2},{4,5},{5,4},{6,7},{7,6},{8,9},{9,8},{10,11... | collective-permute-start | bytes 835592 | tf_op jit(solution)/shard_map/ppermute | solution.py:27
  31.1 1.6 %collective-permute-start.10 = (bf16[64,2176]{1,0:T(8,128)(2,1)S(1)}, bf16[64,2176]{1,0:T(8,128)(2,1)S(1)}, u32[]{:S(2)}, u32[]{:S(2)}) collective-permute-start(bf16[64,2176]{1,0:T(8,128)(2,1)S(1)} %collective-permute-done.4.refs_1_), channel_id=1, source_target_pairs={{0,1},{1,0},{2,3},{3,2},{4,5},{5,4},{6,7},{7,6},{8,9},{9,8},{10,11... | collective-permute-start | bytes 835592 | tf_op jit(solution)/shard_map/ppermute | solution.py:27
  38.4 2.4 %collective-permute-start.14 = (bf16[128,2048]{1,0:T(8,128)(2,1)S(1)}, bf16[128,2048]{1,0:T(8,128)(2,1)S(1)}, u32[]{:S(2)}, u32[]{:S(2)}) collective-permute-start(bf16[128,2048]{1,0:T(8,128)(2,1)S(1)} %get-tuple-element.130), channel_id=1, source_target_pairs={{0,1},{1,0},{2,3},{3,2},{4,5},{5,4},{6,7},{7,6},{8,9},{9,8},{10,11... | collective-permute-start | bytes 1572872 | tf_op jit(solution)/shard_map/ppermute | solution.py:27
  40.4 2.0 %collective-permute-start.11 = (bf16[128,2048]{1,0:T(8,128)(2,1)S(1)}, bf16[128,2048]{1,0:T(8,128)(2,1)S(1)}, u32[]{:S(2)}, u32[]{:S(2)}) collective-permute-start(bf16[128,2048]{1,0:T(8,128)(2,1)S(1)} %get-tuple-element.127), channel_id=1, source_target_pairs={{0,1},{1,0},{2,3},{3,2},{4,5},{5,4},{6,7},{7,6},{8,9},{9,8},{10,11... | collective-permute-start | bytes 1572872 | tf_op jit(solution)/shard_map/ppermute | solution.py:27
  41.0 6.4 %collective-permute-start.15 = (bf16[64,2048]{1,0:T(8,128)(2,1)S(1)}, bf16[64,2048]{1,0:T(8,128)(2,1)S(1)}, u32[]{:S(2)}, u32[]{:S(2)}) collective-permute-start(bf16[64,2048]{1,0:T(8,128)(2,1)S(1)} %slice.224), channel_id=1, source_target_pairs={{0,4},{1,3},{2,6},{3,1},{4,0},{5,7},{6,2},{7,5},{8,12},{9,11},{10,... | collective-permute-start | bytes 786440 | tf_op jit(solution)/shard_map/ppermute | solution.py:27
  42.5 8.4 %collective-permute-start.12 = (bf16[64,2048]{1,0:T(8,128)(2,1)S(1)}, bf16[64,2048]{1,0:T(8,128)(2,1)S(1)}, u32[]{:S(2)}, u32[]{:S(2)}) collective-permute-start(bf16[64,2048]{1,0:T(8,128)(2,1)S(1)} %slice.225), channel_id=1, source_target_pairs={{0,4},{1,3},{2,6},{3,1},{4,0},{5,7},{6,2},{7,5},{8,12},{9,11},{10,... | collective-permute-start | bytes 786440 | tf_op jit(solution)/shard_map/ppermute | solution.py:27
  47.5 5.1 %collective-permute-start.16 = (bf16[32,2048]{1,0:T(8,128)(2,1)S(1)}, bf16[32,2048]{1,0:T(8,128)(2,1)S(1)}, u32[]{:S(2)}, u32[]{:S(2)}) collective-permute-start(bf16[32,2048]{1,0:T(8,128)(2,1)S(1)} %slice.226), channel_id=1, source_target_pairs={{0,2},{1,5},{2,0},{3,7},{4,6},{5,1},{6,4},{7,3},{8,10},{9,13},{10,... | collective-permute-start | bytes 393224 | tf_op jit(solution)/shard_map/ppermute | solution.py:27
  51.1 5.0 %collective-permute-start.13 = (bf16[32,2048]{1,0:T(8,128)(2,1)S(1)}, bf16[32,2048]{1,0:T(8,128)(2,1)S(1)}, u32[]{:S(2)}, u32[]{:S(2)}) collective-permute-start(bf16[32,2048]{1,0:T(8,128)(2,1)S(1)} %slice.227), channel_id=1, source_target_pairs={{0,2},{1,5},{2,0},{3,7},{4,6},{5,1},{6,4},{7,3},{8,10},{9,13},{10,... | collective-permute-start | bytes 393224 | tf_op jit(solution)/shard_map/ppermute | solution.py:27
  56.2 4.9 %collective-permute-start.17 = (bf16[8,4096]{1,0:T(8,128)(2,1)S(1)}, bf16[8,4096]{1,0:T(8,128)(2,1)S(1)}, u32[]{:S(2)}, u32[]{:S(2)}) collective-permute-start(bf16[8,4096]{1,0:T(8,128)(2,1)S(1)} %get-tuple-element.131), channel_id=1, source_target_pairs={{0,24},{8,0},{16,8},{24,16},{1,25},{9,1},{17,9},{25,17},{2,26},{10... | collective-permute-start | bytes 196616 | tf_op jit(solution)/shard_map/ppermute | solution.py:27
  58.5 5.2 %collective-permute-start.18 = (bf16[8,4096]{1,0:T(8,128)(2,1)S(1)}, bf16[8,4096]{1,0:T(8,128)(2,1)S(1)}, u32[]{:S(2)}, u32[]{:S(2)}) collective-permute-start(bf16[8,4096]{1,0:T(8,128)(2,1)S(1)} %get-tuple-element.133), channel_id=1, source_target_pairs={{0,16},{8,24},{16,0},{24,8},{1,17},{9,25},{17,1},{25,9},{2,18},{10... | collective-permute-start | bytes 196616 | tf_op jit(solution)/shard_map/ppermute | solution.py:27
  58.5 6.1 %collective-permute-start.19 = (bf16[8,4096]{1,0:T(8,128)(2,1)S(1)}, bf16[8,4096]{1,0:T(8,128)(2,1)S(1)}, u32[]{:S(2)}, u32[]{:S(2)}) collective-permute-start(bf16[8,4096]{1,0:T(8,128)(2,1)S(1)} %get-tuple-element.132), channel_id=1, source_target_pairs={{0,8},{8,16},{16,24},{24,0},{1,9},{9,17},{17,25},{25,1},{2,10},{10... | collective-permute-start | bytes 196616 | tf_op jit(solution)/shard_map/ppermute | solution.py:27

commit v3 on v2

v3 whole, which is shorter than its diff:
```python
import jax
import jax.numpy as jnp
from jax import lax
from jax.experimental import pallas as pl
from jax.experimental.pallas import tpu as pltpu
from jax.sharding import PartitionSpec as P

LANES = 128
F32 = jnp.float32
BF16 = jnp.bfloat16
MIB = 1 << 20
HALVES = 2
DOWNS = 1
COSTS = False
LOADS = True
CUT = 2048
Z_UP = False
P1_WHOLE = False
Z_HALVES = False
IN_VMEM = pl.BlockSpec(memory_space=pltpu.VMEM)
IN_HBM = pl.BlockSpec(memory_space=pltpu.HBM)
ANYWHERE = pl.BlockSpec(memory_space=pl.ANY)


def near(value):
    return pltpu.with_memory_space_constraint(value, pltpu.VMEM)


def far(value):
    return pltpu.with_memory_space_constraint(value, pltpu.HBM)


def swap(value, axis, to):
    return lax.ppermute(value, axis, [(i, to(i)) for i in range(lax.axis_size(axis))])


def partner(step, steps):
    return lambda i: i ^ (2 << (step if i % 2 == 0 else steps - 1 - step))


def fold(total, step, steps):
    count = total.shape[0] // 2
    back = swap(total[count:].astype(BF16), "expert", partner(step, steps))
    return total[:count] + back.astype(F32)


def pack_kernel(stream_ref, gain_ref, ids_ref, weights_ref, own_ref, *half_refs, experts):
    stream = stream_ref[...].astype(F32)
    inverse = lax.rsqrt(jnp.mean(stream * stream, axis=-1, keepdims=True) + 1e-06)
    rows, features = stream.shape
    for i in range(features // LANES):
        here = slice(i * LANES, (i + 1) * LANES)
        own_ref[:, here] = (stream[:, here] * inverse * gain_ref[i : i + 1, :].astype(F32)).astype(BF16)
    width = own_ref.shape[1] - features
    column = lax.broadcasted_iota(jnp.int32, (rows, width), 1)
    dense = jnp.zeros((rows, width), F32)
    for k in range(ids_ref.shape[1]):
        expert = ids_ref[:, k : k + 1]
        weight = weights_ref[:, k : k + 1]
        high = weight.astype(BF16).astype(F32)
        middle = (weight - high).astype(BF16).astype(F32)
        low = weight - high - middle
        dense = dense + jnp.where(column == expert, high, 0.0)
        dense = dense + jnp.where(column == expert + experts, middle, 0.0)
        dense = dense + jnp.where(column == expert + 2 * experts, low, 0.0)
    own_ref[:, features:] = dense.astype(BF16)
    at = 0
    for ref in half_refs:
        ref[...] = jnp.zeros_like(ref)
        ref[:rows, :] = own_ref[:, at : at + ref.shape[1]]
        at += ref.shape[1]


def load_kernel(*refs, sources, cuts, experts):
    source_refs, sems = refs[:sources], refs[-1]
    out_refs = refs[sources + 1 : -1]
    copies = []
    for i, (source, at, size) in enumerate(cuts):
        copies.append(pltpu.make_async_copy(source_refs[source].at[:, pl.ds(at, size)], out_refs[i], sems.at[i]))
    for copy in copies:
        copy.start()
    if experts:
        spread_ref = out_refs[-1]
        held = experts // lax.axis_size("expert")
        lane = lax.broadcasted_iota(jnp.int32, spread_ref.shape, 0)
        unit = lax.broadcasted_iota(jnp.int32, spread_ref.shape, 1)
        owner = lax.axis_index("expert") * held + unit // (spread_ref.shape[1] // held)
        hit = (lane == owner) | (lane == owner + experts) | (lane == owner + 2 * experts)
        spread_ref[...] = jnp.where(hit, 1.0, 0.0).astype(BF16)
    for copy in copies:
        copy.wait()


def load(arrays, cuts, after, experts=0, width=0):
    rows = arrays[0].shape[0]
    size = sum(rows * n * 2 for _, _, n in cuts)
    return pl.pallas_call(
        lambda *refs: load_kernel(*refs, sources=len(arrays), cuts=cuts, experts=experts),
        out_shape=[pltpu.VMEM((rows, n), BF16) for _, _, n in cuts] + [pltpu.VMEM((width, rows), BF16)] * bool(experts),
        in_specs=[IN_HBM] * len(arrays) + [ANYWHERE],
        out_specs=[IN_VMEM] * (len(cuts) + bool(experts)),
        scratch_shapes=[pltpu.SemaphoreType.DMA((len(cuts),))],
        compiler_params=pltpu.CompilerParams(vmem_limit_bytes=MIB),
        cost_estimate=pl.CostEstimate(flops=0, bytes_accessed=size if LOADS else 0, transcendentals=0),
    )(*[far(a) for a in arrays], after)


def dot_rows(rows, matrix):
    return lax.dot_general(rows, matrix, (((1,), (1,)), ((), ())), preferred_element_type=F32)


def gate_up(rows, gate_ref, up_ref, at, block):
    here = slice(at, at + block)
    both = dot_rows(rows, jnp.concatenate([gate_ref[here], up_ref[here]], axis=0))
    return both[:, :block], both[:, block:]


def first_kernel(*refs, pieces, block):
    piece_refs = refs[:pieces]
    gate_ref, up_ref, rows_ref, gate_out, up_out = refs[pieces:]
    count = piece_refs[0].shape[0]
    for i, ref in enumerate(piece_refs):
        rows_ref[i * count : (i + 1) * count, :] = ref[...]
    for j in range(0, gate_out.shape[1], block):
        gate_out[:, j : j + block], up_out[:, j : j + block] = gate_up(rows_ref[...], gate_ref, up_ref, j, block)


def middle_kernel(rows_ref, gate_ref, up_ref, gate_out, up_out, *, block, start):
    for j in range(0, gate_out.shape[1], block):
        gate_out[:, j : j + block], up_out[:, j : j + block] = gate_up(
            rows_ref[...], gate_ref, up_ref, start + j, block
        )


def second_kernel(*refs, pieces, block, part, start, size):
    piece_refs = refs[:pieces]
    gate_ref, up_ref, *sums, spread_ref, down_hbm, act_ref, down_ref, rows_ref, sem = refs[pieces:]
    fetch = pltpu.make_async_copy(down_hbm.at[:, pl.ds(start, size)], down_ref, sem)
    fetch.start()
    count = piece_refs[0].shape[0]
    for i, ref in enumerate(piece_refs):
        rows_ref[i * count : (i + 1) * count, :] = ref[...]
    cut = sums[0].shape[1]
    for j in range(0, gate_ref.shape[0], block):
        here = slice(j, j + block)
        gate, up = gate_up(rows_ref[:, :part], gate_ref, up_ref, j, block)
        weight = jnp.dot(rows_ref[:, part:], spread_ref[:, here], preferred_element_type=F32)
        gate_in, up_in = sums[:2] if j < cut else sums[2:]
        there = slice(j % cut, j % cut + block)
        gate, up = gate + gate_in[:, there], up + up_in[:, there]
        act_ref[:, here] = (gate / (1.0 + jnp.exp(-gate)) * up * weight).astype(BF16)
    fetch.wait()


def down_kernel(act_ref, down_ref, keep_ref, send_ref, *, chunk, start):
    half = keep_ref.shape[0]
    for j in range(keep_ref.shape[1] // chunk):
        here = slice(j * chunk, (j + 1) * chunk)
        there = slice(start + j * chunk, start + (j + 1) * chunk)
        out = jnp.dot(act_ref[...], down_ref[:, there], preferred_element_type=F32)
        keep_ref[:, here] = out[:half]
        send_ref[:, here] = out[half:].astype(BF16)


def params(mib):
    return pltpu.CompilerParams(vmem_limit_bytes=mib * MIB)


def cost(flops, size):
    if not COSTS:
        flops, size = 0, 0
    return pl.CostEstimate(flops=flops, bytes_accessed=size, transcendentals=0)


def local(stream_in, norm_gain, expert_ids, route_weights, w_gate, w_up, w_down):
    row_count, features = stream_in.shape
    held, slice_size, _ = w_gate.shape
    attn_size = lax.axis_size("attn")
    expert_size = lax.axis_size("expert")
    experts = held * expert_size
    width = -(-3 * experts // LANES) * LANES
    hidden = held * slice_size
    part = features // HALVES
    tokens = row_count * attn_size * expert_size
    half = tokens // 2
    steps = (expert_size // 2).bit_length() - 1
    beside = lambda i: i ^ 1

    w_gate = w_gate.reshape(hidden, features)
    w_up = w_up.reshape(hidden, features)
    w_down = w_down.reshape(hidden, features)

    own, column = pl.pallas_call(
        lambda *refs: pack_kernel(*refs, experts=experts),
        out_shape=[
            pltpu.VMEM((row_count, features + width), BF16),
            pltpu.VMEM((row_count * attn_size, features + width), BF16),
        ],
    )(stream_in, norm_gain.reshape(features // LANES, LANES), expert_ids, route_weights)

    order = range(1, attn_size) if Z_UP else range(attn_size - 1, 0, -1)
    received = {d: swap(own, "attn", lambda i, d=d: (i + d) % attn_size) for d in order}
    gate_1, up_1 = load([w_gate, w_up], [(0, 0, part), (1, 0, part)], own)
    *values, gate_1, up_1 = lax.optimization_barrier((*received.values(), gate_1, up_1))
    for d, value in zip(received, values):
        column = column.at[d * row_count : (d + 1) * row_count].set(value)

    gate_2, up_2 = load([w_gate, w_up], [(0, part, part), (1, part, part)], column)
    for step in range(steps - 1):
        other = swap(column, "expert", partner(step, steps))
        if step == 0:
            other, gate_2, up_2 = lax.optimization_barrier((other, gate_2, up_2))
        column = jnp.concatenate([column, other], axis=0)
    columns = [column[:, :part], column[:, part:]]
    down_1, spread = load([w_down], [(0, 0, CUT)], columns[0], experts, width)
    others = [swap(value, "expert", partner(steps - 1, steps)) for value in columns]
    others[0], down_1, spread = lax.optimization_barrier((others[0], down_1, spread))

    def both_of_pair(pieces):
        return pieces + [swap(piece, "expert", beside) for piece in pieces]

    pieces = both_of_pair([columns[0], others[0]])
    count = len(pieces)
    cut = hidden // 2
    matmul = cost(2 * tokens * hidden * part, 2 * hidden * part)
    rows, gate_a, up_a = pl.pallas_call(
        lambda *refs: first_kernel(*refs, pieces=count, block=LANES),
        out_shape=[pltpu.VMEM((tokens, part), BF16)] + [pltpu.VMEM((tokens, cut), F32)] * 2,
        in_specs=[IN_VMEM] * (count + 2),
        out_specs=[IN_VMEM] * 3,
        compiler_params=params(6),
        cost_estimate=matmul,
    )(*pieces, near(gate_1), near(up_1))
    others[1], rows = lax.optimization_barrier((others[1], rows))
    gate_b, up_b = pl.pallas_call(
        lambda *refs: middle_kernel(*refs, block=LANES, start=cut),
        out_shape=[pltpu.VMEM((tokens, cut), F32)] * 2,
        in_specs=[IN_VMEM] * 3,
        out_specs=[IN_VMEM] * 2,
        compiler_params=params(6),
        cost_estimate=matmul,
    )(near(rows), near(gate_1), near(up_1))
    pieces = both_of_pair([columns[1], others[1]])
    act, down_2 = pl.pallas_call(
        lambda *refs: second_kernel(*refs, pieces=count, block=LANES, part=part, start=CUT, size=features - CUT),
        out_shape=[pltpu.VMEM((tokens, hidden), BF16), pltpu.VMEM((hidden, features - CUT), BF16)],
        in_specs=[IN_VMEM] * (count + 7) + [IN_HBM],
        out_specs=[IN_VMEM] * 2,
        scratch_shapes=[pltpu.VMEM((tokens, part + width), BF16), pltpu.SemaphoreType.DMA],
        compiler_params=params(6),
        cost_estimate=cost(4 * tokens * hidden * part, 4 * hidden * part),
    )(
        *pieces,
        near(gate_2),
        near(up_2),
        *[near(value) for value in (gate_a, up_a, gate_b, up_b)],
        near(spread),
        far(w_down),
    )

    outs = []
    for down in (down_1, down_2):
        size = down.shape[1] // DOWNS
        keeps, sends = [], []
        for i in range(DOWNS):
            keep, send = pl.pallas_call(
                lambda *refs, i=i: down_kernel(*refs, chunk=512, start=i * size),
                out_shape=[pltpu.VMEM((half, size), F32), pltpu.VMEM((half, size), BF16)],
                in_specs=[IN_VMEM] * 2,
                out_specs=[IN_VMEM] * 2,
                compiler_params=params(12),
                cost_estimate=cost(2 * tokens * hidden * size, 2 * hidden * size),
            )(near(act), near(down))
            keeps.append(keep)
            sends.append(swap(send, "expert", beside))
        keep, send = jnp.concatenate(keeps, axis=1), jnp.concatenate(sends, axis=1)
        total = keep + send.astype(F32)
        for step in reversed(range(1 if P1_WHOLE else 0, steps)):
            total = fold(total, step, steps)
        outs.append(total)
    if P1_WHOLE:
        outs = [fold(jnp.concatenate(outs, axis=1), 0, steps)]
    if not Z_HALVES:
        outs = [jnp.concatenate(outs, axis=1)]
    result = []
    for total in outs:
        total = total.reshape(attn_size, row_count, -1)
        back = [swap(total[d].astype(BF16), "attn", lambda i, d=d: (i - d) % attn_size) for d in order]
        result.append(sum([value.astype(F32) for value in back], total[0]))
    return jnp.concatenate(result, axis=1)


def solution(mesh):
    return jax.shard_map(
        local,
        mesh=mesh,
        in_specs=(
            P(("attn", "expert"), None),
            P(),
            P(("attn", "expert"), None),
            P(("attn", "expert"), None),
            P("expert", "attn", None),
            P("expert", "attn", None),
            P("expert", "attn", None),
        ),
        out_specs=P(("attn", "expert"), None),
        check_vma=False,
    )
```

time: 65.5 us -> 63 us (0.962)
  waiting for transfers between devices: 18.3 us -> 14.9 us
  Pallas kernels: 22.7 us -> 24.3 us
    ppermute x20 -> x19, waiting for transfers between devices: 18.3 us -> 14.9 us  [swap(): lax.ppermute(value, axis, [(i, to(i)) for i in range(lax.axis_size(axis))])]
    pallas_call x3, Pallas kernels: 10.2 us -> 12 us  [load(): pl.pallas_call(lambda *refs: load_kernel(*refs, sources=len(arrays), cuts...]
    ppermute x20 -> x19, starting transfers between devices: 22.8 us -> 22.2 us  [swap(): lax.ppermute(value, axis, [(i, to(i)) for i in range(lax.axis_size(axis))])]
    pallas_call x4 -> x5, Pallas kernels: 11.4 us -> 11.3 us  [the longest x1 4.04 us: local(): pl.pallas_call(lambda *refs: second_kernel(*refs, pieces=count, block=LAN...]
  transfers between devices with their start and end apart: 20 -> 19, of which waited for: 11 -> 10; matrix products, arithmetic and copies ran while one was open for 1% -> 1% of each run, Pallas kernels for 24% -> 28%
where the time goes in v3:
time: 63 us; the launch traced here: 62.8 us
  Pallas kernels  24.3 us (39%)
  starting transfers between devices  22.2 us (35%)
  waiting for transfers between devices  14.9 us (24%)
  other arithmetic  1.11 us (2%)
    ppermute x19, starting transfers between devices, swap(): lax.ppermute(value, axis, [(i, to(i)) for i in range(lax.axis_size(axis))])  22.2 us
    ppermute x19, waiting for transfers between devices, swap(): lax.ppermute(value, axis, [(i, to(i)) for i in range(lax.axis_size(axis))])  14.9 us
    pallas_call x3, Pallas kernels, load(): pl.pallas_call(lambda *refs: load_kernel(*refs, sources=len(arrays), cuts...  12 us
    pallas_call x1, Pallas kernels, local(): pl.pallas_call(lambda *refs: second_kernel(*refs, pieces=count, block=LAN...  4.04 us
    pallas_call x2, Pallas kernels, local(): pl.pallas_call(lambda *refs, i=i: down_kernel(*refs, chunk=512, start=i *...  3.57 us
    pallas_call x1, Pallas kernels, local(): pl.pallas_call(lambda *refs: middle_kernel(*refs, block=LANES, start=cut)...  1.83 us
    pallas_call x1, Pallas kernels, local(): pl.pallas_call(lambda *refs: first_kernel(*refs, pieces=count, block=LANE...  1.83 us
  transfers between devices with their start and end apart: 19, of which 10 were waited for; matrix products, arithmetic and copies ran while one was open for 1% of the time, Pallas kernels for 28%

profile of v3, /device:TPU:0, one launch (start us, length us, event | category | flops | bytes accessed | tf_op | source)
XLA Modules:
  0.0 62.8 jit_solution(1507549586031850432)
XLA Ops:
  0.0 1.0 %shard_map.73 = (bf16[8,4224]{1,0:T(8,128)(2,1)S(1)}, bf16[32,4224]{1,0:T(8,128)(2,1)S(1)}) custom-call(bf16[8,4096]{1,0:T(8,128)(2,1)} %refs_0_.1, bf16[32,128]{1,0:T(8,128)(2,1)} %bitcast.10, s32[8,8]{1,0:T(8,128)} %refs_2_.1, f32[8,8]{1,0:T(8,128)} %refs_3_.1), custom_call_target="tpu_custom_call" | custom-call | tf_op jit(solution)/shard_map/pallas_call | solution.py:193
  1.0 5.1 %collective-permute-start = (bf16[8,4224]{1,0:T(8,128)(2,1)S(1)}, bf16[8,4224]{1,0:T(8,128)(2,1)S(1)}, u32[]{:S(2)}, u32[]{:S(2)}) collective-permute-start(bf16[8,4224]{1,0:T(8,128)(2,1)S(1)} %get-tuple-element.74.refs_2_), channel_id=1, source_target_pairs={{0,24},{8,0},{16,8},{24,16},{1,25},{9,1},{17,9},{25,17},{2,26},{10... | collective-permute-start | bytes 202760 | tf_op jit(solution)/shard_map/ppermute | solution.py:34
  6.1 0.0 collective-permute-start.1
  6.1 1.0 %collective-permute-start.2 = (bf16[8,4224]{1,0:T(8,128)(2,1)S(1)}, bf16[8,4224]{1,0:T(8,128)(2,1)S(1)}, u32[]{:S(2)}, u32[]{:S(2)}) collective-permute-start(bf16[8,4224]{1,0:T(8,128)(2,1)S(1)} %get-tuple-element.74.refs_2_), channel_id=1, source_target_pairs={{0,8},{8,16},{16,24},{24,0},{1,9},{9,17},{17,25},{25,1},{2,10},{10... | collective-permute-start | bytes 202760 | tf_op jit(solution)/shard_map/ppermute | solution.py:34
  7.1 4.6 %shard_map.74 = (bf16[1536,2048]{1,0:T(8,128)(2,1)S(1)}, bf16[1536,2048]{1,0:T(8,128)(2,1)S(1)}) custom-call(bf16[1536,4096]{1,0:T(8,128)(2,1)} %bitcast.6, bf16[1536,4096]{1,0:T(8,128)(2,1)} %bitcast.8, bf16[8,4224]{1,0:T(8,128)(2,1)S(1)} %get-tuple-element.74.refs_2_), custom_call_target="tpu_custom_call" | custom-call | bytes 12582912 | tf_op jit(solution)/shard_map/pallas_call | solution.py:97
  11.8 0.0 collective-permute-done
  11.8 1.0 %collective-permute-done.1 = bf16[8,4224]{1,0:T(8,128)(2,1)S(1)} collective-permute-done((bf16[8,4224]{1,0:T(8,128)(2,1)S(1)}, bf16[8,4224]{1,0:T(8,128)(2,1)S(1)}, u32[]{:S(2)}, u32[]{:S(2)}) %collective-permute-start.1) | collective-permute-done | bytes 67616 | tf_op jit(solution)/shard_map/ppermute | solution.py:34
  12.8 0.0 collective-permute-done.2
  12.8 1.6 %collective-permute-start.3 = (bf16[32,4224]{1,0:T(8,128)(2,1)S(1)}, bf16[32,4224]{1,0:T(8,128)(2,1)S(1)}, u32[]{:S(2)}, u32[]{:S(2)}) collective-permute-start(bf16[32,4224]{1,0:T(8,128)(2,1)S(1)} %constant_dynamic-update-slice_fusion.refs_2_), channel_id=1, source_target_pairs={{0,2},{1,5},{2,0},{3,7},{4,6},{5,1},{6,4},{7,3},{8,10},{9,13},{10,... | collective-permute-start | bytes 811016 | tf_op jit(solution)/shard_map/ppermute | solution.py:34
  14.4 4.6 %shard_map.75 = (bf16[1536,2048]{1,0:T(8,128)(2,1)S(1)}, bf16[1536,2048]{1,0:T(8,128)(2,1)S(1)}) custom-call(bf16[1536,4096]{1,0:T(8,128)(2,1)} %bitcast.7, bf16[1536,4096]{1,0:T(8,128)(2,1)} %bitcast.9, bf16[32,4224]{1,0:T(8,128)(2,1)S(1)} %constant_dynamic-update-slice_fusion.refs_2_), custom_call_target="tpu_custom_call" | custom-call | bytes 12582912 | tf_op jit(solution)/shard_map/pallas_call | solution.py:97
  19.0 0.3 collective-permute-done.3
  19.4 1.6 %collective-permute-start.5 = (bf16[64,2048]{1,0:T(8,128)(2,1)S(1)}, bf16[64,2048]{1,0:T(8,128)(2,1)S(1)}, u32[]{:S(2)}, u32[]{:S(2)}) collective-permute-start(bf16[64,2048]{1,0:T(8,128)(2,1)S(1)} %pad_maximum_fusion.1.refs_1_.refs_0_), channel_id=1, source_target_pairs={{0,4},{1,3},{2,6},{3,1},{4,0},{5,7},{6,2},{7,5},{8,12},{9,11},{10,... | collective-permute-start | bytes 786440 | tf_op jit(solution)/shard_map/ppermute | solution.py:34
  21.0 0.6 collective-permute-start.4
  21.5 0.0 collective-permute-start.6
  21.5 2.8 %shard_map.76 = (bf16[1536,2048]{1,0:T(8,128)(2,1)S(1)}, bf16[128,1536]{1,0:T(8,128)(2,1)S(1)}) custom-call(bf16[1536,4096]{1,0:T(8,128)(2,1)} %bitcast.4, bf16[64,2048]{1,0:T(8,128)(2,1)S(1)} %pad_maximum_fusion.1.refs_1_.refs_0_), custom_call_target="tpu_custom_call" | custom-call | bytes 6291456 | tf_op jit(solution)/shard_map/pallas_call | solution.py:97
  24.3 1.5 %collective-permute-done.5.refs_1_ = bf16[64,2048]{1,0:T(8,128)(2,1)S(1)} collective-permute-done((bf16[64,2048]{1,0:T(8,128)(2,1)S(1)}, bf16[64,2048]{1,0:T(8,128)(2,1)S(1)}, u32[]{:S(2)}, u32[]{:S(2)}) %collective-permute-start.5) | collective-permute-done | bytes 262176 | tf_op jit(solution)/shard_map/ppermute | solution.py:34
  25.8 0.0 collective-permute-start.7
  25.8 0.5 collective-permute-start.8
  26.3 0.0 collective-permute-done.6.refs_2_
  26.3 1.0 %collective-permute-done.7.refs_3_ = bf16[64,2048]{1,0:T(8,128)(2,1)S(1)} collective-permute-done((bf16[64,2048]{1,0:T(8,128)(2,1)S(1)}, bf16[64,2048]{1,0:T(8,128)(2,1)S(1)}, u32[]{:S(2)}, u32[]{:S(2)}) %collective-permute-start.7) | collective-permute-done | bytes 262176 | tf_op jit(solution)/shard_map/ppermute | solution.py:34
  27.3 1.8 %shard_map.77 = (bf16[256,2048]{1,0:T(8,128)(2,1)S(1)}, f32[256,768]{1,0:T(8,128)S(1)}, f32[256,768]{1,0:T(8,128)S(1)}) custom-call(bf16[64,2048]{1,0:T(8,128)(2,1)S(1)} %pad_maximum_fusion.1.refs_1_.refs_0_, bf16[64,2048]{1,0:T(8,128)(2,1)S(1)} %collective-permute-done.5.refs_1_, bf16[64,2048]{1,0:T(8,128)(2,1)S(1)} %collective-permute-done.6.refs_2_, ...), custom_call_target="tpu_custom_call" | custom-call | tf_op jit(solution)/shard_map/pallas_call | solution.py:226
  29.2 0.0 collective-permute-done.4.refs_1_
  29.2 0.2 collective-permute-start.9
  29.4 1.8 %shard_map.78 = (f32[256,768]{1,0:T(8,128)S(1)}, f32[256,768]{1,0:T(8,128)S(1)}) custom-call(bf16[256,2048]{1,0:T(8,128)(2,1)S(1)} %get-tuple-element.94.refs_0_, bf16[1536,2048]{1,0:T(8,128)(2,1)S(1)} %get-tuple-element.86.refs_4_.refs_1_, bf16[1536,2048]{1,0:T(8,128)(2,1)S(1)} %get-tuple-element.87.refs_5_.refs_2_), custom_call_target="tpu_custom_call" | custom-call | tf_op jit(solution)/shard_map/pallas_call | solution.py:235
  31.2 0.0 collective-permute-done.8.refs_2_
  31.2 0.0 collective-permute-done.9.refs_3_
  31.2 4.0 %shard_map.79 = (bf16[256,1536]{1,0:T(8,128)(2,1)S(1)}, bf16[1536,2048]{1,0:T(8,128)(2,1)S(1)}) custom-call(bf16[64,2176]{1,0:T(8,128)(2,1)S(1)} %fusion.1.refs_0_, bf16[64,2176]{1,0:T(8,128)(2,1)S(1)} %collective-permute-done.4.refs_1_, bf16[64,2176]{1,0:T(8,128)(2,1)S(1)} %collective-permute-done.8.refs_2_, ...), custom_call_target="tpu_custom_call" | custom-call | tf_op jit(solution)/shard_map/pallas_call | solution.py:244
  35.3 1.8 %shard_map.81 = (f32[128,2048]{1,0:T(8,128)S(1)}, bf16[128,2048]{1,0:T(8,128)(2,1)S(1)}) custom-call(bf16[256,1536]{1,0:T(8,128)(2,1)S(1)} %get-tuple-element.98.refs_0_, bf16[1536,2048]{1,0:T(8,128)(2,1)S(1)} %get-tuple-element.102.refs_1_), custom_call_target="tpu_custom_call" | custom-call | tf_op jit(solution)/shard_map/pallas_call | solution.py:266
  37.1 0.4 collective-permute-start.13
  37.5 1.8 %shard_map.80 = (f32[128,2048]{1,0:T(8,128)S(1)}, bf16[128,2048]{1,0:T(8,128)(2,1)S(1)}) custom-call(bf16[256,1536]{1,0:T(8,128)(2,1)S(1)} %get-tuple-element.98.refs_0_, bf16[1536,2048]{1,0:T(8,128)(2,1)S(1)} %get-tuple-element.99.refs_1_), custom_call_target="tpu_custom_call" | custom-call | tf_op jit(solution)/shard_map/pallas_call | solution.py:266
  39.3 0.2 collective-permute-start.10
  39.5 0.0 collective-permute-done.13
  39.5 0.1 convert_add_fusion
  39.7 1.6 %collective-permute-start.14 = (bf16[64,2048]{1,0:T(8,128)(2,1)S(1)}, bf16[64,2048]{1,0:T(8,128)(2,1)S(1)}, u32[]{:S(2)}, u32[]{:S(2)}) collective-permute-start(bf16[64,2048]{1,0:T(8,128)(2,1)S(1)} %slice.159), channel_id=1, source_target_pairs={{0,4},{1,3},{2,6},{3,1},{4,0},{5,7},{6,2},{7,5},{8,12},{9,11},{10,... | collective-permute-start | bytes 786440 | tf_op jit(solution)/shard_map/ppermute | solution.py:34
  41.2 0.0 collective-permute-done.10
  41.3 0.1 convert_add_fusion.1
  41.4 1.6 %collective-permute-start.11 = (bf16[64,2048]{1,0:T(8,128)(2,1)S(1)}, bf16[64,2048]{1,0:T(8,128)(2,1)S(1)}, u32[]{:S(2)}, u32[]{:S(2)}) collective-permute-start(bf16[64,2048]{1,0:T(8,128)(2,1)S(1)} %slice.160), channel_id=1, source_target_pairs={{0,4},{1,3},{2,6},{3,1},{4,0},{5,7},{6,2},{7,5},{8,12},{9,11},{10,... | collective-permute-start | bytes 786440 | tf_op jit(solution)/shard_map/ppermute | solution.py:34
  43.0 3.1 %collective-permute-done.14 = bf16[64,2048]{1,0:T(8,128)(2,1)S(1)} collective-permute-done((bf16[64,2048]{1,0:T(8,128)(2,1)S(1)}, bf16[64,2048]{1,0:T(8,128)(2,1)S(1)}, u32[]{:S(2)}, u32[]{:S(2)}) %collective-permute-start.14) | collective-permute-done | bytes 262176 | tf_op jit(solution)/shard_map/ppermute | solution.py:34
  46.2 1.6 %collective-permute-start.15 = (bf16[32,2048]{1,0:T(8,128)(2,1)S(1)}, bf16[32,2048]{1,0:T(8,128)(2,1)S(1)}, u32[]{:S(2)}, u32[]{:S(2)}) collective-permute-start(bf16[32,2048]{1,0:T(8,128)(2,1)S(1)} %slice.161), channel_id=1, source_target_pairs={{0,2},{1,5},{2,0},{3,7},{4,6},{5,1},{6,4},{7,3},{8,10},{9,13},{10,... | collective-permute-start | bytes 393224 | tf_op jit(solution)/shard_map/ppermute | solution.py:34
  47.7 1.7 %collective-permute-done.11 = bf16[64,2048]{1,0:T(8,128)(2,1)S(1)} collective-permute-done((bf16[64,2048]{1,0:T(8,128)(2,1)S(1)}, bf16[64,2048]{1,0:T(8,128)(2,1)S(1)}, u32[]{:S(2)}, u32[]{:S(2)}) %collective-permute-start.11) | collective-permute-done | bytes 262176 | tf_op jit(solution)/shard_map/ppermute | solution.py:34
  49.4 0.1 slice_add_fusion.1
  49.5 1.6 %collective-permute-start.12 = (bf16[32,2048]{1,0:T(8,128)(2,1)S(1)}, bf16[32,2048]{1,0:T(8,128)(2,1)S(1)}, u32[]{:S(2)}, u32[]{:S(2)}) collective-permute-start(bf16[32,2048]{1,0:T(8,128)(2,1)S(1)} %slice.162), channel_id=1, source_target_pairs={{0,2},{1,5},{2,0},{3,7},{4,6},{5,1},{6,4},{7,3},{8,10},{9,13},{10,... | collective-permute-start | bytes 393224 | tf_op jit(solution)/shard_map/ppermute | solution.py:34
  51.0 0.2 collective-permute-done.15
  51.2 3.3 %collective-permute-done.12 = bf16[32,2048]{1,0:T(8,128)(2,1)S(1)} collective-permute-done((bf16[32,2048]{1,0:T(8,128)(2,1)S(1)}, bf16[32,2048]{1,0:T(8,128)(2,1)S(1)}, u32[]{:S(2)}, u32[]{:S(2)}) %collective-permute-start.12) | collective-permute-done | bytes 131104 | tf_op jit(solution)/shard_map/ppermute | solution.py:34
  54.6 1.5 %collective-permute-start.16 = (bf16[8,4096]{1,0:T(8,128)(2,1)S(1)}, bf16[8,4096]{1,0:T(8,128)(2,1)S(1)}, u32[]{:S(2)}, u32[]{:S(2)}) collective-permute-start(bf16[8,4096]{1,0:T(8,128)(2,1)S(1)} %get-tuple-element.105), channel_id=1, source_target_pairs={{0,8},{8,16},{16,24},{24,0},{1,9},{9,17},{17,25},{25,1},{2,10},{10... | collective-permute-start | bytes 196616 | tf_op jit(solution)/shard_map/ppermute | solution.py:34
  56.2 0.9 %collective-permute-start.17 = (bf16[8,4096]{1,0:T(8,128)(2,1)S(1)}, bf16[8,4096]{1,0:T(8,128)(2,1)S(1)}, u32[]{:S(2)}, u32[]{:S(2)}) collective-permute-start(bf16[8,4096]{1,0:T(8,128)(2,1)S(1)} %get-tuple-element.107), channel_id=1, source_target_pairs={{0,16},{8,24},{16,0},{24,8},{1,17},{9,25},{17,1},{25,9},{2,18},{10... | collective-permute-start | bytes 196616 | tf_op jit(solution)/shard_map/ppermute | solution.py:34
  57.1 2.3 %collective-permute-start.18 = (bf16[8,4096]{1,0:T(8,128)(2,1)S(1)}, bf16[8,4096]{1,0:T(8,128)(2,1)S(1)}, u32[]{:S(2)}, u32[]{:S(2)}) collective-permute-start(bf16[8,4096]{1,0:T(8,128)(2,1)S(1)} %get-tuple-element.106), channel_id=1, source_target_pairs={{0,24},{8,0},{16,8},{24,16},{1,25},{9,1},{17,9},{25,17},{2,26},{10... | collective-permute-start | bytes 196616 | tf_op jit(solution)/shard_map/ppermute | solution.py:34
  59.3 1.4 %collective-permute-done.16 = bf16[8,4096]{1,0:T(8,128)(2,1)S(1)} collective-permute-done((bf16[8,4096]{1,0:T(8,128)(2,1)S(1)}, bf16[8,4096]{1,0:T(8,128)(2,1)S(1)}, u32[]{:S(2)}, u32[]{:S(2)}) %collective-permute-start.16) | collective-permute-done | bytes 65568 | tf_op jit(solution)/shard_map/ppermute | solution.py:34
  60.8 1.4 %collective-permute-done.17 = bf16[8,4096]{1,0:T(8,128)(2,1)S(1)} collective-permute-done((bf16[8,4096]{1,0:T(8,128)(2,1)S(1)}, bf16[8,4096]{1,0:T(8,128)(2,1)S(1)}, u32[]{:S(2)}, u32[]{:S(2)}) %collective-permute-start.17) | collective-permute-done | bytes 65568 | tf_op jit(solution)/shard_map/ppermute | solution.py:34
  62.1 0.0 collective-permute-done.18
  62.1 0.7 %fusion.5 = f32[8,4096]{1,0:T(8,128)} fusion(f32[32,2048]{1,0:T(8,128)S(1)} %slice_add_fusion.3, f32[32,2048]{1,0:T(8,128)S(1)} %slice_add_fusion.2, bf16[8,4096]{1,0:T(8,128)(2,1)S(1)} %collective-permute-done.18, bf16[8,4096]{1,0:T(8,128)(2,1)S(1)} %collective-permute-done.17, bf16[8,4096]{1,0:T(8,128)(2,1)S(1)} %collective-permute-done.16), kind=kLoop, calls=%fused_computation.21 | loop fusion | flops 229376 | bytes 851968 | tf_op jit(solution)/shard_map/add | solution.py:289
  (14 shorter events, 0.3 us)
Async XLA Ops:
  1.0 10.7 %collective-permute-start = (bf16[8,4224]{1,0:T(8,128)(2,1)S(1)}, bf16[8,4224]{1,0:T(8,128)(2,1)S(1)}, u32[]{:S(2)}, u32[]{:S(2)}) collective-permute-start(bf16[8,4224]{1,0:T(8,128)(2,1)S(1)} %get-tuple-element.74.refs_2_), channel_id=1, source_target_pairs={{0,24},{8,0},{16,8},{24,16},{1,25},{9,1},{17,9},{25,17},{2,26},{10... | collective-permute-start | bytes 202760 | tf_op jit(solution)/shard_map/ppermute | solution.py:34
  6.1 6.6 %collective-permute-start.1 = (bf16[8,4224]{1,0:T(8,128)(2,1)S(1)}, bf16[8,4224]{1,0:T(8,128)(2,1)S(1)}, u32[]{:S(2)}, u32[]{:S(2)}) collective-permute-start(bf16[8,4224]{1,0:T(8,128)(2,1)S(1)} %get-tuple-element.74.refs_2_), channel_id=1, source_target_pairs={{0,16},{8,24},{16,0},{24,8},{1,17},{9,25},{17,1},{25,9},{2,18},{10... | collective-permute-start | bytes 202760 | tf_op jit(solution)/shard_map/ppermute | solution.py:34
  6.1 6.6 %collective-permute-start.2 = (bf16[8,4224]{1,0:T(8,128)(2,1)S(1)}, bf16[8,4224]{1,0:T(8,128)(2,1)S(1)}, u32[]{:S(2)}, u32[]{:S(2)}) collective-permute-start(bf16[8,4224]{1,0:T(8,128)(2,1)S(1)} %get-tuple-element.74.refs_2_), channel_id=1, source_target_pairs={{0,8},{8,16},{16,24},{24,0},{1,9},{9,17},{17,25},{25,1},{2,10},{10... | collective-permute-start | bytes 202760 | tf_op jit(solution)/shard_map/ppermute | solution.py:34
  12.8 6.5 %collective-permute-start.3 = (bf16[32,4224]{1,0:T(8,128)(2,1)S(1)}, bf16[32,4224]{1,0:T(8,128)(2,1)S(1)}, u32[]{:S(2)}, u32[]{:S(2)}) collective-permute-start(bf16[32,4224]{1,0:T(8,128)(2,1)S(1)} %constant_dynamic-update-slice_fusion.refs_2_), channel_id=1, source_target_pairs={{0,2},{1,5},{2,0},{3,7},{4,6},{5,1},{6,4},{7,3},{8,10},{9,13},{10,... | collective-permute-start | bytes 811016 | tf_op jit(solution)/shard_map/ppermute | solution.py:34
  19.4 6.4 %collective-permute-start.5 = (bf16[64,2048]{1,0:T(8,128)(2,1)S(1)}, bf16[64,2048]{1,0:T(8,128)(2,1)S(1)}, u32[]{:S(2)}, u32[]{:S(2)}) collective-permute-start(bf16[64,2048]{1,0:T(8,128)(2,1)S(1)} %pad_maximum_fusion.1.refs_1_.refs_0_), channel_id=1, source_target_pairs={{0,4},{1,3},{2,6},{3,1},{4,0},{5,7},{6,2},{7,5},{8,12},{9,11},{10,... | collective-permute-start | bytes 786440 | tf_op jit(solution)/shard_map/ppermute | solution.py:34
  21.0 8.2 %collective-permute-start.4 = (bf16[64,2176]{1,0:T(8,128)(2,1)S(1)}, bf16[64,2176]{1,0:T(8,128)(2,1)S(1)}, u32[]{:S(2)}, u32[]{:S(2)}) collective-permute-start(bf16[64,2176]{1,0:T(8,128)(2,1)S(1)} %fusion.1.refs_0_), channel_id=1, source_target_pairs={{0,4},{1,3},{2,6},{3,1},{4,0},{5,7},{6,2},{7,5},{8,12},{9,11},{10,... | collective-permute-start | bytes 835592 | tf_op jit(solution)/shard_map/ppermute | solution.py:34
  21.5 4.8 %collective-permute-start.6 = (bf16[64,2048]{1,0:T(8,128)(2,1)S(1)}, bf16[64,2048]{1,0:T(8,128)(2,1)S(1)}, u32[]{:S(2)}, u32[]{:S(2)}) collective-permute-start(bf16[64,2048]{1,0:T(8,128)(2,1)S(1)} %pad_maximum_fusion.1.refs_1_.refs_0_), channel_id=1, source_target_pairs={{0,1},{1,0},{2,3},{3,2},{4,5},{5,4},{6,7},{7,6},{8,9},{9,8},{10,11... | collective-permute-start | bytes 786440 | tf_op jit(solution)/shard_map/ppermute | solution.py:34
  25.8 1.5 %collective-permute-start.7 = (bf16[64,2048]{1,0:T(8,128)(2,1)S(1)}, bf16[64,2048]{1,0:T(8,128)(2,1)S(1)}, u32[]{:S(2)}, u32[]{:S(2)}) collective-permute-start(bf16[64,2048]{1,0:T(8,128)(2,1)S(1)} %collective-permute-done.5.refs_1_), channel_id=1, source_target_pairs={{0,1},{1,0},{2,3},{3,2},{4,5},{5,4},{6,7},{7,6},{8,9},{9,8},{10,11... | collective-permute-start | bytes 786440 | tf_op jit(solution)/shard_map/ppermute | solution.py:34
  25.8 5.4 %collective-permute-start.8 = (bf16[64,2176]{1,0:T(8,128)(2,1)S(1)}, bf16[64,2176]{1,0:T(8,128)(2,1)S(1)}, u32[]{:S(2)}, u32[]{:S(2)}) collective-permute-start(bf16[64,2176]{1,0:T(8,128)(2,1)S(1)} %fusion.1.refs_0_), channel_id=1, source_target_pairs={{0,1},{1,0},{2,3},{3,2},{4,5},{5,4},{6,7},{7,6},{8,9},{9,8},{10,11... | collective-permute-start | bytes 835592 | tf_op jit(solution)/shard_map/ppermute | solution.py:34
  29.2 2.1 %collective-permute-start.9 = (bf16[64,2176]{1,0:T(8,128)(2,1)S(1)}, bf16[64,2176]{1,0:T(8,128)(2,1)S(1)}, u32[]{:S(2)}, u32[]{:S(2)}) collective-permute-start(bf16[64,2176]{1,0:T(8,128)(2,1)S(1)} %collective-permute-done.4.refs_1_), channel_id=1, source_target_pairs={{0,1},{1,0},{2,3},{3,2},{4,5},{5,4},{6,7},{7,6},{8,9},{9,8},{10,11... | collective-permute-start | bytes 835592 | tf_op jit(solution)/shard_map/ppermute | solution.py:34
  37.1 2.4 %collective-permute-start.13 = (bf16[128,2048]{1,0:T(8,128)(2,1)S(1)}, bf16[128,2048]{1,0:T(8,128)(2,1)S(1)}, u32[]{:S(2)}, u32[]{:S(2)}) collective-permute-start(bf16[128,2048]{1,0:T(8,128)(2,1)S(1)} %get-tuple-element.104), channel_id=1, source_target_pairs={{0,1},{1,0},{2,3},{3,2},{4,5},{5,4},{6,7},{7,6},{8,9},{9,8},{10,11... | collective-permute-start | bytes 1572872 | tf_op jit(solution)/shard_map/ppermute | solution.py:34
  39.3 2.0 %collective-permute-start.10 = (bf16[128,2048]{1,0:T(8,128)(2,1)S(1)}, bf16[128,2048]{1,0:T(8,128)(2,1)S(1)}, u32[]{:S(2)}, u32[]{:S(2)}) collective-permute-start(bf16[128,2048]{1,0:T(8,128)(2,1)S(1)} %get-tuple-element.101), channel_id=1, source_target_pairs={{0,1},{1,0},{2,3},{3,2},{4,5},{5,4},{6,7},{7,6},{8,9},{9,8},{10,11... | collective-permute-start | bytes 1572872 | tf_op jit(solution)/shard_map/ppermute | solution.py:34
  39.7 6.4 %collective-permute-start.14 = (bf16[64,2048]{1,0:T(8,128)(2,1)S(1)}, bf16[64,2048]{1,0:T(8,128)(2,1)S(1)}, u32[]{:S(2)}, u32[]{:S(2)}) collective-permute-start(bf16[64,2048]{1,0:T(8,128)(2,1)S(1)} %slice.159), channel_id=1, source_target_pairs={{0,4},{1,3},{2,6},{3,1},{4,0},{5,7},{6,2},{7,5},{8,12},{9,11},{10,... | collective-permute-start | bytes 786440 | tf_op jit(solution)/shard_map/ppermute | solution.py:34
  41.4 8.0 %collective-permute-start.11 = (bf16[64,2048]{1,0:T(8,128)(2,1)S(1)}, bf16[64,2048]{1,0:T(8,128)(2,1)S(1)}, u32[]{:S(2)}, u32[]{:S(2)}) collective-permute-start(bf16[64,2048]{1,0:T(8,128)(2,1)S(1)} %slice.160), channel_id=1, source_target_pairs={{0,4},{1,3},{2,6},{3,1},{4,0},{5,7},{6,2},{7,5},{8,12},{9,11},{10,... | collective-permute-start | bytes 786440 | tf_op jit(solution)/shard_map/ppermute | solution.py:34
  46.2 5.0 %collective-permute-start.15 = (bf16[32,2048]{1,0:T(8,128)(2,1)S(1)}, bf16[32,2048]{1,0:T(8,128)(2,1)S(1)}, u32[]{:S(2)}, u32[]{:S(2)}) collective-permute-start(bf16[32,2048]{1,0:T(8,128)(2,1)S(1)} %slice.161), channel_id=1, source_target_pairs={{0,2},{1,5},{2,0},{3,7},{4,6},{5,1},{6,4},{7,3},{8,10},{9,13},{10,... | collective-permute-start | bytes 393224 | tf_op jit(solution)/shard_map/ppermute | solution.py:34
  49.5 5.0 %collective-permute-start.12 = (bf16[32,2048]{1,0:T(8,128)(2,1)S(1)}, bf16[32,2048]{1,0:T(8,128)(2,1)S(1)}, u32[]{:S(2)}, u32[]{:S(2)}) collective-permute-start(bf16[32,2048]{1,0:T(8,128)(2,1)S(1)} %slice.162), channel_id=1, source_target_pairs={{0,2},{1,5},{2,0},{3,7},{4,6},{5,1},{6,4},{7,3},{8,10},{9,13},{10,... | collective-permute-start | bytes 393224 | tf_op jit(solution)/shard_map/ppermute | solution.py:34
  54.6 6.1 %collective-permute-start.16 = (bf16[8,4096]{1,0:T(8,128)(2,1)S(1)}, bf16[8,4096]{1,0:T(8,128)(2,1)S(1)}, u32[]{:S(2)}, u32[]{:S(2)}) collective-permute-start(bf16[8,4096]{1,0:T(8,128)(2,1)S(1)} %get-tuple-element.105), channel_id=1, source_target_pairs={{0,8},{8,16},{16,24},{24,0},{1,9},{9,17},{17,25},{25,1},{2,10},{10... | collective-permute-start | bytes 196616 | tf_op jit(solution)/shard_map/ppermute | solution.py:34
  56.2 6.0 %collective-permute-start.17 = (bf16[8,4096]{1,0:T(8,128)(2,1)S(1)}, bf16[8,4096]{1,0:T(8,128)(2,1)S(1)}, u32[]{:S(2)}, u32[]{:S(2)}) collective-permute-start(bf16[8,4096]{1,0:T(8,128)(2,1)S(1)} %get-tuple-element.107), channel_id=1, source_target_pairs={{0,16},{8,24},{16,0},{24,8},{1,17},{9,25},{17,1},{25,9},{2,18},{10... | collective-permute-start | bytes 196616 | tf_op jit(solution)/shard_map/ppermute | solution.py:34
  57.1 5.1 %collective-permute-start.18 = (bf16[8,4096]{1,0:T(8,128)(2,1)S(1)}, bf16[8,4096]{1,0:T(8,128)(2,1)S(1)}, u32[]{:S(2)}, u32[]{:S(2)}) collective-permute-start(bf16[8,4096]{1,0:T(8,128)(2,1)S(1)} %get-tuple-element.106), channel_id=1, source_target_pairs={{0,24},{8,0},{16,8},{24,16},{1,25},{9,1},{17,9},{25,17},{2,26},{10... | collective-permute-start | bytes 196616 | tf_op jit(solution)/shard_map/ppermute | solution.py:34

commit v4 on v3

v4 whole, which is shorter than its diff:
```python
import jax
import jax.numpy as jnp
from jax import lax
from jax.experimental import pallas as pl
from jax.experimental.pallas import tpu as pltpu
from jax.sharding import PartitionSpec as P

LANES = 128
F32 = jnp.float32
BF16 = jnp.bfloat16
MIB = 1 << 20
AG_CUT = 1792
RS_CUTS = (2048, 2048)
ROWS_FIRST = 768
P1_SPLIT = False
AG_ORDER = (3, 2, 1)
RS_ORDER = (2, 1, 3)
XOR = False
IN_VMEM = pl.BlockSpec(memory_space=pltpu.VMEM)
IN_HBM = pl.BlockSpec(memory_space=pltpu.HBM)
ANYWHERE = pl.BlockSpec(memory_space=pl.ANY)


def near(value):
    return pltpu.with_memory_space_constraint(value, pltpu.VMEM)


def far(value):
    return pltpu.with_memory_space_constraint(value, pltpu.HBM)


def swap(value, axis, to):
    return lax.ppermute(value, axis, [(i, to(i)) for i in range(lax.axis_size(axis))])


def hop(distance, size):
    if XOR:
        return lambda i: i ^ abs(distance)
    return lambda i: (i + distance) % size


def order_of(order, size):
    return order if len(order) == size - 1 else range(size - 1, 0, -1)


def partner(step, steps):
    return lambda i: i ^ (2 << (step if i % 2 == 0 else steps - 1 - step))


def fold(total, step, steps):
    count = total.shape[0] // 2
    back = swap(total[count:].astype(BF16), "expert", partner(step, steps))
    return total[:count] + back.astype(F32)


def pack_kernel(stream_ref, gain_ref, ids_ref, weights_ref, own_ref, *half_refs, experts):
    stream = stream_ref[...].astype(F32)
    inverse = lax.rsqrt(jnp.mean(stream * stream, axis=-1, keepdims=True) + 1e-06)
    rows, features = stream.shape
    for i in range(features // LANES):
        here = slice(i * LANES, (i + 1) * LANES)
        own_ref[:, here] = (stream[:, here] * inverse * gain_ref[i : i + 1, :].astype(F32)).astype(BF16)
    width = own_ref.shape[1] - features
    column = lax.broadcasted_iota(jnp.int32, (rows, width), 1)
    dense = jnp.zeros((rows, width), F32)
    for k in range(ids_ref.shape[1]):
        expert = ids_ref[:, k : k + 1]
        weight = weights_ref[:, k : k + 1]
        high = weight.astype(BF16).astype(F32)
        middle = (weight - high).astype(BF16).astype(F32)
        low = weight - high - middle
        dense = dense + jnp.where(column == expert, high, 0.0)
        dense = dense + jnp.where(column == expert + experts, middle, 0.0)
        dense = dense + jnp.where(column == expert + 2 * experts, low, 0.0)
    own_ref[:, features:] = dense.astype(BF16)
    at = 0
    for ref in half_refs:
        ref[...] = jnp.zeros_like(ref)
        ref[:rows, :] = own_ref[:, at : at + ref.shape[1]]
        at += ref.shape[1]


def fetches(cuts, source_refs, out_refs, sems):
    return [
        pltpu.make_async_copy(source_refs[source].at[pl.ds(*rows), pl.ds(*columns)], out_refs[i], sems.at[i])
        for i, (source, rows, columns) in enumerate(cuts)
    ]


def load_kernel(*refs, sources, cuts, experts):
    out_refs = refs[sources + 1 : -1]
    copies = fetches(cuts, refs[:sources], out_refs, refs[-1])
    for copy in copies:
        copy.start()
    if experts:
        spread_ref = out_refs[-1]
        held = experts // lax.axis_size("expert")
        lane = lax.broadcasted_iota(jnp.int32, spread_ref.shape, 0)
        unit = lax.broadcasted_iota(jnp.int32, spread_ref.shape, 1)
        owner = lax.axis_index("expert") * held + unit // (spread_ref.shape[1] // held)
        hit = (lane == owner) | (lane == owner + experts) | (lane == owner + 2 * experts)
        spread_ref[...] = jnp.where(hit, 1.0, 0.0).astype(BF16)
    for copy in copies:
        copy.wait()


def loaded(cuts):
    return [pltpu.VMEM((rows[1], columns[1]), BF16) for _, rows, columns in cuts]


def load(arrays, cuts, after, experts=0, width=0):
    hidden = arrays[0].shape[0]
    outs = loaded(cuts) + [pltpu.VMEM((width, hidden), BF16)] * bool(experts)
    return pl.pallas_call(
        lambda *refs: load_kernel(*refs, sources=len(arrays), cuts=cuts, experts=experts),
        out_shape=outs,
        in_specs=[IN_HBM] * len(arrays) + [ANYWHERE],
        out_specs=[IN_VMEM] * len(outs),
        scratch_shapes=[pltpu.SemaphoreType.DMA((len(cuts),))],
        compiler_params=params(1),
        cost_estimate=NO_COST,
    )(*[far(a) for a in arrays], after)


def dot_rows(rows, matrix):
    return lax.dot_general(rows, matrix, (((1,), (1,)), ((), ())), preferred_element_type=F32)


def gate_up(rows, gate_ref, up_ref, at, block):
    here = slice(at, at + block)
    both = dot_rows(rows, jnp.concatenate([gate_ref[here], up_ref[here]], axis=0))
    return both[:, :block], both[:, block:]


def first_kernel(*refs, pieces, block):
    piece_refs = refs[:pieces]
    gate_ref, up_ref, rows_ref, gate_out, up_out = refs[pieces:]
    count = piece_refs[0].shape[0]
    for i, ref in enumerate(piece_refs):
        rows_ref[i * count : (i + 1) * count, :] = ref[...]
    for j in range(0, gate_out.shape[1], block):
        gate_out[:, j : j + block], up_out[:, j : j + block] = gate_up(rows_ref[...], gate_ref, up_ref, j, block)


def middle_kernel(rows_ref, gate_ref, up_ref, gate_out, up_out, *, block, start):
    for j in range(0, gate_out.shape[1], block):
        gate_out[:, j : j + block], up_out[:, j : j + block] = gate_up(
            rows_ref[...], gate_ref, up_ref, start + j, block
        )


def second_kernel(*refs, pieces, block, part, cuts):
    piece_refs = refs[:pieces]
    gate_ref, up_ref, *sums = refs[pieces : pieces + 6]
    spread_ref, down_hbm, act_ref, *down_refs, rows_ref, sems = refs[pieces + 6 :]
    copies = fetches(cuts, (down_hbm,), down_refs, sems)
    for copy in copies:
        copy.start()
    count = piece_refs[0].shape[0]
    for i, ref in enumerate(piece_refs):
        rows_ref[i * count : (i + 1) * count, :] = ref[...]
    cut = sums[0].shape[1]
    for j in range(0, gate_ref.shape[0], block):
        here = slice(j, j + block)
        gate, up = gate_up(rows_ref[:, :part], gate_ref, up_ref, j, block)
        weight = jnp.dot(rows_ref[:, part:], spread_ref[:, here], preferred_element_type=F32)
        gate_in, up_in = sums[:2] if j < cut else sums[2:]
        at = j if j < cut else j - cut
        gate, up = gate + gate_in[:, at : at + block], up + up_in[:, at : at + block]
        act_ref[:, here] = (gate / (1.0 + jnp.exp(-gate)) * up * weight).astype(BF16)
    for copy in copies:
        copy.wait()


def down_kernel(act_ref, down_ref, keep_ref, send_ref, *, chunk):
    half = keep_ref.shape[0]
    for j in range(keep_ref.shape[1] // chunk):
        here = slice(j * chunk, (j + 1) * chunk)
        out = jnp.dot(act_ref[...], down_ref[:, here], preferred_element_type=F32)
        keep_ref[:, here] = out[:half]
        send_ref[:, here] = out[half:].astype(BF16)


def params(mib):
    return pltpu.CompilerParams(vmem_limit_bytes=mib * MIB)


NO_COST = pl.CostEstimate(flops=0, bytes_accessed=0, transcendentals=0)


def local(stream_in, norm_gain, expert_ids, route_weights, w_gate, w_up, w_down):
    row_count, features = stream_in.shape
    held, slice_size, _ = w_gate.shape
    attn_size = lax.axis_size("attn")
    expert_size = lax.axis_size("expert")
    experts = held * expert_size
    width = -(-3 * experts // LANES) * LANES
    hidden = held * slice_size
    rest = features - AG_CUT
    tokens = row_count * attn_size * expert_size
    half = tokens // 2
    steps = (expert_size // 2).bit_length() - 1
    cut = ROWS_FIRST * hidden // 1536
    every = (0, hidden)
    beside = lambda i: i ^ 1

    w_gate = w_gate.reshape(hidden, features)
    w_up = w_up.reshape(hidden, features)
    w_down = w_down.reshape(hidden, features)

    own, column = pl.pallas_call(
        lambda *refs: pack_kernel(*refs, experts=experts),
        out_shape=[
            pltpu.VMEM((row_count, features + width), BF16),
            pltpu.VMEM((row_count * attn_size, features + width), BF16),
        ],
    )(stream_in, norm_gain.reshape(features // LANES, LANES), expert_ids, route_weights)

    received = {d: swap(own, "attn", hop(d, attn_size)) for d in order_of(AG_ORDER, attn_size)}
    (gate_1,) = load([w_gate], [(0, every, (0, AG_CUT))], own)
    *values, gate_1 = lax.optimization_barrier((*received.values(), gate_1))
    for d, value in zip(received, values):
        column = column.at[d * row_count : (d + 1) * row_count].set(value)

    gate_2, up_1 = load([w_gate, w_up], [(0, every, (AG_CUT, rest)), (1, every, (0, AG_CUT))], column)
    columns = [column[:, :AG_CUT], column[:, AG_CUT:]] if P1_SPLIT else [column]
    for step in range(steps - 1):
        others = [swap(value, "expert", partner(step, steps)) for value in columns]
        if step == 0:
            others[0], gate_2, up_1 = lax.optimization_barrier((others[0], gate_2, up_1))
        columns = [jnp.concatenate(pair, axis=0) for pair in zip(columns, others)]
    if not P1_SPLIT:
        columns = [columns[0][:, :AG_CUT], columns[0][:, AG_CUT:]]
    up_2, spread = load([w_up], [(0, every, (AG_CUT, rest))], columns[0], experts, width)
    others = [swap(value, "expert", partner(steps - 1, steps)) for value in columns]
    others[0], up_2, spread = lax.optimization_barrier((others[0], up_2, spread))

    def both_of_pair(pieces):
        return pieces + [swap(piece, "expert", beside) for piece in pieces]

    pieces = both_of_pair([columns[0], others[0]])
    count = len(pieces)
    rows, gate_a, up_a = pl.pallas_call(
        lambda *refs: first_kernel(*refs, pieces=count, block=LANES),
        out_shape=[pltpu.VMEM((tokens, AG_CUT), BF16)] + [pltpu.VMEM((tokens, cut), F32)] * 2,
        in_specs=[IN_VMEM] * (count + 2),
        out_specs=[IN_VMEM] * 3,
        compiler_params=params(6),
        cost_estimate=NO_COST,
    )(*pieces, near(gate_1), near(up_1))
    others[1], rows = lax.optimization_barrier((others[1], rows))
    gate_b, up_b = pl.pallas_call(
        lambda *refs: middle_kernel(*refs, block=LANES, start=cut),
        out_shape=[pltpu.VMEM((tokens, hidden - cut), F32)] * 2,
        in_specs=[IN_VMEM] * 3,
        out_specs=[IN_VMEM] * 2,
        compiler_params=params(6),
        cost_estimate=NO_COST,
    )(near(rows), near(gate_1), near(up_1))
    pieces = both_of_pair([columns[1], others[1]])
    starts = [sum(RS_CUTS[:i]) for i in range(len(RS_CUTS))]
    cuts = [(0, every, (at, size)) for at, size in zip(starts, RS_CUTS)]
    act, *downs = pl.pallas_call(
        lambda *refs: second_kernel(*refs, pieces=count, block=LANES, part=rest, cuts=cuts),
        out_shape=[pltpu.VMEM((tokens, hidden), BF16)] + loaded(cuts),
        in_specs=[IN_VMEM] * (count + 7) + [IN_HBM],
        out_specs=[IN_VMEM] * (1 + len(cuts)),
        scratch_shapes=[pltpu.VMEM((tokens, rest + width), BF16), pltpu.SemaphoreType.DMA((len(cuts),))],
        compiler_params=params(6),
        cost_estimate=NO_COST,
    )(
        *pieces,
        *[near(value) for value in (gate_2, up_2, gate_a, up_a, gate_b, up_b, spread)],
        far(w_down),
    )

    outs = []
    for size, down in zip(RS_CUTS, downs):
        keep, send = pl.pallas_call(
            lambda *refs: down_kernel(*refs, chunk=512),
            out_shape=[pltpu.VMEM((half, size), F32), pltpu.VMEM((half, size), BF16)],
            in_specs=[IN_VMEM] * 2,
            out_specs=[IN_VMEM] * 2,
            compiler_params=params(12),
            cost_estimate=NO_COST,
        )(near(act), near(down))
        total = keep + swap(send, "expert", beside).astype(F32)
        for step in reversed(range(steps)):
            total = fold(total, step, steps)
        outs.append(total)
    total = jnp.concatenate(outs, axis=1).reshape(attn_size, row_count, features)
    back = [swap(total[d].astype(BF16), "attn", hop(-d, attn_size)) for d in order_of(RS_ORDER, attn_size)]
    return sum([value.astype(F32) for value in back], total[0])


def solution(mesh):
    return jax.shard_map(
        local,
        mesh=mesh,
        in_specs=(
            P(("attn", "expert"), None),
            P(),
            P(("attn", "expert"), None),
            P(("attn", "expert"), None),
            P("expert", "attn", None),
            P("expert", "attn", None),
            P("expert", "attn", None),
        ),
        out_specs=P(("attn", "expert"), None),
        check_vma=False,
    )
```

time: 63 us -> 62.5 us (level)
  starting transfers between devices: 22.2 us -> 23.4 us
  Pallas kernels: 24.3 us -> 23.2 us
    pallas_call x3, Pallas kernels: 12 us -> 10.2 us  [load(): pl.pallas_call(lambda *refs: load_kernel(*refs, sources=len(arrays), cuts...]
    pallas_call x1, Pallas kernels: 4.04 us -> 5.23 us  [local(): pl.pallas_call(lambda *refs: second_kernel(*refs, pieces=count, block=LAN...]
    ppermute x19, starting transfers between devices: 22.2 us -> 23.4 us  [swap(): lax.ppermute(value, axis, [(i, to(i)) for i in range(lax.axis_size(axis))])]
  transfers between devices with their start and end apart: 19 -> 19, of which waited for: 10 -> 14; matrix products, arithmetic and copies ran while one was open for 1% -> 1% of each run, Pallas kernels for 28% -> 24%
where the time goes in v4:
time: 62.5 us; the launch traced here: 62.3 us
  starting transfers between devices  23.4 us (37%)
  Pallas kernels  23.2 us (37%)
  waiting for transfers between devices  14.3 us (23%)
  other arithmetic  1.12 us (2%)
    ppermute x19, starting transfers between devices, swap(): lax.ppermute(value, axis, [(i, to(i)) for i in range(lax.axis_size(axis))])  23.4 us
    ppermute x19, waiting for transfers between devices, swap(): lax.ppermute(value, axis, [(i, to(i)) for i in range(lax.axis_size(axis))])  14.3 us
    pallas_call x3, Pallas kernels, load(): pl.pallas_call(lambda *refs: load_kernel(*refs, sources=len(arrays), cuts...  10.2 us
    pallas_call x1, Pallas kernels, local(): pl.pallas_call(lambda *refs: second_kernel(*refs, pieces=count, block=LAN...  5.23 us
    pallas_call x2, Pallas kernels, local(): pl.pallas_call(lambda *refs: down_kernel(*refs, chunk=512), out_shape=[pl...  3.57 us
    pallas_call x1, Pallas kernels, local(): pl.pallas_call(lambda *refs: first_kernel(*refs, pieces=count, block=LANE...  1.61 us
    pallas_call x1, Pallas kernels, local(): pl.pallas_call(lambda *refs: middle_kernel(*refs, block=LANES, start=cut)...  1.61 us
  transfers between devices with their start and end apart: 19, of which 14 were waited for; matrix products, arithmetic and copies ran while one was open for 1% of the time, Pallas kernels for 24%

profile of v4, /device:TPU:0, one launch (start us, length us, event | category | flops | bytes accessed | tf_op | source)
XLA Modules:
  0.0 62.3 jit_solution(16307904169266974116)
XLA Ops:
  0.0 1.0 %shard_map.73 = (bf16[8,4224]{1,0:T(8,128)(2,1)S(1)}, bf16[32,4224]{1,0:T(8,128)(2,1)S(1)}) custom-call(bf16[8,4096]{1,0:T(8,128)(2,1)} %refs_0_.1, bf16[32,128]{1,0:T(8,128)(2,1)} %bitcast.9, s32[8,8]{1,0:T(8,128)} %refs_2_.1, f32[8,8]{1,0:T(8,128)} %refs_3_.1), custom_call_target="tpu_custom_call" | custom-call | tf_op jit(solution)/shard_map/pallas_call | solution.py:211
  1.0 3.1 %collective-permute-start.2 = (bf16[8,4224]{1,0:T(8,128)(2,1)S(1)}, bf16[8,4224]{1,0:T(8,128)(2,1)S(1)}, u32[]{:S(2)}, u32[]{:S(2)}) collective-permute-start(bf16[8,4224]{1,0:T(8,128)(2,1)S(1)} %get-tuple-element.72.refs_1_), channel_id=1, source_target_pairs={{0,8},{8,16},{16,24},{24,0},{1,9},{9,17},{17,25},{25,1},{2,10},{10... | collective-permute-start | bytes 202760 | tf_op jit(solution)/shard_map/ppermute | solution.py:33
  4.1 2.6 %collective-permute-start.1 = (bf16[8,4224]{1,0:T(8,128)(2,1)S(1)}, bf16[8,4224]{1,0:T(8,128)(2,1)S(1)}, u32[]{:S(2)}, u32[]{:S(2)}) collective-permute-start(bf16[8,4224]{1,0:T(8,128)(2,1)S(1)} %get-tuple-element.72.refs_1_), channel_id=1, source_target_pairs={{0,16},{8,24},{16,0},{24,8},{1,17},{9,25},{17,1},{25,9},{2,18},{10... | collective-permute-start | bytes 202760 | tf_op jit(solution)/shard_map/ppermute | solution.py:33
  6.7 1.3 %collective-permute-start = (bf16[8,4224]{1,0:T(8,128)(2,1)S(1)}, bf16[8,4224]{1,0:T(8,128)(2,1)S(1)}, u32[]{:S(2)}, u32[]{:S(2)}) collective-permute-start(bf16[8,4224]{1,0:T(8,128)(2,1)S(1)} %get-tuple-element.72.refs_1_), channel_id=1, source_target_pairs={{0,24},{8,0},{16,8},{24,16},{1,25},{9,1},{17,9},{25,17},{2,26},{10... | collective-permute-start | bytes 202760 | tf_op jit(solution)/shard_map/ppermute | solution.py:33
  8.0 2.6 %shard_map.74.refs_4_.refs_1_ = bf16[1536,1792]{1,0:T(8,128)(2,1)S(1)} custom-call(bf16[1536,4096]{1,0:T(8,128)(2,1)} %bitcast.4, bf16[8,4224]{1,0:T(8,128)(2,1)S(1)} %get-tuple-element.72.refs_1_), custom_call_target="tpu_custom_call" | custom-call | tf_op jit(solution)/shard_map/pallas_call | solution.py:114
  10.6 0.0 collective-permute-done.2
  10.6 0.7 %collective-permute-done.1 = bf16[8,4224]{1,0:T(8,128)(2,1)S(1)} collective-permute-done((bf16[8,4224]{1,0:T(8,128)(2,1)S(1)}, bf16[8,4224]{1,0:T(8,128)(2,1)S(1)}, u32[]{:S(2)}, u32[]{:S(2)}) %collective-permute-start.1) | collective-permute-done | bytes 67616 | tf_op jit(solution)/shard_map/ppermute | solution.py:33
  11.3 0.2 collective-permute-done
  11.5 1.7 %collective-permute-start.3 = (bf16[32,4224]{1,0:T(8,128)(2,1)S(1)}, bf16[32,4224]{1,0:T(8,128)(2,1)S(1)}, u32[]{:S(2)}, u32[]{:S(2)}) collective-permute-start(bf16[32,4224]{1,0:T(8,128)(2,1)S(1)} %constant_dynamic-update-slice_fusion.refs_2_), channel_id=1, source_target_pairs={{0,2},{1,5},{2,0},{3,7},{4,6},{5,1},{6,4},{7,3},{8,10},{9,13},{10,... | collective-permute-start | bytes 811016 | tf_op jit(solution)/shard_map/ppermute | solution.py:33
  13.2 4.6 %shard_map.75 = (bf16[1536,2304]{1,0:T(8,128)(2,1)S(1)}, bf16[1536,1792]{1,0:T(8,128)(2,1)S(1)}) custom-call(bf16[1536,4096]{1,0:T(8,128)(2,1)} %bitcast.5, bf16[1536,4096]{1,0:T(8,128)(2,1)} %bitcast.6, bf16[32,4224]{1,0:T(8,128)(2,1)S(1)} %constant_dynamic-update-slice_fusion.refs_2_), custom_call_target="tpu_custom_call" | custom-call | tf_op jit(solution)/shard_map/pallas_call | solution.py:114
  17.8 0.3 collective-permute-done.3
  18.0 1.7 %collective-permute-start.5 = (bf16[64,1792]{1,0:T(8,128)(2,1)S(1)}, bf16[64,1792]{1,0:T(8,128)(2,1)S(1)}, u32[]{:S(2)}, u32[]{:S(2)}) collective-permute-start(bf16[64,1792]{1,0:T(8,128)(2,1)S(1)} %pad_maximum_fusion.1.refs_1_.refs_0_), channel_id=1, source_target_pairs={{0,4},{1,3},{2,6},{3,1},{4,0},{5,7},{6,2},{7,5},{8,12},{9,11},{10,... | collective-permute-start | bytes 688136 | tf_op jit(solution)/shard_map/ppermute | solution.py:33
  19.8 0.5 collective-permute-start.4
  20.2 0.0 collective-permute-start.6
  20.2 3.0 %shard_map.76 = (bf16[1536,2304]{1,0:T(8,128)(2,1)S(1)}, bf16[128,1536]{1,0:T(8,128)(2,1)S(1)}) custom-call(bf16[1536,4096]{1,0:T(8,128)(2,1)} %bitcast.7, bf16[64,1792]{1,0:T(8,128)(2,1)S(1)} %pad_maximum_fusion.1.refs_1_.refs_0_), custom_call_target="tpu_custom_call" | custom-call | tf_op jit(solution)/shard_map/pallas_call | solution.py:114
  23.3 0.9 %collective-permute-done.5.refs_1_ = bf16[64,1792]{1,0:T(8,128)(2,1)S(1)} collective-permute-done((bf16[64,1792]{1,0:T(8,128)(2,1)S(1)}, bf16[64,1792]{1,0:T(8,128)(2,1)S(1)}, u32[]{:S(2)}, u32[]{:S(2)}) %collective-permute-start.5) | collective-permute-done | bytes 229408 | tf_op jit(solution)/shard_map/ppermute | solution.py:33
  24.1 0.0 collective-permute-start.7
  24.1 0.5 collective-permute-start.8
  24.6 0.0 collective-permute-done.6.refs_2_
  24.6 1.0 %collective-permute-done.7.refs_3_ = bf16[64,1792]{1,0:T(8,128)(2,1)S(1)} collective-permute-done((bf16[64,1792]{1,0:T(8,128)(2,1)S(1)}, bf16[64,1792]{1,0:T(8,128)(2,1)S(1)}, u32[]{:S(2)}, u32[]{:S(2)}) %collective-permute-start.7) | collective-permute-done | bytes 229408 | tf_op jit(solution)/shard_map/ppermute | solution.py:33
  25.6 1.6 %shard_map.77 = (bf16[256,1792]{1,0:T(8,128)(2,1)S(1)}, f32[256,768]{1,0:T(8,128)S(1)}, f32[256,768]{1,0:T(8,128)S(1)}) custom-call(bf16[64,1792]{1,0:T(8,128)(2,1)S(1)} %pad_maximum_fusion.1.refs_1_.refs_0_, bf16[64,1792]{1,0:T(8,128)(2,1)S(1)} %collective-permute-done.5.refs_1_, bf16[64,1792]{1,0:T(8,128)(2,1)S(1)} %collective-permute-done.6.refs_2_, ...), custom_call_target="tpu_custom_call" | custom-call | tf_op jit(solution)/shard_map/pallas_call | solution.py:243
  27.2 0.2 collective-permute-done.4.refs_1_
  27.5 0.0 collective-permute-start.9
  27.5 1.6 %shard_map.78 = (f32[256,768]{1,0:T(8,128)S(1)}, f32[256,768]{1,0:T(8,128)S(1)}) custom-call(bf16[256,1792]{1,0:T(8,128)(2,1)S(1)} %get-tuple-element.90.refs_0_, bf16[1536,1792]{1,0:T(8,128)(2,1)S(1)} %shard_map.74.refs_4_.refs_1_, bf16[1536,1792]{1,0:T(8,128)(2,1)S(1)} %get-tuple-element.83.refs_5_.refs_2_), custom_call_target="tpu_custom_call" | custom-call | tf_op jit(solution)/shard_map/pallas_call | solution.py:252
  29.1 0.0 collective-permute-done.8.refs_2_
  29.1 0.0 collective-permute-done.9.refs_3_
  29.1 5.2 %shard_map.79 = (bf16[256,1536]{1,0:T(8,128)(2,1)S(1)}, bf16[1536,2048]{1,0:T(8,128)(2,1)S(1)}, bf16[1536,2048]{1,0:T(8,128)(2,1)S(1)}) custom-call(bf16[64,2432]{1,0:T(8,128)(2,1)S(1)} %fusion.1.refs_0_, bf16[64,2432]{1,0:T(8,128)(2,1)S(1)} %collective-permute-done.4.refs_1_, bf16[64,2432]{1,0:T(8,128)(2,1)S(1)} %collective-permute-done.8.refs_2_, ...), custom_call_target="tpu_custom_call" | custom-call | tf_op jit(solution)/shard_map/pallas_call | solution.py:263
  34.4 1.8 %shard_map.80 = (f32[128,2048]{1,0:T(8,128)S(1)}, bf16[128,2048]{1,0:T(8,128)(2,1)S(1)}) custom-call(bf16[256,1536]{1,0:T(8,128)(2,1)S(1)} %get-tuple-element.94.refs_0_, bf16[1536,2048]{1,0:T(8,128)(2,1)S(1)} %get-tuple-element.95.refs_1_), custom_call_target="tpu_custom_call" | custom-call | tf_op jit(solution)/shard_map/pallas_call | solution.py:279
  36.1 0.6 collective-permute-start.10
  36.7 1.8 %shard_map.81 = (f32[128,2048]{1,0:T(8,128)S(1)}, bf16[128,2048]{1,0:T(8,128)(2,1)S(1)}) custom-call(bf16[256,1536]{1,0:T(8,128)(2,1)S(1)} %get-tuple-element.94.refs_0_, bf16[1536,2048]{1,0:T(8,128)(2,1)S(1)} %get-tuple-element.98.refs_1_), custom_call_target="tpu_custom_call" | custom-call | tf_op jit(solution)/shard_map/pallas_call | solution.py:279
  38.5 0.1 collective-permute-start.13
  38.6 0.0 collective-permute-done.10
  38.6 0.1 convert_add_fusion.1
  38.7 1.7 %collective-permute-start.11 = (bf16[64,2048]{1,0:T(8,128)(2,1)S(1)}, bf16[64,2048]{1,0:T(8,128)(2,1)S(1)}, u32[]{:S(2)}, u32[]{:S(2)}) collective-permute-start(bf16[64,2048]{1,0:T(8,128)(2,1)S(1)} %slice.160), channel_id=1, source_target_pairs={{0,4},{1,3},{2,6},{3,1},{4,0},{5,7},{6,2},{7,5},{8,12},{9,11},{10,... | collective-permute-start | bytes 786440 | tf_op jit(solution)/shard_map/ppermute | solution.py:33
  40.4 0.1 collective-permute-done.13
  40.5 0.1 convert_add_fusion
  40.6 1.7 %collective-permute-start.14 = (bf16[64,2048]{1,0:T(8,128)(2,1)S(1)}, bf16[64,2048]{1,0:T(8,128)(2,1)S(1)}, u32[]{:S(2)}, u32[]{:S(2)}) collective-permute-start(bf16[64,2048]{1,0:T(8,128)(2,1)S(1)} %slice.159), channel_id=1, source_target_pairs={{0,4},{1,3},{2,6},{3,1},{4,0},{5,7},{6,2},{7,5},{8,12},{9,11},{10,... | collective-permute-start | bytes 786440 | tf_op jit(solution)/shard_map/ppermute | solution.py:33
  42.3 2.9 %collective-permute-done.11 = bf16[64,2048]{1,0:T(8,128)(2,1)S(1)} collective-permute-done((bf16[64,2048]{1,0:T(8,128)(2,1)S(1)}, bf16[64,2048]{1,0:T(8,128)(2,1)S(1)}, u32[]{:S(2)}, u32[]{:S(2)}) %collective-permute-start.11) | collective-permute-done | bytes 262176 | tf_op jit(solution)/shard_map/ppermute | solution.py:33
  45.3 1.7 %collective-permute-start.12 = (bf16[32,2048]{1,0:T(8,128)(2,1)S(1)}, bf16[32,2048]{1,0:T(8,128)(2,1)S(1)}, u32[]{:S(2)}, u32[]{:S(2)}) collective-permute-start(bf16[32,2048]{1,0:T(8,128)(2,1)S(1)} %slice.162), channel_id=1, source_target_pairs={{0,2},{1,5},{2,0},{3,7},{4,6},{5,1},{6,4},{7,3},{8,10},{9,13},{10,... | collective-permute-start | bytes 393224 | tf_op jit(solution)/shard_map/ppermute | solution.py:33
  46.9 1.4 %collective-permute-done.14 = bf16[64,2048]{1,0:T(8,128)(2,1)S(1)} collective-permute-done((bf16[64,2048]{1,0:T(8,128)(2,1)S(1)}, bf16[64,2048]{1,0:T(8,128)(2,1)S(1)}, u32[]{:S(2)}, u32[]{:S(2)}) %collective-permute-start.14) | collective-permute-done | bytes 262176 | tf_op jit(solution)/shard_map/ppermute | solution.py:33
  48.4 0.1 slice_add_fusion
  48.5 1.7 %collective-permute-start.15 = (bf16[32,2048]{1,0:T(8,128)(2,1)S(1)}, bf16[32,2048]{1,0:T(8,128)(2,1)S(1)}, u32[]{:S(2)}, u32[]{:S(2)}) collective-permute-start(bf16[32,2048]{1,0:T(8,128)(2,1)S(1)} %slice.161), channel_id=1, source_target_pairs={{0,2},{1,5},{2,0},{3,7},{4,6},{5,1},{6,4},{7,3},{8,10},{9,13},{10,... | collective-permute-start | bytes 393224 | tf_op jit(solution)/shard_map/ppermute | solution.py:33
  50.1 0.2 collective-permute-done.12
  50.3 3.2 %collective-permute-done.15 = bf16[32,2048]{1,0:T(8,128)(2,1)S(1)} collective-permute-done((bf16[32,2048]{1,0:T(8,128)(2,1)S(1)}, bf16[32,2048]{1,0:T(8,128)(2,1)S(1)}, u32[]{:S(2)}, u32[]{:S(2)}) %collective-permute-start.15) | collective-permute-done | bytes 131104 | tf_op jit(solution)/shard_map/ppermute | solution.py:33
  53.6 0.9 %collective-permute-start.16 = (bf16[8,4096]{1,0:T(8,128)(2,1)S(1)}, bf16[8,4096]{1,0:T(8,128)(2,1)S(1)}, u32[]{:S(2)}, u32[]{:S(2)}) collective-permute-start(bf16[8,4096]{1,0:T(8,128)(2,1)S(1)} %get-tuple-element.101), channel_id=1, source_target_pairs={{0,16},{8,24},{16,0},{24,8},{1,17},{9,25},{17,1},{25,9},{2,18},{10... | collective-permute-start | bytes 196616 | tf_op jit(solution)/shard_map/ppermute | solution.py:33
  54.4 2.9 %collective-permute-start.18 = (bf16[8,4096]{1,0:T(8,128)(2,1)S(1)}, bf16[8,4096]{1,0:T(8,128)(2,1)S(1)}, u32[]{:S(2)}, u32[]{:S(2)}) collective-permute-start(bf16[8,4096]{1,0:T(8,128)(2,1)S(1)} %get-tuple-element.102), channel_id=1, source_target_pairs={{0,8},{8,16},{16,24},{24,0},{1,9},{9,17},{17,25},{25,1},{2,10},{10... | collective-permute-start | bytes 196616 | tf_op jit(solution)/shard_map/ppermute | solution.py:33
  57.4 0.9 %collective-permute-start.17 = (bf16[8,4096]{1,0:T(8,128)(2,1)S(1)}, bf16[8,4096]{1,0:T(8,128)(2,1)S(1)}, u32[]{:S(2)}, u32[]{:S(2)}) collective-permute-start(bf16[8,4096]{1,0:T(8,128)(2,1)S(1)} %get-tuple-element.103), channel_id=1, source_target_pairs={{0,24},{8,0},{16,8},{24,16},{1,25},{9,1},{17,9},{25,17},{2,26},{10... | collective-permute-start | bytes 196616 | tf_op jit(solution)/shard_map/ppermute | solution.py:33
  58.3 1.0 %collective-permute-done.16 = bf16[8,4096]{1,0:T(8,128)(2,1)S(1)} collective-permute-done((bf16[8,4096]{1,0:T(8,128)(2,1)S(1)}, bf16[8,4096]{1,0:T(8,128)(2,1)S(1)}, u32[]{:S(2)}, u32[]{:S(2)}) %collective-permute-start.16) | collective-permute-done | bytes 65568 | tf_op jit(solution)/shard_map/ppermute | solution.py:33
  59.2 1.5 %collective-permute-done.18 = bf16[8,4096]{1,0:T(8,128)(2,1)S(1)} collective-permute-done((bf16[8,4096]{1,0:T(8,128)(2,1)S(1)}, bf16[8,4096]{1,0:T(8,128)(2,1)S(1)}, u32[]{:S(2)}, u32[]{:S(2)}) %collective-permute-start.18) | collective-permute-done | bytes 65568 | tf_op jit(solution)/shard_map/ppermute | solution.py:33
  60.7 0.9 %collective-permute-done.17 = bf16[8,4096]{1,0:T(8,128)(2,1)S(1)} collective-permute-done((bf16[8,4096]{1,0:T(8,128)(2,1)S(1)}, bf16[8,4096]{1,0:T(8,128)(2,1)S(1)}, u32[]{:S(2)}, u32[]{:S(2)}) %collective-permute-start.17) | collective-permute-done | bytes 65568 | tf_op jit(solution)/shard_map/ppermute | solution.py:33
  61.6 0.7 %fusion.5 = f32[8,4096]{1,0:T(8,128)} fusion(f32[32,2048]{1,0:T(8,128)S(1)} %slice_add_fusion.3, f32[32,2048]{1,0:T(8,128)S(1)} %slice_add_fusion.2, bf16[8,4096]{1,0:T(8,128)(2,1)S(1)} %collective-permute-done.18, bf16[8,4096]{1,0:T(8,128)(2,1)S(1)} %collective-permute-done.17, bf16[8,4096]{1,0:T(8,128)(2,1)S(1)} %collective-permute-done.16), kind=kLoop, calls=%fused_computation.21 | loop fusion | flops 229376 | bytes 851968 | tf_op jit(solution)/shard_map/add | solution.py:293
  (14 shorter events, 0.3 us)
Async XLA Ops:
  1.0 9.6 %collective-permute-start.2 = (bf16[8,4224]{1,0:T(8,128)(2,1)S(1)}, bf16[8,4224]{1,0:T(8,128)(2,1)S(1)}, u32[]{:S(2)}, u32[]{:S(2)}) collective-permute-start(bf16[8,4224]{1,0:T(8,128)(2,1)S(1)} %get-tuple-element.72.refs_1_), channel_id=1, source_target_pairs={{0,8},{8,16},{16,24},{24,0},{1,9},{9,17},{17,25},{25,1},{2,10},{10... | collective-permute-start | bytes 202760 | tf_op jit(solution)/shard_map/ppermute | solution.py:33
  4.1 7.2 %collective-permute-start.1 = (bf16[8,4224]{1,0:T(8,128)(2,1)S(1)}, bf16[8,4224]{1,0:T(8,128)(2,1)S(1)}, u32[]{:S(2)}, u32[]{:S(2)}) collective-permute-start(bf16[8,4224]{1,0:T(8,128)(2,1)S(1)} %get-tuple-element.72.refs_1_), channel_id=1, source_target_pairs={{0,16},{8,24},{16,0},{24,8},{1,17},{9,25},{17,1},{25,9},{2,18},{10... | collective-permute-start | bytes 202760 | tf_op jit(solution)/shard_map/ppermute | solution.py:33
  6.7 4.8 %collective-permute-start = (bf16[8,4224]{1,0:T(8,128)(2,1)S(1)}, bf16[8,4224]{1,0:T(8,128)(2,1)S(1)}, u32[]{:S(2)}, u32[]{:S(2)}) collective-permute-start(bf16[8,4224]{1,0:T(8,128)(2,1)S(1)} %get-tuple-element.72.refs_1_), channel_id=1, source_target_pairs={{0,24},{8,0},{16,8},{24,16},{1,25},{9,1},{17,9},{25,17},{2,26},{10... | collective-permute-start | bytes 202760 | tf_op jit(solution)/shard_map/ppermute | solution.py:33
  11.5 6.5 %collective-permute-start.3 = (bf16[32,4224]{1,0:T(8,128)(2,1)S(1)}, bf16[32,4224]{1,0:T(8,128)(2,1)S(1)}, u32[]{:S(2)}, u32[]{:S(2)}) collective-permute-start(bf16[32,4224]{1,0:T(8,128)(2,1)S(1)} %constant_dynamic-update-slice_fusion.refs_2_), channel_id=1, source_target_pairs={{0,2},{1,5},{2,0},{3,7},{4,6},{5,1},{6,4},{7,3},{8,10},{9,13},{10,... | collective-permute-start | bytes 811016 | tf_op jit(solution)/shard_map/ppermute | solution.py:33
  18.0 6.1 %collective-permute-start.5 = (bf16[64,1792]{1,0:T(8,128)(2,1)S(1)}, bf16[64,1792]{1,0:T(8,128)(2,1)S(1)}, u32[]{:S(2)}, u32[]{:S(2)}) collective-permute-start(bf16[64,1792]{1,0:T(8,128)(2,1)S(1)} %pad_maximum_fusion.1.refs_1_.refs_0_), channel_id=1, source_target_pairs={{0,4},{1,3},{2,6},{3,1},{4,0},{5,7},{6,2},{7,5},{8,12},{9,11},{10,... | collective-permute-start | bytes 688136 | tf_op jit(solution)/shard_map/ppermute | solution.py:33
  19.8 7.7 %collective-permute-start.4 = (bf16[64,2432]{1,0:T(8,128)(2,1)S(1)}, bf16[64,2432]{1,0:T(8,128)(2,1)S(1)}, u32[]{:S(2)}, u32[]{:S(2)}) collective-permute-start(bf16[64,2432]{1,0:T(8,128)(2,1)S(1)} %fusion.1.refs_0_), channel_id=1, source_target_pairs={{0,4},{1,3},{2,6},{3,1},{4,0},{5,7},{6,2},{7,5},{8,12},{9,11},{10,... | collective-permute-start | bytes 933896 | tf_op jit(solution)/shard_map/ppermute | solution.py:33
  20.2 4.4 %collective-permute-start.6 = (bf16[64,1792]{1,0:T(8,128)(2,1)S(1)}, bf16[64,1792]{1,0:T(8,128)(2,1)S(1)}, u32[]{:S(2)}, u32[]{:S(2)}) collective-permute-start(bf16[64,1792]{1,0:T(8,128)(2,1)S(1)} %pad_maximum_fusion.1.refs_1_.refs_0_), channel_id=1, source_target_pairs={{0,1},{1,0},{2,3},{3,2},{4,5},{5,4},{6,7},{7,6},{8,9},{9,8},{10,11... | collective-permute-start | bytes 688136 | tf_op jit(solution)/shard_map/ppermute | solution.py:33
  24.1 1.5 %collective-permute-start.7 = (bf16[64,1792]{1,0:T(8,128)(2,1)S(1)}, bf16[64,1792]{1,0:T(8,128)(2,1)S(1)}, u32[]{:S(2)}, u32[]{:S(2)}) collective-permute-start(bf16[64,1792]{1,0:T(8,128)(2,1)S(1)} %collective-permute-done.5.refs_1_), channel_id=1, source_target_pairs={{0,1},{1,0},{2,3},{3,2},{4,5},{5,4},{6,7},{7,6},{8,9},{9,8},{10,11... | collective-permute-start | bytes 688136 | tf_op jit(solution)/shard_map/ppermute | solution.py:33
  24.1 5.0 %collective-permute-start.8 = (bf16[64,2432]{1,0:T(8,128)(2,1)S(1)}, bf16[64,2432]{1,0:T(8,128)(2,1)S(1)}, u32[]{:S(2)}, u32[]{:S(2)}) collective-permute-start(bf16[64,2432]{1,0:T(8,128)(2,1)S(1)} %fusion.1.refs_0_), channel_id=1, source_target_pairs={{0,1},{1,0},{2,3},{3,2},{4,5},{5,4},{6,7},{7,6},{8,9},{9,8},{10,11... | collective-permute-start | bytes 933896 | tf_op jit(solution)/shard_map/ppermute | solution.py:33
  27.5 1.6 %collective-permute-start.9 = (bf16[64,2432]{1,0:T(8,128)(2,1)S(1)}, bf16[64,2432]{1,0:T(8,128)(2,1)S(1)}, u32[]{:S(2)}, u32[]{:S(2)}) collective-permute-start(bf16[64,2432]{1,0:T(8,128)(2,1)S(1)} %collective-permute-done.4.refs_1_), channel_id=1, source_target_pairs={{0,1},{1,0},{2,3},{3,2},{4,5},{5,4},{6,7},{7,6},{8,9},{9,8},{10,11... | collective-permute-start | bytes 933896 | tf_op jit(solution)/shard_map/ppermute | solution.py:33
  36.1 2.4 %collective-permute-start.10 = (bf16[128,2048]{1,0:T(8,128)(2,1)S(1)}, bf16[128,2048]{1,0:T(8,128)(2,1)S(1)}, u32[]{:S(2)}, u32[]{:S(2)}) collective-permute-start(bf16[128,2048]{1,0:T(8,128)(2,1)S(1)} %get-tuple-element.97), channel_id=1, source_target_pairs={{0,1},{1,0},{2,3},{3,2},{4,5},{5,4},{6,7},{7,6},{8,9},{9,8},{10,11... | collective-permute-start | bytes 1572872 | tf_op jit(solution)/shard_map/ppermute | solution.py:33
  38.5 2.0 %collective-permute-start.13 = (bf16[128,2048]{1,0:T(8,128)(2,1)S(1)}, bf16[128,2048]{1,0:T(8,128)(2,1)S(1)}, u32[]{:S(2)}, u32[]{:S(2)}) collective-permute-start(bf16[128,2048]{1,0:T(8,128)(2,1)S(1)} %get-tuple-element.100), channel_id=1, source_target_pairs={{0,1},{1,0},{2,3},{3,2},{4,5},{5,4},{6,7},{7,6},{8,9},{9,8},{10,11... | collective-permute-start | bytes 1572872 | tf_op jit(solution)/shard_map/ppermute | solution.py:33
  38.7 6.4 %collective-permute-start.11 = (bf16[64,2048]{1,0:T(8,128)(2,1)S(1)}, bf16[64,2048]{1,0:T(8,128)(2,1)S(1)}, u32[]{:S(2)}, u32[]{:S(2)}) collective-permute-start(bf16[64,2048]{1,0:T(8,128)(2,1)S(1)} %slice.160), channel_id=1, source_target_pairs={{0,4},{1,3},{2,6},{3,1},{4,0},{5,7},{6,2},{7,5},{8,12},{9,11},{10,... | collective-permute-start | bytes 786440 | tf_op jit(solution)/shard_map/ppermute | solution.py:33
  40.6 7.7 %collective-permute-start.14 = (bf16[64,2048]{1,0:T(8,128)(2,1)S(1)}, bf16[64,2048]{1,0:T(8,128)(2,1)S(1)}, u32[]{:S(2)}, u32[]{:S(2)}) collective-permute-start(bf16[64,2048]{1,0:T(8,128)(2,1)S(1)} %slice.159), channel_id=1, source_target_pairs={{0,4},{1,3},{2,6},{3,1},{4,0},{5,7},{6,2},{7,5},{8,12},{9,11},{10,... | collective-permute-start | bytes 786440 | tf_op jit(solution)/shard_map/ppermute | solution.py:33
  45.3 5.0 %collective-permute-start.12 = (bf16[32,2048]{1,0:T(8,128)(2,1)S(1)}, bf16[32,2048]{1,0:T(8,128)(2,1)S(1)}, u32[]{:S(2)}, u32[]{:S(2)}) collective-permute-start(bf16[32,2048]{1,0:T(8,128)(2,1)S(1)} %slice.162), channel_id=1, source_target_pairs={{0,2},{1,5},{2,0},{3,7},{4,6},{5,1},{6,4},{7,3},{8,10},{9,13},{10,... | collective-permute-start | bytes 393224 | tf_op jit(solution)/shard_map/ppermute | solution.py:33
  48.5 5.0 %collective-permute-start.15 = (bf16[32,2048]{1,0:T(8,128)(2,1)S(1)}, bf16[32,2048]{1,0:T(8,128)(2,1)S(1)}, u32[]{:S(2)}, u32[]{:S(2)}) collective-permute-start(bf16[32,2048]{1,0:T(8,128)(2,1)S(1)} %slice.161), channel_id=1, source_target_pairs={{0,2},{1,5},{2,0},{3,7},{4,6},{5,1},{6,4},{7,3},{8,10},{9,13},{10,... | collective-permute-start | bytes 393224 | tf_op jit(solution)/shard_map/ppermute | solution.py:33
  53.6 5.6 %collective-permute-start.16 = (bf16[8,4096]{1,0:T(8,128)(2,1)S(1)}, bf16[8,4096]{1,0:T(8,128)(2,1)S(1)}, u32[]{:S(2)}, u32[]{:S(2)}) collective-permute-start(bf16[8,4096]{1,0:T(8,128)(2,1)S(1)} %get-tuple-element.101), channel_id=1, source_target_pairs={{0,16},{8,24},{16,0},{24,8},{1,17},{9,25},{17,1},{25,9},{2,18},{10... | collective-permute-start | bytes 196616 | tf_op jit(solution)/shard_map/ppermute | solution.py:33
  54.4 6.2 %collective-permute-start.18 = (bf16[8,4096]{1,0:T(8,128)(2,1)S(1)}, bf16[8,4096]{1,0:T(8,128)(2,1)S(1)}, u32[]{:S(2)}, u32[]{:S(2)}) collective-permute-start(bf16[8,4096]{1,0:T(8,128)(2,1)S(1)} %get-tuple-element.102), channel_id=1, source_target_pairs={{0,8},{8,16},{16,24},{24,0},{1,9},{9,17},{17,25},{25,1},{2,10},{10... | collective-permute-start | bytes 196616 | tf_op jit(solution)/shard_map/ppermute | solution.py:33
  57.4 4.3 %collective-permute-start.17 = (bf16[8,4096]{1,0:T(8,128)(2,1)S(1)}, bf16[8,4096]{1,0:T(8,128)(2,1)S(1)}, u32[]{:S(2)}, u32[]{:S(2)}) collective-permute-start(bf16[8,4096]{1,0:T(8,128)(2,1)S(1)} %get-tuple-element.103), channel_id=1, source_target_pairs={{0,24},{8,0},{16,8},{24,16},{1,25},{9,1},{17,9},{25,17},{2,26},{10... | collective-permute-start | bytes 196616 | tf_op jit(solution)/shard_map/ppermute | solution.py:33

commit v5 on v4

--- a/solution.py
+++ b/solution.py
@@ -11,11 +11,10 @@
 MIB = 1 << 20
 AG_CUT = 1792
 RS_CUTS = (2048, 2048)
+EARLY = 256
 ROWS_FIRST = 768
-P1_SPLIT = False
-AG_ORDER = (3, 2, 1)
-RS_ORDER = (2, 1, 3)
-XOR = False
+AG_ORDER = (1, 2, 3)
+RS_ORDER = (2, 3, 1)
 IN_VMEM = pl.BlockSpec(memory_space=pltpu.VMEM)
 IN_HBM = pl.BlockSpec(memory_space=pltpu.HBM)
 ANYWHERE = pl.BlockSpec(memory_space=pl.ANY)
@@ -34,8 +33,6 @@
 
 
 def hop(distance, size):
-    if XOR:
-        return lambda i: i ^ abs(distance)
     return lambda i: (i + distance) % size
 
 
@@ -53,13 +50,20 @@
     return total[:count] + back.astype(F32)
 
 
-def pack_kernel(stream_ref, gain_ref, ids_ref, weights_ref, own_ref, *half_refs, experts):
+def pack_kernel(stream_ref, gain_ref, ids_ref, weights_ref, own_ref, column_ref, *, experts):
     stream = stream_ref[...].astype(F32)
     inverse = lax.rsqrt(jnp.mean(stream * stream, axis=-1, keepdims=True) + 1e-06)
     rows, features = stream.shape
+    blank = column_ref.shape[0] - rows
+
+    def put(value, here):
+        own_ref[:, here] = value.astype(BF16)
+        empty = jnp.zeros((blank, value.shape[1]), F32)
+        column_ref[:, here] = jnp.concatenate([value, empty], axis=0).astype(BF16)
+
     for i in range(features // LANES):
         here = slice(i * LANES, (i + 1) * LANES)
-        own_ref[:, here] = (stream[:, here] * inverse * gain_ref[i : i + 1, :].astype(F32)).astype(BF16)
+        put(stream[:, here] * inverse * gain_ref[i : i + 1, :].astype(F32), here)
     width = own_ref.shape[1] - features
     column = lax.broadcasted_iota(jnp.int32, (rows, width), 1)
     dense = jnp.zeros((rows, width), F32)
@@ -72,12 +76,7 @@
         dense = dense + jnp.where(column == expert, high, 0.0)
         dense = dense + jnp.where(column == expert + experts, middle, 0.0)
         dense = dense + jnp.where(column == expert + 2 * experts, low, 0.0)
-    own_ref[:, features:] = dense.astype(BF16)
-    at = 0
-    for ref in half_refs:
-        ref[...] = jnp.zeros_like(ref)
-        ref[:rows, :] = own_ref[:, at : at + ref.shape[1]]
-        at += ref.shape[1]
+    put(dense, slice(features, features + width))
 
 
 def fetches(cuts, source_refs, out_refs, sems):
@@ -172,11 +171,17 @@
         copy.wait()
 
 
-def down_kernel(act_ref, down_ref, keep_ref, send_ref, *, chunk):
+def down_kernel(act_ref, *refs, chunk, start):
+    *down_refs, keep_ref, send_ref = refs
     half = keep_ref.shape[0]
-    for j in range(keep_ref.shape[1] // chunk):
-        here = slice(j * chunk, (j + 1) * chunk)
-        out = jnp.dot(act_ref[...], down_ref[:, here], preferred_element_type=F32)
+    depths = [ref.shape[0] for ref in down_refs]
+    starts = [sum(depths[:i]) for i in range(len(depths))]
+    for j in range(0, keep_ref.shape[1], chunk):
+        here, there = slice(j, j + chunk), slice(start + j, start + j + chunk)
+        out = sum(
+            jnp.dot(act_ref[:, at : at + depth], ref[:, there], preferred_element_type=F32)
+            for at, depth, ref in zip(starts, depths, down_refs)
+        )
         keep_ref[:, here] = out[:half]
         send_ref[:, here] = out[half:].astype(BF16)
 
@@ -217,20 +222,21 @@
     )(stream_in, norm_gain.reshape(features // LANES, LANES), expert_ids, route_weights)
 
     received = {d: swap(own, "attn", hop(d, attn_size)) for d in order_of(AG_ORDER, attn_size)}
-    (gate_1,) = load([w_gate], [(0, every, (0, AG_CUT))], own)
+    early = EARLY * hidden // 1536
+    cuts = [(0, every, (0, AG_CUT)), (1, (0, early), (0, features))]
+    gate_1, *downs_1 = load([w_gate, w_down], cuts, own)
     *values, gate_1 = lax.optimization_barrier((*received.values(), gate_1))
     for d, value in zip(received, values):
         column = column.at[d * row_count : (d + 1) * row_count].set(value)
 
     gate_2, up_1 = load([w_gate, w_up], [(0, every, (AG_CUT, rest)), (1, every, (0, AG_CUT))], column)
-    columns = [column[:, :AG_CUT], column[:, AG_CUT:]] if P1_SPLIT else [column]
+    columns = [column]
     for step in range(steps - 1):
         others = [swap(value, "expert", partner(step, steps)) for value in columns]
         if step == 0:
             others[0], gate_2, up_1 = lax.optimization_barrier((others[0], gate_2, up_1))
         columns = [jnp.concatenate(pair, axis=0) for pair in zip(columns, others)]
-    if not P1_SPLIT:
-        columns = [columns[0][:, :AG_CUT], columns[0][:, AG_CUT:]]
+    columns = [columns[0][:, :AG_CUT], columns[0][:, AG_CUT:]]
     up_2, spread = load([w_up], [(0, every, (AG_CUT, rest))], columns[0], experts, width)
     others = [swap(value, "expert", partner(steps - 1, steps)) for value in columns]
     others[0], up_2, spread = lax.optimization_barrier((others[0], up_2, spread))
@@ -259,8 +265,8 @@
     )(near(rows), near(gate_1), near(up_1))
     pieces = both_of_pair([columns[1], others[1]])
     starts = [sum(RS_CUTS[:i]) for i in range(len(RS_CUTS))]
-    cuts = [(0, every, (at, size)) for at, size in zip(starts, RS_CUTS)]
-    act, *downs = pl.pallas_call(
+    cuts = [(0, (early, hidden - early), (0, features))]
+    act, *downs_3 = pl.pallas_call(
         lambda *refs: second_kernel(*refs, pieces=count, block=LANES, part=rest, cuts=cuts),
         out_shape=[pltpu.VMEM((tokens, hidden), BF16)] + loaded(cuts),
         in_specs=[IN_VMEM] * (count + 7) + [IN_HBM],
@@ -274,16 +280,17 @@
         far(w_down),
     )
 
+    downs = [*downs_1, *downs_3]
     outs = []
-    for size, down in zip(RS_CUTS, downs):
+    for start, size in zip(starts, RS_CUTS):
         keep, send = pl.pallas_call(
-            lambda *refs: down_kernel(*refs, chunk=512),
+            lambda *refs, start=start: down_kernel(*refs, chunk=512, start=start),
             out_shape=[pltpu.VMEM((half, size), F32), pltpu.VMEM((half, size), BF16)],
-            in_specs=[IN_VMEM] * 2,
+            in_specs=[IN_VMEM] * (1 + len(downs)),
             out_specs=[IN_VMEM] * 2,
             compiler_params=params(12),
             cost_estimate=NO_COST,
-        )(near(act), near(down))
+        )(near(act), *[near(down) for down in downs])
         total = keep + swap(send, "expert", beside).astype(F32)
         for step in reversed(range(steps)):
             total = fold(total, step, steps)

time: 62.5 us -> 61.9 us (level)
  waiting for transfers between devices: 14.3 us -> 13.5 us
    ppermute x19, waiting for transfers between devices: 14.3 us -> 13.5 us  [swap(): lax.ppermute(value, axis, [(i, to(i)) for i in range(lax.axis_size(axis))])]
    pallas_call x3, Pallas kernels: 10.2 us -> 10.9 us  [load(): pl.pallas_call(lambda *refs: load_kernel(*refs, sources=len(arrays), cuts...]
    pallas_call x1, Pallas kernels: 5.23 us -> 4.61 us  [local(): pl.pallas_call(lambda *refs: second_kernel(*refs, pieces=count, block=LAN...]
  transfers between devices with their start and end apart: 19 -> 19, of which waited for: 14 -> 13; matrix products, arithmetic and copies ran while one was open for 1% -> 1% of each run, Pallas kernels for 24% -> 26%
where the time goes in v5:
time: 61.9 us; the launch traced here: 61.7 us
  starting transfers between devices  23.4 us (38%)
  Pallas kernels  23.3 us (38%)
  waiting for transfers between devices  13.5 us (22%)
  other arithmetic  1.13 us (2%)
    ppermute x19, starting transfers between devices, swap(): lax.ppermute(value, axis, [(i, to(i)) for i in range(lax.axis_size(axis))])  23.4 us
    ppermute x19, waiting for transfers between devices, swap(): lax.ppermute(value, axis, [(i, to(i)) for i in range(lax.axis_size(axis))])  13.5 us
    pallas_call x3, Pallas kernels, load(): pl.pallas_call(lambda *refs: load_kernel(*refs, sources=len(arrays), cuts...  10.9 us
    pallas_call x1, Pallas kernels, local(): pl.pallas_call(lambda *refs: second_kernel(*refs, pieces=count, block=LAN...  4.61 us
    pallas_call x2, Pallas kernels, local(): pl.pallas_call(lambda *refs, start=start: down_kernel(*refs, chunk=512, s...  3.57 us
    pallas_call x1, Pallas kernels, local(): pl.pallas_call(lambda *refs: first_kernel(*refs, pieces=count, block=LANE...  1.61 us
    pallas_call x1, Pallas kernels, local(): pl.pallas_call(lambda *refs: middle_kernel(*refs, block=LANES, start=cut)...  1.61 us
  transfers between devices with their start and end apart: 19, of which 13 were waited for; matrix products, arithmetic and copies ran while one was open for 1% of the time, Pallas kernels for 26%

profile of v5, /device:TPU:0, one launch (start us, length us, event | category | flops | bytes accessed | tf_op | source)
XLA Modules:
  0.0 61.7 jit_solution(2370194281575801433)
XLA Ops:
  0.0 1.0 %shard_map.73 = (bf16[8,4224]{1,0:T(8,128)(2,1)S(1)}, bf16[32,4224]{1,0:T(8,128)(2,1)S(1)}) custom-call(bf16[8,4096]{1,0:T(8,128)(2,1)} %refs_0_.1, bf16[32,128]{1,0:T(8,128)(2,1)} %bitcast.10, s32[8,8]{1,0:T(8,128)} %refs_2_.1, f32[8,8]{1,0:T(8,128)} %refs_3_.1), custom_call_target="tpu_custom_call" | custom-call | tf_op jit(solution)/shard_map/pallas_call | solution.py:216
  1.0 3.1 %collective-permute-start = (bf16[8,4224]{1,0:T(8,128)(2,1)S(1)}, bf16[8,4224]{1,0:T(8,128)(2,1)S(1)}, u32[]{:S(2)}, u32[]{:S(2)}) collective-permute-start(bf16[8,4224]{1,0:T(8,128)(2,1)S(1)} %get-tuple-element.73.refs_2_), channel_id=1, source_target_pairs={{0,8},{8,16},{16,24},{24,0},{1,9},{9,17},{17,25},{25,1},{2,10},{10... | collective-permute-start | bytes 202760 | tf_op jit(solution)/shard_map/ppermute | solution.py:32
  4.1 2.6 %collective-permute-start.1 = (bf16[8,4224]{1,0:T(8,128)(2,1)S(1)}, bf16[8,4224]{1,0:T(8,128)(2,1)S(1)}, u32[]{:S(2)}, u32[]{:S(2)}) collective-permute-start(bf16[8,4224]{1,0:T(8,128)(2,1)S(1)} %get-tuple-element.73.refs_2_), channel_id=1, source_target_pairs={{0,16},{8,24},{16,0},{24,8},{1,17},{9,25},{17,1},{25,9},{2,18},{10... | collective-permute-start | bytes 202760 | tf_op jit(solution)/shard_map/ppermute | solution.py:32
  6.7 1.3 %collective-permute-start.2 = (bf16[8,4224]{1,0:T(8,128)(2,1)S(1)}, bf16[8,4224]{1,0:T(8,128)(2,1)S(1)}, u32[]{:S(2)}, u32[]{:S(2)}) collective-permute-start(bf16[8,4224]{1,0:T(8,128)(2,1)S(1)} %get-tuple-element.73.refs_2_), channel_id=1, source_target_pairs={{0,24},{8,0},{16,8},{24,16},{1,25},{9,1},{17,9},{25,17},{2,26},{10... | collective-permute-start | bytes 202760 | tf_op jit(solution)/shard_map/ppermute | solution.py:32
  8.0 3.3 %shard_map.74 = (bf16[1536,1792]{1,0:T(8,128)(2,1)S(1)}, bf16[256,4096]{1,0:T(8,128)(2,1)S(1)}) custom-call(bf16[1536,4096]{1,0:T(8,128)(2,1)} %bitcast.4, bf16[1536,4096]{1,0:T(8,128)(2,1)} %bitcast.8, bf16[8,4224]{1,0:T(8,128)(2,1)S(1)} %get-tuple-element.73.refs_2_), custom_call_target="tpu_custom_call" | custom-call | tf_op jit(solution)/shard_map/pallas_call | solution.py:113
  11.3 0.0 collective-permute-done
  11.3 0.0 collective-permute-done.1
  11.3 0.1 collective-permute-done.2
  11.5 1.7 %collective-permute-start.3 = (bf16[32,4224]{1,0:T(8,128)(2,1)S(1)}, bf16[32,4224]{1,0:T(8,128)(2,1)S(1)}, u32[]{:S(2)}, u32[]{:S(2)}) collective-permute-start(bf16[32,4224]{1,0:T(8,128)(2,1)S(1)} %constant_dynamic-update-slice_fusion.refs_2_), channel_id=1, source_target_pairs={{0,2},{1,5},{2,0},{3,7},{4,6},{5,1},{6,4},{7,3},{8,10},{9,13},{10,... | collective-permute-start | bytes 811016 | tf_op jit(solution)/shard_map/ppermute | solution.py:32
  13.2 4.6 %shard_map.75 = (bf16[1536,2304]{1,0:T(8,128)(2,1)S(1)}, bf16[1536,1792]{1,0:T(8,128)(2,1)S(1)}) custom-call(bf16[1536,4096]{1,0:T(8,128)(2,1)} %bitcast.5, bf16[1536,4096]{1,0:T(8,128)(2,1)} %bitcast.6, bf16[32,4224]{1,0:T(8,128)(2,1)S(1)} %constant_dynamic-update-slice_fusion.refs_2_), custom_call_target="tpu_custom_call" | custom-call | tf_op jit(solution)/shard_map/pallas_call | solution.py:113
  17.8 0.3 collective-permute-done.3
  18.0 1.7 %collective-permute-start.5 = (bf16[64,1792]{1,0:T(8,128)(2,1)S(1)}, bf16[64,1792]{1,0:T(8,128)(2,1)S(1)}, u32[]{:S(2)}, u32[]{:S(2)}) collective-permute-start(bf16[64,1792]{1,0:T(8,128)(2,1)S(1)} %pad_maximum_fusion.1.refs_1_.refs_0_), channel_id=1, source_target_pairs={{0,4},{1,3},{2,6},{3,1},{4,0},{5,7},{6,2},{7,5},{8,12},{9,11},{10,... | collective-permute-start | bytes 688136 | tf_op jit(solution)/shard_map/ppermute | solution.py:32
  19.8 0.5 collective-permute-start.4
  20.2 3.0 %shard_map.76 = (bf16[1536,2304]{1,0:T(8,128)(2,1)S(1)}, bf16[128,1536]{1,0:T(8,128)(2,1)S(1)}) custom-call(bf16[1536,4096]{1,0:T(8,128)(2,1)} %bitcast.7, bf16[64,1792]{1,0:T(8,128)(2,1)S(1)} %pad_maximum_fusion.1.refs_1_.refs_0_), custom_call_target="tpu_custom_call" | custom-call | tf_op jit(solution)/shard_map/pallas_call | solution.py:113
  23.3 0.1 collective-permute-start.6
  23.3 0.8 %collective-permute-done.5.refs_1_ = bf16[64,1792]{1,0:T(8,128)(2,1)S(1)} collective-permute-done((bf16[64,1792]{1,0:T(8,128)(2,1)S(1)}, bf16[64,1792]{1,0:T(8,128)(2,1)S(1)}, u32[]{:S(2)}, u32[]{:S(2)}) %collective-permute-start.5) | collective-permute-done | bytes 229408 | tf_op jit(solution)/shard_map/ppermute | solution.py:32
  24.1 0.0 collective-permute-start.7
  24.1 0.5 collective-permute-start.8
  24.6 0.2 collective-permute-done.6.refs_2_
  24.8 0.8 %collective-permute-done.7.refs_3_ = bf16[64,1792]{1,0:T(8,128)(2,1)S(1)} collective-permute-done((bf16[64,1792]{1,0:T(8,128)(2,1)S(1)}, bf16[64,1792]{1,0:T(8,128)(2,1)S(1)}, u32[]{:S(2)}, u32[]{:S(2)}) %collective-permute-start.7) | collective-permute-done | bytes 229408 | tf_op jit(solution)/shard_map/ppermute | solution.py:32
  25.6 1.6 %shard_map.77 = (bf16[256,1792]{1,0:T(8,128)(2,1)S(1)}, f32[256,768]{1,0:T(8,128)S(1)}, f32[256,768]{1,0:T(8,128)S(1)}) custom-call(bf16[64,1792]{1,0:T(8,128)(2,1)S(1)} %pad_maximum_fusion.1.refs_1_.refs_0_, bf16[64,1792]{1,0:T(8,128)(2,1)S(1)} %collective-permute-done.5.refs_1_, bf16[64,1792]{1,0:T(8,128)(2,1)S(1)} %collective-permute-done.6.refs_2_, ...), custom_call_target="tpu_custom_call" | custom-call | tf_op jit(solution)/shard_map/pallas_call | solution.py:249
  27.2 0.2 collective-permute-done.4.refs_1_
  27.5 0.0 collective-permute-start.9
  27.5 1.6 %shard_map.78 = (f32[256,768]{1,0:T(8,128)S(1)}, f32[256,768]{1,0:T(8,128)S(1)}) custom-call(bf16[256,1792]{1,0:T(8,128)(2,1)S(1)} %get-tuple-element.92.refs_0_, bf16[1536,1792]{1,0:T(8,128)(2,1)S(1)} %get-tuple-element.84.refs_4_.refs_1_, bf16[1536,1792]{1,0:T(8,128)(2,1)S(1)} %get-tuple-element.85.refs_5_.refs_2_), custom_call_target="tpu_custom_call" | custom-call | tf_op jit(solution)/shard_map/pallas_call | solution.py:258
  29.1 0.0 collective-permute-done.8.refs_2_
  29.1 0.0 collective-permute-done.9.refs_3_
  29.1 4.6 %shard_map.79 = (bf16[256,1536]{1,0:T(8,128)(2,1)S(1)}, bf16[1280,4096]{1,0:T(8,128)(2,1)S(1)}) custom-call(bf16[64,2432]{1,0:T(8,128)(2,1)S(1)} %fusion.1.refs_0_, bf16[64,2432]{1,0:T(8,128)(2,1)S(1)} %collective-permute-done.4.refs_1_, bf16[64,2432]{1,0:T(8,128)(2,1)S(1)} %collective-permute-done.8.refs_2_, ...), custom_call_target="tpu_custom_call" | custom-call | tf_op jit(solution)/shard_map/pallas_call | solution.py:269
  33.7 1.8 %shard_map.81 = (f32[128,2048]{1,0:T(8,128)S(1)}, bf16[128,2048]{1,0:T(8,128)(2,1)S(1)}) custom-call(bf16[256,1536]{1,0:T(8,128)(2,1)S(1)} %get-tuple-element.96.refs_0_, bf16[256,4096]{1,0:T(8,128)(2,1)S(1)} %get-tuple-element.97.refs_1_, bf16[1280,4096]{1,0:T(8,128)(2,1)S(1)} %get-tuple-element.98.refs_2_), custom_call_target="tpu_custom_call" | custom-call | tf_op jit(solution)/shard_map/pallas_call | solution.py:286
  35.5 0.6 collective-permute-start.13
  36.1 1.8 %shard_map.80 = (f32[128,2048]{1,0:T(8,128)S(1)}, bf16[128,2048]{1,0:T(8,128)(2,1)S(1)}) custom-call(bf16[256,1536]{1,0:T(8,128)(2,1)S(1)} %get-tuple-element.96.refs_0_, bf16[256,4096]{1,0:T(8,128)(2,1)S(1)} %get-tuple-element.97.refs_1_, bf16[1280,4096]{1,0:T(8,128)(2,1)S(1)} %get-tuple-element.98.refs_2_), custom_call_target="tpu_custom_call" | custom-call | tf_op jit(solution)/shard_map/pallas_call | solution.py:286
  37.9 0.1 collective-permute-start.10
  38.0 0.0 collective-permute-done.13
  38.0 0.1 convert_add_fusion
  38.1 1.7 %collective-permute-start.14 = (bf16[64,2048]{1,0:T(8,128)(2,1)S(1)}, bf16[64,2048]{1,0:T(8,128)(2,1)S(1)}, u32[]{:S(2)}, u32[]{:S(2)}) collective-permute-start(bf16[64,2048]{1,0:T(8,128)(2,1)S(1)} %slice.159), channel_id=1, source_target_pairs={{0,4},{1,3},{2,6},{3,1},{4,0},{5,7},{6,2},{7,5},{8,12},{9,11},{10,... | collective-permute-start | bytes 786440 | tf_op jit(solution)/shard_map/ppermute | solution.py:32
  39.8 0.0 collective-permute-done.10
  39.9 0.1 convert_add_fusion.1
  40.0 1.7 %collective-permute-start.11 = (bf16[64,2048]{1,0:T(8,128)(2,1)S(1)}, bf16[64,2048]{1,0:T(8,128)(2,1)S(1)}, u32[]{:S(2)}, u32[]{:S(2)}) collective-permute-start(bf16[64,2048]{1,0:T(8,128)(2,1)S(1)} %slice.160), channel_id=1, source_target_pairs={{0,4},{1,3},{2,6},{3,1},{4,0},{5,7},{6,2},{7,5},{8,12},{9,11},{10,... | collective-permute-start | bytes 786440 | tf_op jit(solution)/shard_map/ppermute | solution.py:32
  41.7 2.9 %collective-permute-done.14 = bf16[64,2048]{1,0:T(8,128)(2,1)S(1)} collective-permute-done((bf16[64,2048]{1,0:T(8,128)(2,1)S(1)}, bf16[64,2048]{1,0:T(8,128)(2,1)S(1)}, u32[]{:S(2)}, u32[]{:S(2)}) %collective-permute-start.14) | collective-permute-done | bytes 262176 | tf_op jit(solution)/shard_map/ppermute | solution.py:32
  44.6 1.7 %collective-permute-start.15 = (bf16[32,2048]{1,0:T(8,128)(2,1)S(1)}, bf16[32,2048]{1,0:T(8,128)(2,1)S(1)}, u32[]{:S(2)}, u32[]{:S(2)}) collective-permute-start(bf16[32,2048]{1,0:T(8,128)(2,1)S(1)} %slice.161), channel_id=1, source_target_pairs={{0,2},{1,5},{2,0},{3,7},{4,6},{5,1},{6,4},{7,3},{8,10},{9,13},{10,... | collective-permute-start | bytes 393224 | tf_op jit(solution)/shard_map/ppermute | solution.py:32
  46.3 1.4 %collective-permute-done.11 = bf16[64,2048]{1,0:T(8,128)(2,1)S(1)} collective-permute-done((bf16[64,2048]{1,0:T(8,128)(2,1)S(1)}, bf16[64,2048]{1,0:T(8,128)(2,1)S(1)}, u32[]{:S(2)}, u32[]{:S(2)}) %collective-permute-start.11) | collective-permute-done | bytes 262176 | tf_op jit(solution)/shard_map/ppermute | solution.py:32
  47.8 0.1 slice_add_fusion.1
  47.8 1.7 %collective-permute-start.12 = (bf16[32,2048]{1,0:T(8,128)(2,1)S(1)}, bf16[32,2048]{1,0:T(8,128)(2,1)S(1)}, u32[]{:S(2)}, u32[]{:S(2)}) collective-permute-start(bf16[32,2048]{1,0:T(8,128)(2,1)S(1)} %slice.162), channel_id=1, source_target_pairs={{0,2},{1,5},{2,0},{3,7},{4,6},{5,1},{6,4},{7,3},{8,10},{9,13},{10,... | collective-permute-start | bytes 393224 | tf_op jit(solution)/shard_map/ppermute | solution.py:32
  49.5 0.2 collective-permute-done.15
  49.7 3.2 %collective-permute-done.12 = bf16[32,2048]{1,0:T(8,128)(2,1)S(1)} collective-permute-done((bf16[32,2048]{1,0:T(8,128)(2,1)S(1)}, bf16[32,2048]{1,0:T(8,128)(2,1)S(1)}, u32[]{:S(2)}, u32[]{:S(2)}) %collective-permute-start.12) | collective-permute-done | bytes 131104 | tf_op jit(solution)/shard_map/ppermute | solution.py:32
  53.0 0.9 %collective-permute-start.16 = (bf16[8,4096]{1,0:T(8,128)(2,1)S(1)}, bf16[8,4096]{1,0:T(8,128)(2,1)S(1)}, u32[]{:S(2)}, u32[]{:S(2)}) collective-permute-start(bf16[8,4096]{1,0:T(8,128)(2,1)S(1)} %get-tuple-element.103), channel_id=1, source_target_pairs={{0,16},{8,24},{16,0},{24,8},{1,17},{9,25},{17,1},{25,9},{2,18},{10... | collective-permute-start | bytes 196616 | tf_op jit(solution)/shard_map/ppermute | solution.py:32
  53.8 2.9 %collective-permute-start.17 = (bf16[8,4096]{1,0:T(8,128)(2,1)S(1)}, bf16[8,4096]{1,0:T(8,128)(2,1)S(1)}, u32[]{:S(2)}, u32[]{:S(2)}) collective-permute-start(bf16[8,4096]{1,0:T(8,128)(2,1)S(1)} %get-tuple-element.105), channel_id=1, source_target_pairs={{0,8},{8,16},{16,24},{24,0},{1,9},{9,17},{17,25},{25,1},{2,10},{10... | collective-permute-start | bytes 196616 | tf_op jit(solution)/shard_map/ppermute | solution.py:32
  56.7 0.9 %collective-permute-start.18 = (bf16[8,4096]{1,0:T(8,128)(2,1)S(1)}, bf16[8,4096]{1,0:T(8,128)(2,1)S(1)}, u32[]{:S(2)}, u32[]{:S(2)}) collective-permute-start(bf16[8,4096]{1,0:T(8,128)(2,1)S(1)} %get-tuple-element.104), channel_id=1, source_target_pairs={{0,24},{8,0},{16,8},{24,16},{1,25},{9,1},{17,9},{25,17},{2,26},{10... | collective-permute-start | bytes 196616 | tf_op jit(solution)/shard_map/ppermute | solution.py:32
  57.7 0.9 %collective-permute-done.16 = bf16[8,4096]{1,0:T(8,128)(2,1)S(1)} collective-permute-done((bf16[8,4096]{1,0:T(8,128)(2,1)S(1)}, bf16[8,4096]{1,0:T(8,128)(2,1)S(1)}, u32[]{:S(2)}, u32[]{:S(2)}) %collective-permute-start.16) | collective-permute-done | bytes 65568 | tf_op jit(solution)/shard_map/ppermute | solution.py:32
  58.6 1.5 %collective-permute-done.17 = bf16[8,4096]{1,0:T(8,128)(2,1)S(1)} collective-permute-done((bf16[8,4096]{1,0:T(8,128)(2,1)S(1)}, bf16[8,4096]{1,0:T(8,128)(2,1)S(1)}, u32[]{:S(2)}, u32[]{:S(2)}) %collective-permute-start.17) | collective-permute-done | bytes 65568 | tf_op jit(solution)/shard_map/ppermute | solution.py:32
  60.1 0.9 %collective-permute-done.18 = bf16[8,4096]{1,0:T(8,128)(2,1)S(1)} collective-permute-done((bf16[8,4096]{1,0:T(8,128)(2,1)S(1)}, bf16[8,4096]{1,0:T(8,128)(2,1)S(1)}, u32[]{:S(2)}, u32[]{:S(2)}) %collective-permute-start.18) | collective-permute-done | bytes 65568 | tf_op jit(solution)/shard_map/ppermute | solution.py:32
  61.0 0.7 %fusion.5 = f32[8,4096]{1,0:T(8,128)} fusion(f32[32,2048]{1,0:T(8,128)S(1)} %slice_add_fusion.3, f32[32,2048]{1,0:T(8,128)S(1)} %slice_add_fusion.2, bf16[8,4096]{1,0:T(8,128)(2,1)S(1)} %collective-permute-done.18, bf16[8,4096]{1,0:T(8,128)(2,1)S(1)} %collective-permute-done.17, bf16[8,4096]{1,0:T(8,128)(2,1)S(1)} %collective-permute-done.16), kind=kLoop, calls=%fused_computation.21 | loop fusion | flops 229376 | bytes 851968 | tf_op jit(solution)/shard_map/add | solution.py:300
  (14 shorter events, 0.3 us)
Async XLA Ops:
  1.0 10.3 %collective-permute-start = (bf16[8,4224]{1,0:T(8,128)(2,1)S(1)}, bf16[8,4224]{1,0:T(8,128)(2,1)S(1)}, u32[]{:S(2)}, u32[]{:S(2)}) collective-permute-start(bf16[8,4224]{1,0:T(8,128)(2,1)S(1)} %get-tuple-element.73.refs_2_), channel_id=1, source_target_pairs={{0,8},{8,16},{16,24},{24,0},{1,9},{9,17},{17,25},{25,1},{2,10},{10... | collective-permute-start | bytes 202760 | tf_op jit(solution)/shard_map/ppermute | solution.py:32
  4.1 7.2 %collective-permute-start.1 = (bf16[8,4224]{1,0:T(8,128)(2,1)S(1)}, bf16[8,4224]{1,0:T(8,128)(2,1)S(1)}, u32[]{:S(2)}, u32[]{:S(2)}) collective-permute-start(bf16[8,4224]{1,0:T(8,128)(2,1)S(1)} %get-tuple-element.73.refs_2_), channel_id=1, source_target_pairs={{0,16},{8,24},{16,0},{24,8},{1,17},{9,25},{17,1},{25,9},{2,18},{10... | collective-permute-start | bytes 202760 | tf_op jit(solution)/shard_map/ppermute | solution.py:32
  6.7 4.8 %collective-permute-start.2 = (bf16[8,4224]{1,0:T(8,128)(2,1)S(1)}, bf16[8,4224]{1,0:T(8,128)(2,1)S(1)}, u32[]{:S(2)}, u32[]{:S(2)}) collective-permute-start(bf16[8,4224]{1,0:T(8,128)(2,1)S(1)} %get-tuple-element.73.refs_2_), channel_id=1, source_target_pairs={{0,24},{8,0},{16,8},{24,16},{1,25},{9,1},{17,9},{25,17},{2,26},{10... | collective-permute-start | bytes 202760 | tf_op jit(solution)/shard_map/ppermute | solution.py:32
  11.5 6.5 %collective-permute-start.3 = (bf16[32,4224]{1,0:T(8,128)(2,1)S(1)}, bf16[32,4224]{1,0:T(8,128)(2,1)S(1)}, u32[]{:S(2)}, u32[]{:S(2)}) collective-permute-start(bf16[32,4224]{1,0:T(8,128)(2,1)S(1)} %constant_dynamic-update-slice_fusion.refs_2_), channel_id=1, source_target_pairs={{0,2},{1,5},{2,0},{3,7},{4,6},{5,1},{6,4},{7,3},{8,10},{9,13},{10,... | collective-permute-start | bytes 811016 | tf_op jit(solution)/shard_map/ppermute | solution.py:32
  18.0 6.1 %collective-permute-start.5 = (bf16[64,1792]{1,0:T(8,128)(2,1)S(1)}, bf16[64,1792]{1,0:T(8,128)(2,1)S(1)}, u32[]{:S(2)}, u32[]{:S(2)}) collective-permute-start(bf16[64,1792]{1,0:T(8,128)(2,1)S(1)} %pad_maximum_fusion.1.refs_1_.refs_0_), channel_id=1, source_target_pairs={{0,4},{1,3},{2,6},{3,1},{4,0},{5,7},{6,2},{7,5},{8,12},{9,11},{10,... | collective-permute-start | bytes 688136 | tf_op jit(solution)/shard_map/ppermute | solution.py:32
  19.8 7.7 %collective-permute-start.4 = (bf16[64,2432]{1,0:T(8,128)(2,1)S(1)}, bf16[64,2432]{1,0:T(8,128)(2,1)S(1)}, u32[]{:S(2)}, u32[]{:S(2)}) collective-permute-start(bf16[64,2432]{1,0:T(8,128)(2,1)S(1)} %fusion.1.refs_0_), channel_id=1, source_target_pairs={{0,4},{1,3},{2,6},{3,1},{4,0},{5,7},{6,2},{7,5},{8,12},{9,11},{10,... | collective-permute-start | bytes 933896 | tf_op jit(solution)/shard_map/ppermute | solution.py:32
  23.3 1.6 %collective-permute-start.6 = (bf16[64,1792]{1,0:T(8,128)(2,1)S(1)}, bf16[64,1792]{1,0:T(8,128)(2,1)S(1)}, u32[]{:S(2)}, u32[]{:S(2)}) collective-permute-start(bf16[64,1792]{1,0:T(8,128)(2,1)S(1)} %pad_maximum_fusion.1.refs_1_.refs_0_), channel_id=1, source_target_pairs={{0,1},{1,0},{2,3},{3,2},{4,5},{5,4},{6,7},{7,6},{8,9},{9,8},{10,11... | collective-permute-start | bytes 688136 | tf_op jit(solution)/shard_map/ppermute | solution.py:32
  24.1 1.5 %collective-permute-start.7 = (bf16[64,1792]{1,0:T(8,128)(2,1)S(1)}, bf16[64,1792]{1,0:T(8,128)(2,1)S(1)}, u32[]{:S(2)}, u32[]{:S(2)}) collective-permute-start(bf16[64,1792]{1,0:T(8,128)(2,1)S(1)} %collective-permute-done.5.refs_1_), channel_id=1, source_target_pairs={{0,1},{1,0},{2,3},{3,2},{4,5},{5,4},{6,7},{7,6},{8,9},{9,8},{10,11... | collective-permute-start | bytes 688136 | tf_op jit(solution)/shard_map/ppermute | solution.py:32
  24.1 5.0 %collective-permute-start.8 = (bf16[64,2432]{1,0:T(8,128)(2,1)S(1)}, bf16[64,2432]{1,0:T(8,128)(2,1)S(1)}, u32[]{:S(2)}, u32[]{:S(2)}) collective-permute-start(bf16[64,2432]{1,0:T(8,128)(2,1)S(1)} %fusion.1.refs_0_), channel_id=1, source_target_pairs={{0,1},{1,0},{2,3},{3,2},{4,5},{5,4},{6,7},{7,6},{8,9},{9,8},{10,11... | collective-permute-start | bytes 933896 | tf_op jit(solution)/shard_map/ppermute | solution.py:32
  27.5 1.6 %collective-permute-start.9 = (bf16[64,2432]{1,0:T(8,128)(2,1)S(1)}, bf16[64,2432]{1,0:T(8,128)(2,1)S(1)}, u32[]{:S(2)}, u32[]{:S(2)}) collective-permute-start(bf16[64,2432]{1,0:T(8,128)(2,1)S(1)} %collective-permute-done.4.refs_1_), channel_id=1, source_target_pairs={{0,1},{1,0},{2,3},{3,2},{4,5},{5,4},{6,7},{7,6},{8,9},{9,8},{10,11... | collective-permute-start | bytes 933896 | tf_op jit(solution)/shard_map/ppermute | solution.py:32
  35.5 2.5 %collective-permute-start.13 = (bf16[128,2048]{1,0:T(8,128)(2,1)S(1)}, bf16[128,2048]{1,0:T(8,128)(2,1)S(1)}, u32[]{:S(2)}, u32[]{:S(2)}) collective-permute-start(bf16[128,2048]{1,0:T(8,128)(2,1)S(1)} %get-tuple-element.102), channel_id=1, source_target_pairs={{0,1},{1,0},{2,3},{3,2},{4,5},{5,4},{6,7},{7,6},{8,9},{9,8},{10,11... | collective-permute-start | bytes 1572872 | tf_op jit(solution)/shard_map/ppermute | solution.py:32
  37.9 2.0 %collective-permute-start.10 = (bf16[128,2048]{1,0:T(8,128)(2,1)S(1)}, bf16[128,2048]{1,0:T(8,128)(2,1)S(1)}, u32[]{:S(2)}, u32[]{:S(2)}) collective-permute-start(bf16[128,2048]{1,0:T(8,128)(2,1)S(1)} %get-tuple-element.100), channel_id=1, source_target_pairs={{0,1},{1,0},{2,3},{3,2},{4,5},{5,4},{6,7},{7,6},{8,9},{9,8},{10,11... | collective-permute-start | bytes 1572872 | tf_op jit(solution)/shard_map/ppermute | solution.py:32
  38.1 6.4 %collective-permute-start.14 = (bf16[64,2048]{1,0:T(8,128)(2,1)S(1)}, bf16[64,2048]{1,0:T(8,128)(2,1)S(1)}, u32[]{:S(2)}, u32[]{:S(2)}) collective-permute-start(bf16[64,2048]{1,0:T(8,128)(2,1)S(1)} %slice.159), channel_id=1, source_target_pairs={{0,4},{1,3},{2,6},{3,1},{4,0},{5,7},{6,2},{7,5},{8,12},{9,11},{10,... | collective-permute-start | bytes 786440 | tf_op jit(solution)/shard_map/ppermute | solution.py:32
  40.0 7.7 %collective-permute-start.11 = (bf16[64,2048]{1,0:T(8,128)(2,1)S(1)}, bf16[64,2048]{1,0:T(8,128)(2,1)S(1)}, u32[]{:S(2)}, u32[]{:S(2)}) collective-permute-start(bf16[64,2048]{1,0:T(8,128)(2,1)S(1)} %slice.160), channel_id=1, source_target_pairs={{0,4},{1,3},{2,6},{3,1},{4,0},{5,7},{6,2},{7,5},{8,12},{9,11},{10,... | collective-permute-start | bytes 786440 | tf_op jit(solution)/shard_map/ppermute | solution.py:32
  44.6 5.0 %collective-permute-start.15 = (bf16[32,2048]{1,0:T(8,128)(2,1)S(1)}, bf16[32,2048]{1,0:T(8,128)(2,1)S(1)}, u32[]{:S(2)}, u32[]{:S(2)}) collective-permute-start(bf16[32,2048]{1,0:T(8,128)(2,1)S(1)} %slice.161), channel_id=1, source_target_pairs={{0,2},{1,5},{2,0},{3,7},{4,6},{5,1},{6,4},{7,3},{8,10},{9,13},{10,... | collective-permute-start | bytes 393224 | tf_op jit(solution)/shard_map/ppermute | solution.py:32
  47.8 5.0 %collective-permute-start.12 = (bf16[32,2048]{1,0:T(8,128)(2,1)S(1)}, bf16[32,2048]{1,0:T(8,128)(2,1)S(1)}, u32[]{:S(2)}, u32[]{:S(2)}) collective-permute-start(bf16[32,2048]{1,0:T(8,128)(2,1)S(1)} %slice.162), channel_id=1, source_target_pairs={{0,2},{1,5},{2,0},{3,7},{4,6},{5,1},{6,4},{7,3},{8,10},{9,13},{10,... | collective-permute-start | bytes 393224 | tf_op jit(solution)/shard_map/ppermute | solution.py:32
  53.0 5.6 %collective-permute-start.16 = (bf16[8,4096]{1,0:T(8,128)(2,1)S(1)}, bf16[8,4096]{1,0:T(8,128)(2,1)S(1)}, u32[]{:S(2)}, u32[]{:S(2)}) collective-permute-start(bf16[8,4096]{1,0:T(8,128)(2,1)S(1)} %get-tuple-element.103), channel_id=1, source_target_pairs={{0,16},{8,24},{16,0},{24,8},{1,17},{9,25},{17,1},{25,9},{2,18},{10... | collective-permute-start | bytes 196616 | tf_op jit(solution)/shard_map/ppermute | solution.py:32
  53.8 6.2 %collective-permute-start.17 = (bf16[8,4096]{1,0:T(8,128)(2,1)S(1)}, bf16[8,4096]{1,0:T(8,128)(2,1)S(1)}, u32[]{:S(2)}, u32[]{:S(2)}) collective-permute-start(bf16[8,4096]{1,0:T(8,128)(2,1)S(1)} %get-tuple-element.105), channel_id=1, source_target_pairs={{0,8},{8,16},{16,24},{24,0},{1,9},{9,17},{17,25},{25,1},{2,10},{10... | collective-permute-start | bytes 196616 | tf_op jit(solution)/shard_map/ppermute | solution.py:32
  56.7 4.3 %collective-permute-start.18 = (bf16[8,4096]{1,0:T(8,128)(2,1)S(1)}, bf16[8,4096]{1,0:T(8,128)(2,1)S(1)}, u32[]{:S(2)}, u32[]{:S(2)}) collective-permute-start(bf16[8,4096]{1,0:T(8,128)(2,1)S(1)} %get-tuple-element.104), channel_id=1, source_target_pairs={{0,24},{8,0},{16,8},{24,16},{1,25},{9,1},{17,9},{25,17},{2,26},{10... | collective-permute-start | bytes 196616 | tf_op jit(solution)/shard_map/ppermute | solution.py:32

commit v6 on v5

--- a/solution.py
+++ b/solution.py
@@ -207,6 +207,7 @@
     steps = (expert_size // 2).bit_length() - 1
     cut = ROWS_FIRST * hidden // 1536
     every = (0, hidden)
+    block = 2 * LANES if cut % (2 * LANES) == 0 else LANES
     beside = lambda i: i ^ 1
 
     w_gate = w_gate.reshape(hidden, features)
@@ -247,7 +248,7 @@
     pieces = both_of_pair([columns[0], others[0]])
     count = len(pieces)
     rows, gate_a, up_a = pl.pallas_call(
-        lambda *refs: first_kernel(*refs, pieces=count, block=LANES),
+        lambda *refs: first_kernel(*refs, pieces=count, block=block),
         out_shape=[pltpu.VMEM((tokens, AG_CUT), BF16)] + [pltpu.VMEM((tokens, cut), F32)] * 2,
         in_specs=[IN_VMEM] * (count + 2),
         out_specs=[IN_VMEM] * 3,
@@ -256,7 +257,7 @@
     )(*pieces, near(gate_1), near(up_1))
     others[1], rows = lax.optimization_barrier((others[1], rows))
     gate_b, up_b = pl.pallas_call(
-        lambda *refs: middle_kernel(*refs, block=LANES, start=cut),
+        lambda *refs: middle_kernel(*refs, block=block, start=cut),
         out_shape=[pltpu.VMEM((tokens, hidden - cut), F32)] * 2,
         in_specs=[IN_VMEM] * 3,
         out_specs=[IN_VMEM] * 2,
@@ -267,7 +268,7 @@
     starts = [sum(RS_CUTS[:i]) for i in range(len(RS_CUTS))]
     cuts = [(0, (early, hidden - early), (0, features))]
     act, *downs_3 = pl.pallas_call(
-        lambda *refs: second_kernel(*refs, pieces=count, block=LANES, part=rest, cuts=cuts),
+        lambda *refs: second_kernel(*refs, pieces=count, block=block, part=rest, cuts=cuts),
         out_shape=[pltpu.VMEM((tokens, hidden), BF16)] + loaded(cuts),
         in_specs=[IN_VMEM] * (count + 7) + [IN_HBM],
         out_specs=[IN_VMEM] * (1 + len(cuts)),

time: 61.9 us -> 65.1 us (1.052)
  Pallas kernels: 23.3 us -> 26.5 us
    pallas_call x3, Pallas kernels: 7.83 us -> 11.1 us  [the longest x1 7.84 us: local(): pl.pallas_call(lambda *refs: second_kernel(*refs, pieces=count, block=blo...]
  transfers between devices with their start and end apart: 19 -> 19, of which waited for: 13 -> 13; matrix products, arithmetic and copies ran while one was open for 1% -> 1% of each run, Pallas kernels for 26% -> 24%
where the time goes in v6:
time: 65.1 us; the launch traced here: 64.9 us
  Pallas kernels  26.5 us (41%)
  starting transfers between devices  23.4 us (36%)
  waiting for transfers between devices  13.5 us (21%)
  other arithmetic  1.13 us (2%)
    ppermute x19, starting transfers between devices, swap(): lax.ppermute(value, axis, [(i, to(i)) for i in range(lax.axis_size(axis))])  23.4 us
    ppermute x19, waiting for transfers between devices, swap(): lax.ppermute(value, axis, [(i, to(i)) for i in range(lax.axis_size(axis))])  13.5 us
    pallas_call x3, Pallas kernels, load(): pl.pallas_call(lambda *refs: load_kernel(*refs, sources=len(arrays), cuts...  10.9 us
    pallas_call x1, Pallas kernels, local(): pl.pallas_call(lambda *refs: second_kernel(*refs, pieces=count, block=blo...  7.84 us
    pallas_call x2, Pallas kernels, local(): pl.pallas_call(lambda *refs, start=start: down_kernel(*refs, chunk=512, s...  3.57 us
    pallas_call x1, Pallas kernels, local(): pl.pallas_call(lambda *refs: first_kernel(*refs, pieces=count, block=bloc...  1.61 us
    pallas_call x1, Pallas kernels, local(): pl.pallas_call(lambda *refs: middle_kernel(*refs, block=block, start=cut)...  1.61 us
  transfers between devices with their start and end apart: 19, of which 13 were waited for; matrix products, arithmetic and copies ran while one was open for 1% of the time, Pallas kernels for 24%

profile of v6, /device:TPU:0, one launch (start us, length us, event | category | flops | bytes accessed | tf_op | source)
XLA Modules:
  0.0 64.9 jit_solution(7165244901978430997)
XLA Ops:
  0.0 1.0 %shard_map.73 = (bf16[8,4224]{1,0:T(8,128)(2,1)S(1)}, bf16[32,4224]{1,0:T(8,128)(2,1)S(1)}) custom-call(bf16[8,4096]{1,0:T(8,128)(2,1)} %refs_0_.1, bf16[32,128]{1,0:T(8,128)(2,1)} %bitcast.10, s32[8,8]{1,0:T(8,128)} %refs_2_.1, f32[8,8]{1,0:T(8,128)} %refs_3_.1), custom_call_target="tpu_custom_call" | custom-call | tf_op jit(solution)/shard_map/pallas_call | solution.py:217
  1.0 3.1 %collective-permute-start = (bf16[8,4224]{1,0:T(8,128)(2,1)S(1)}, bf16[8,4224]{1,0:T(8,128)(2,1)S(1)}, u32[]{:S(2)}, u32[]{:S(2)}) collective-permute-start(bf16[8,4224]{1,0:T(8,128)(2,1)S(1)} %get-tuple-element.73.refs_2_), channel_id=1, source_target_pairs={{0,8},{8,16},{16,24},{24,0},{1,9},{9,17},{17,25},{25,1},{2,10},{10... | collective-permute-start | bytes 202760 | tf_op jit(solution)/shard_map/ppermute | solution.py:32
  4.1 2.6 %collective-permute-start.1 = (bf16[8,4224]{1,0:T(8,128)(2,1)S(1)}, bf16[8,4224]{1,0:T(8,128)(2,1)S(1)}, u32[]{:S(2)}, u32[]{:S(2)}) collective-permute-start(bf16[8,4224]{1,0:T(8,128)(2,1)S(1)} %get-tuple-element.73.refs_2_), channel_id=1, source_target_pairs={{0,16},{8,24},{16,0},{24,8},{1,17},{9,25},{17,1},{25,9},{2,18},{10... | collective-permute-start | bytes 202760 | tf_op jit(solution)/shard_map/ppermute | solution.py:32
  6.7 1.3 %collective-permute-start.2 = (bf16[8,4224]{1,0:T(8,128)(2,1)S(1)}, bf16[8,4224]{1,0:T(8,128)(2,1)S(1)}, u32[]{:S(2)}, u32[]{:S(2)}) collective-permute-start(bf16[8,4224]{1,0:T(8,128)(2,1)S(1)} %get-tuple-element.73.refs_2_), channel_id=1, source_target_pairs={{0,24},{8,0},{16,8},{24,16},{1,25},{9,1},{17,9},{25,17},{2,26},{10... | collective-permute-start | bytes 202760 | tf_op jit(solution)/shard_map/ppermute | solution.py:32
  8.0 3.3 %shard_map.74 = (bf16[1536,1792]{1,0:T(8,128)(2,1)S(1)}, bf16[256,4096]{1,0:T(8,128)(2,1)S(1)}) custom-call(bf16[1536,4096]{1,0:T(8,128)(2,1)} %bitcast.4, bf16[1536,4096]{1,0:T(8,128)(2,1)} %bitcast.8, bf16[8,4224]{1,0:T(8,128)(2,1)S(1)} %get-tuple-element.73.refs_2_), custom_call_target="tpu_custom_call" | custom-call | tf_op jit(solution)/shard_map/pallas_call | solution.py:113
  11.3 0.0 collective-permute-done
  11.3 0.0 collective-permute-done.1
  11.3 0.1 collective-permute-done.2
  11.5 1.7 %collective-permute-start.3 = (bf16[32,4224]{1,0:T(8,128)(2,1)S(1)}, bf16[32,4224]{1,0:T(8,128)(2,1)S(1)}, u32[]{:S(2)}, u32[]{:S(2)}) collective-permute-start(bf16[32,4224]{1,0:T(8,128)(2,1)S(1)} %constant_dynamic-update-slice_fusion.refs_2_), channel_id=1, source_target_pairs={{0,2},{1,5},{2,0},{3,7},{4,6},{5,1},{6,4},{7,3},{8,10},{9,13},{10,... | collective-permute-start | bytes 811016 | tf_op jit(solution)/shard_map/ppermute | solution.py:32
  13.2 4.6 %shard_map.75 = (bf16[1536,2304]{1,0:T(8,128)(2,1)S(1)}, bf16[1536,1792]{1,0:T(8,128)(2,1)S(1)}) custom-call(bf16[1536,4096]{1,0:T(8,128)(2,1)} %bitcast.5, bf16[1536,4096]{1,0:T(8,128)(2,1)} %bitcast.6, bf16[32,4224]{1,0:T(8,128)(2,1)S(1)} %constant_dynamic-update-slice_fusion.refs_2_), custom_call_target="tpu_custom_call" | custom-call | tf_op jit(solution)/shard_map/pallas_call | solution.py:113
  17.8 0.3 collective-permute-done.3
  18.0 1.7 %collective-permute-start.5 = (bf16[64,1792]{1,0:T(8,128)(2,1)S(1)}, bf16[64,1792]{1,0:T(8,128)(2,1)S(1)}, u32[]{:S(2)}, u32[]{:S(2)}) collective-permute-start(bf16[64,1792]{1,0:T(8,128)(2,1)S(1)} %pad_maximum_fusion.1.refs_1_.refs_0_), channel_id=1, source_target_pairs={{0,4},{1,3},{2,6},{3,1},{4,0},{5,7},{6,2},{7,5},{8,12},{9,11},{10,... | collective-permute-start | bytes 688136 | tf_op jit(solution)/shard_map/ppermute | solution.py:32
  19.8 0.5 collective-permute-start.4
  20.2 3.0 %shard_map.76 = (bf16[1536,2304]{1,0:T(8,128)(2,1)S(1)}, bf16[128,1536]{1,0:T(8,128)(2,1)S(1)}) custom-call(bf16[1536,4096]{1,0:T(8,128)(2,1)} %bitcast.7, bf16[64,1792]{1,0:T(8,128)(2,1)S(1)} %pad_maximum_fusion.1.refs_1_.refs_0_), custom_call_target="tpu_custom_call" | custom-call | tf_op jit(solution)/shard_map/pallas_call | solution.py:113
  23.3 0.1 collective-permute-start.6
  23.3 0.8 %collective-permute-done.5.refs_1_ = bf16[64,1792]{1,0:T(8,128)(2,1)S(1)} collective-permute-done((bf16[64,1792]{1,0:T(8,128)(2,1)S(1)}, bf16[64,1792]{1,0:T(8,128)(2,1)S(1)}, u32[]{:S(2)}, u32[]{:S(2)}) %collective-permute-start.5) | collective-permute-done | bytes 229408 | tf_op jit(solution)/shard_map/ppermute | solution.py:32
  24.1 0.0 collective-permute-start.7
  24.1 0.5 collective-permute-start.8
  24.6 0.2 collective-permute-done.6.refs_2_
  24.8 0.8 %collective-permute-done.7.refs_3_ = bf16[64,1792]{1,0:T(8,128)(2,1)S(1)} collective-permute-done((bf16[64,1792]{1,0:T(8,128)(2,1)S(1)}, bf16[64,1792]{1,0:T(8,128)(2,1)S(1)}, u32[]{:S(2)}, u32[]{:S(2)}) %collective-permute-start.7) | collective-permute-done | bytes 229408 | tf_op jit(solution)/shard_map/ppermute | solution.py:32
  25.6 1.6 %shard_map.77 = (bf16[256,1792]{1,0:T(8,128)(2,1)S(1)}, f32[256,768]{1,0:T(8,128)S(1)}, f32[256,768]{1,0:T(8,128)S(1)}) custom-call(bf16[64,1792]{1,0:T(8,128)(2,1)S(1)} %pad_maximum_fusion.1.refs_1_.refs_0_, bf16[64,1792]{1,0:T(8,128)(2,1)S(1)} %collective-permute-done.5.refs_1_, bf16[64,1792]{1,0:T(8,128)(2,1)S(1)} %collective-permute-done.6.refs_2_, ...), custom_call_target="tpu_custom_call" | custom-call | tf_op jit(solution)/shard_map/pallas_call | solution.py:250
  27.2 0.2 collective-permute-done.4.refs_1_
  27.5 0.0 collective-permute-start.9
  27.5 1.6 %shard_map.78 = (f32[256,768]{1,0:T(8,128)S(1)}, f32[256,768]{1,0:T(8,128)S(1)}) custom-call(bf16[256,1792]{1,0:T(8,128)(2,1)S(1)} %get-tuple-element.92.refs_0_, bf16[1536,1792]{1,0:T(8,128)(2,1)S(1)} %get-tuple-element.84.refs_4_.refs_1_, bf16[1536,1792]{1,0:T(8,128)(2,1)S(1)} %get-tuple-element.85.refs_5_.refs_2_), custom_call_target="tpu_custom_call" | custom-call | tf_op jit(solution)/shard_map/pallas_call | solution.py:259
  29.1 0.0 collective-permute-done.8.refs_2_
  29.1 0.0 collective-permute-done.9.refs_3_
  29.1 7.8 %shard_map.79 = (bf16[256,1536]{1,0:T(8,128)(2,1)S(1)}, bf16[1280,4096]{1,0:T(8,128)(2,1)S(1)}) custom-call(bf16[64,2432]{1,0:T(8,128)(2,1)S(1)} %fusion.1.refs_0_, bf16[64,2432]{1,0:T(8,128)(2,1)S(1)} %collective-permute-done.4.refs_1_, bf16[64,2432]{1,0:T(8,128)(2,1)S(1)} %collective-permute-done.8.refs_2_, ...), custom_call_target="tpu_custom_call" | custom-call | tf_op jit(solution)/shard_map/pallas_call | solution.py:270
  37.0 1.8 %shard_map.81 = (f32[128,2048]{1,0:T(8,128)S(1)}, bf16[128,2048]{1,0:T(8,128)(2,1)S(1)}) custom-call(bf16[256,1536]{1,0:T(8,128)(2,1)S(1)} %get-tuple-element.96.refs_0_, bf16[256,4096]{1,0:T(8,128)(2,1)S(1)} %get-tuple-element.97.refs_1_, bf16[1280,4096]{1,0:T(8,128)(2,1)S(1)} %get-tuple-element.98.refs_2_), custom_call_target="tpu_custom_call" | custom-call | tf_op jit(solution)/shard_map/pallas_call | solution.py:287
  38.8 0.6 collective-permute-start.13
  39.3 1.8 %shard_map.80 = (f32[128,2048]{1,0:T(8,128)S(1)}, bf16[128,2048]{1,0:T(8,128)(2,1)S(1)}) custom-call(bf16[256,1536]{1,0:T(8,128)(2,1)S(1)} %get-tuple-element.96.refs_0_, bf16[256,4096]{1,0:T(8,128)(2,1)S(1)} %get-tuple-element.97.refs_1_, bf16[1280,4096]{1,0:T(8,128)(2,1)S(1)} %get-tuple-element.98.refs_2_), custom_call_target="tpu_custom_call" | custom-call | tf_op jit(solution)/shard_map/pallas_call | solution.py:287
  41.1 0.1 collective-permute-start.10
  41.2 0.0 collective-permute-done.13
  41.2 0.1 convert_add_fusion
  41.4 1.7 %collective-permute-start.14 = (bf16[64,2048]{1,0:T(8,128)(2,1)S(1)}, bf16[64,2048]{1,0:T(8,128)(2,1)S(1)}, u32[]{:S(2)}, u32[]{:S(2)}) collective-permute-start(bf16[64,2048]{1,0:T(8,128)(2,1)S(1)} %slice.159), channel_id=1, source_target_pairs={{0,4},{1,3},{2,6},{3,1},{4,0},{5,7},{6,2},{7,5},{8,12},{9,11},{10,... | collective-permute-start | bytes 786440 | tf_op jit(solution)/shard_map/ppermute | solution.py:32
  43.1 0.0 collective-permute-done.10
  43.1 0.1 convert_add_fusion.1
  43.3 1.7 %collective-permute-start.11 = (bf16[64,2048]{1,0:T(8,128)(2,1)S(1)}, bf16[64,2048]{1,0:T(8,128)(2,1)S(1)}, u32[]{:S(2)}, u32[]{:S(2)}) collective-permute-start(bf16[64,2048]{1,0:T(8,128)(2,1)S(1)} %slice.160), channel_id=1, source_target_pairs={{0,4},{1,3},{2,6},{3,1},{4,0},{5,7},{6,2},{7,5},{8,12},{9,11},{10,... | collective-permute-start | bytes 786440 | tf_op jit(solution)/shard_map/ppermute | solution.py:32
  44.9 2.9 %collective-permute-done.14 = bf16[64,2048]{1,0:T(8,128)(2,1)S(1)} collective-permute-done((bf16[64,2048]{1,0:T(8,128)(2,1)S(1)}, bf16[64,2048]{1,0:T(8,128)(2,1)S(1)}, u32[]{:S(2)}, u32[]{:S(2)}) %collective-permute-start.14) | collective-permute-done | bytes 262176 | tf_op jit(solution)/shard_map/ppermute | solution.py:32
  47.9 1.7 %collective-permute-start.15 = (bf16[32,2048]{1,0:T(8,128)(2,1)S(1)}, bf16[32,2048]{1,0:T(8,128)(2,1)S(1)}, u32[]{:S(2)}, u32[]{:S(2)}) collective-permute-start(bf16[32,2048]{1,0:T(8,128)(2,1)S(1)} %slice.161), channel_id=1, source_target_pairs={{0,2},{1,5},{2,0},{3,7},{4,6},{5,1},{6,4},{7,3},{8,10},{9,13},{10,... | collective-permute-start | bytes 393224 | tf_op jit(solution)/shard_map/ppermute | solution.py:32
  49.5 1.4 %collective-permute-done.11 = bf16[64,2048]{1,0:T(8,128)(2,1)S(1)} collective-permute-done((bf16[64,2048]{1,0:T(8,128)(2,1)S(1)}, bf16[64,2048]{1,0:T(8,128)(2,1)S(1)}, u32[]{:S(2)}, u32[]{:S(2)}) %collective-permute-start.11) | collective-permute-done | bytes 262176 | tf_op jit(solution)/shard_map/ppermute | solution.py:32
  51.0 0.1 slice_add_fusion.1
  51.1 1.7 %collective-permute-start.12 = (bf16[32,2048]{1,0:T(8,128)(2,1)S(1)}, bf16[32,2048]{1,0:T(8,128)(2,1)S(1)}, u32[]{:S(2)}, u32[]{:S(2)}) collective-permute-start(bf16[32,2048]{1,0:T(8,128)(2,1)S(1)} %slice.162), channel_id=1, source_target_pairs={{0,2},{1,5},{2,0},{3,7},{4,6},{5,1},{6,4},{7,3},{8,10},{9,13},{10,... | collective-permute-start | bytes 393224 | tf_op jit(solution)/shard_map/ppermute | solution.py:32
  52.7 0.2 collective-permute-done.15
  52.9 3.2 %collective-permute-done.12 = bf16[32,2048]{1,0:T(8,128)(2,1)S(1)} collective-permute-done((bf16[32,2048]{1,0:T(8,128)(2,1)S(1)}, bf16[32,2048]{1,0:T(8,128)(2,1)S(1)}, u32[]{:S(2)}, u32[]{:S(2)}) %collective-permute-start.12) | collective-permute-done | bytes 131104 | tf_op jit(solution)/shard_map/ppermute | solution.py:32
  56.2 0.9 %collective-permute-start.16 = (bf16[8,4096]{1,0:T(8,128)(2,1)S(1)}, bf16[8,4096]{1,0:T(8,128)(2,1)S(1)}, u32[]{:S(2)}, u32[]{:S(2)}) collective-permute-start(bf16[8,4096]{1,0:T(8,128)(2,1)S(1)} %get-tuple-element.103), channel_id=1, source_target_pairs={{0,16},{8,24},{16,0},{24,8},{1,17},{9,25},{17,1},{25,9},{2,18},{10... | collective-permute-start | bytes 196616 | tf_op jit(solution)/shard_map/ppermute | solution.py:32
  57.1 2.9 %collective-permute-start.17 = (bf16[8,4096]{1,0:T(8,128)(2,1)S(1)}, bf16[8,4096]{1,0:T(8,128)(2,1)S(1)}, u32[]{:S(2)}, u32[]{:S(2)}) collective-permute-start(bf16[8,4096]{1,0:T(8,128)(2,1)S(1)} %get-tuple-element.105), channel_id=1, source_target_pairs={{0,8},{8,16},{16,24},{24,0},{1,9},{9,17},{17,25},{25,1},{2,10},{10... | collective-permute-start | bytes 196616 | tf_op jit(solution)/shard_map/ppermute | solution.py:32
  60.0 0.9 %collective-permute-start.18 = (bf16[8,4096]{1,0:T(8,128)(2,1)S(1)}, bf16[8,4096]{1,0:T(8,128)(2,1)S(1)}, u32[]{:S(2)}, u32[]{:S(2)}) collective-permute-start(bf16[8,4096]{1,0:T(8,128)(2,1)S(1)} %get-tuple-element.104), channel_id=1, source_target_pairs={{0,24},{8,0},{16,8},{24,16},{1,25},{9,1},{17,9},{25,17},{2,26},{10... | collective-permute-start | bytes 196616 | tf_op jit(solution)/shard_map/ppermute | solution.py:32
  60.9 1.0 %collective-permute-done.16 = bf16[8,4096]{1,0:T(8,128)(2,1)S(1)} collective-permute-done((bf16[8,4096]{1,0:T(8,128)(2,1)S(1)}, bf16[8,4096]{1,0:T(8,128)(2,1)S(1)}, u32[]{:S(2)}, u32[]{:S(2)}) %collective-permute-start.16) | collective-permute-done | bytes 65568 | tf_op jit(solution)/shard_map/ppermute | solution.py:32
  61.8 1.5 %collective-permute-done.17 = bf16[8,4096]{1,0:T(8,128)(2,1)S(1)} collective-permute-done((bf16[8,4096]{1,0:T(8,128)(2,1)S(1)}, bf16[8,4096]{1,0:T(8,128)(2,1)S(1)}, u32[]{:S(2)}, u32[]{:S(2)}) %collective-permute-start.17) | collective-permute-done | bytes 65568 | tf_op jit(solution)/shard_map/ppermute | solution.py:32
  63.3 0.9 %collective-permute-done.18 = bf16[8,4096]{1,0:T(8,128)(2,1)S(1)} collective-permute-done((bf16[8,4096]{1,0:T(8,128)(2,1)S(1)}, bf16[8,4096]{1,0:T(8,128)(2,1)S(1)}, u32[]{:S(2)}, u32[]{:S(2)}) %collective-permute-start.18) | collective-permute-done | bytes 65568 | tf_op jit(solution)/shard_map/ppermute | solution.py:32
  64.2 0.7 %fusion.5 = f32[8,4096]{1,0:T(8,128)} fusion(f32[32,2048]{1,0:T(8,128)S(1)} %slice_add_fusion.3, f32[32,2048]{1,0:T(8,128)S(1)} %slice_add_fusion.2, bf16[8,4096]{1,0:T(8,128)(2,1)S(1)} %collective-permute-done.18, bf16[8,4096]{1,0:T(8,128)(2,1)S(1)} %collective-permute-done.17, bf16[8,4096]{1,0:T(8,128)(2,1)S(1)} %collective-permute-done.16), kind=kLoop, calls=%fused_computation.21 | loop fusion | flops 229376 | bytes 851968 | tf_op jit(solution)/shard_map/add | solution.py:301
  (14 shorter events, 0.3 us)
Async XLA Ops:
  1.0 10.3 %collective-permute-start = (bf16[8,4224]{1,0:T(8,128)(2,1)S(1)}, bf16[8,4224]{1,0:T(8,128)(2,1)S(1)}, u32[]{:S(2)}, u32[]{:S(2)}) collective-permute-start(bf16[8,4224]{1,0:T(8,128)(2,1)S(1)} %get-tuple-element.73.refs_2_), channel_id=1, source_target_pairs={{0,8},{8,16},{16,24},{24,0},{1,9},{9,17},{17,25},{25,1},{2,10},{10... | collective-permute-start | bytes 202760 | tf_op jit(solution)/shard_map/ppermute | solution.py:32
  4.1 7.2 %collective-permute-start.1 = (bf16[8,4224]{1,0:T(8,128)(2,1)S(1)}, bf16[8,4224]{1,0:T(8,128)(2,1)S(1)}, u32[]{:S(2)}, u32[]{:S(2)}) collective-permute-start(bf16[8,4224]{1,0:T(8,128)(2,1)S(1)} %get-tuple-element.73.refs_2_), channel_id=1, source_target_pairs={{0,16},{8,24},{16,0},{24,8},{1,17},{9,25},{17,1},{25,9},{2,18},{10... | collective-permute-start | bytes 202760 | tf_op jit(solution)/shard_map/ppermute | solution.py:32
  6.7 4.8 %collective-permute-start.2 = (bf16[8,4224]{1,0:T(8,128)(2,1)S(1)}, bf16[8,4224]{1,0:T(8,128)(2,1)S(1)}, u32[]{:S(2)}, u32[]{:S(2)}) collective-permute-start(bf16[8,4224]{1,0:T(8,128)(2,1)S(1)} %get-tuple-element.73.refs_2_), channel_id=1, source_target_pairs={{0,24},{8,0},{16,8},{24,16},{1,25},{9,1},{17,9},{25,17},{2,26},{10... | collective-permute-start | bytes 202760 | tf_op jit(solution)/shard_map/ppermute | solution.py:32
  11.5 6.5 %collective-permute-start.3 = (bf16[32,4224]{1,0:T(8,128)(2,1)S(1)}, bf16[32,4224]{1,0:T(8,128)(2,1)S(1)}, u32[]{:S(2)}, u32[]{:S(2)}) collective-permute-start(bf16[32,4224]{1,0:T(8,128)(2,1)S(1)} %constant_dynamic-update-slice_fusion.refs_2_), channel_id=1, source_target_pairs={{0,2},{1,5},{2,0},{3,7},{4,6},{5,1},{6,4},{7,3},{8,10},{9,13},{10,... | collective-permute-start | bytes 811016 | tf_op jit(solution)/shard_map/ppermute | solution.py:32
  18.0 6.1 %collective-permute-start.5 = (bf16[64,1792]{1,0:T(8,128)(2,1)S(1)}, bf16[64,1792]{1,0:T(8,128)(2,1)S(1)}, u32[]{:S(2)}, u32[]{:S(2)}) collective-permute-start(bf16[64,1792]{1,0:T(8,128)(2,1)S(1)} %pad_maximum_fusion.1.refs_1_.refs_0_), channel_id=1, source_target_pairs={{0,4},{1,3},{2,6},{3,1},{4,0},{5,7},{6,2},{7,5},{8,12},{9,11},{10,... | collective-permute-start | bytes 688136 | tf_op jit(solution)/shard_map/ppermute | solution.py:32
  19.8 7.7 %collective-permute-start.4 = (bf16[64,2432]{1,0:T(8,128)(2,1)S(1)}, bf16[64,2432]{1,0:T(8,128)(2,1)S(1)}, u32[]{:S(2)}, u32[]{:S(2)}) collective-permute-start(bf16[64,2432]{1,0:T(8,128)(2,1)S(1)} %fusion.1.refs_0_), channel_id=1, source_target_pairs={{0,4},{1,3},{2,6},{3,1},{4,0},{5,7},{6,2},{7,5},{8,12},{9,11},{10,... | collective-permute-start | bytes 933896 | tf_op jit(solution)/shard_map/ppermute | solution.py:32
  23.3 1.6 %collective-permute-start.6 = (bf16[64,1792]{1,0:T(8,128)(2,1)S(1)}, bf16[64,1792]{1,0:T(8,128)(2,1)S(1)}, u32[]{:S(2)}, u32[]{:S(2)}) collective-permute-start(bf16[64,1792]{1,0:T(8,128)(2,1)S(1)} %pad_maximum_fusion.1.refs_1_.refs_0_), channel_id=1, source_target_pairs={{0,1},{1,0},{2,3},{3,2},{4,5},{5,4},{6,7},{7,6},{8,9},{9,8},{10,11... | collective-permute-start | bytes 688136 | tf_op jit(solution)/shard_map/ppermute | solution.py:32
  24.1 1.5 %collective-permute-start.7 = (bf16[64,1792]{1,0:T(8,128)(2,1)S(1)}, bf16[64,1792]{1,0:T(8,128)(2,1)S(1)}, u32[]{:S(2)}, u32[]{:S(2)}) collective-permute-start(bf16[64,1792]{1,0:T(8,128)(2,1)S(1)} %collective-permute-done.5.refs_1_), channel_id=1, source_target_pairs={{0,1},{1,0},{2,3},{3,2},{4,5},{5,4},{6,7},{7,6},{8,9},{9,8},{10,11... | collective-permute-start | bytes 688136 | tf_op jit(solution)/shard_map/ppermute | solution.py:32
  24.1 5.0 %collective-permute-start.8 = (bf16[64,2432]{1,0:T(8,128)(2,1)S(1)}, bf16[64,2432]{1,0:T(8,128)(2,1)S(1)}, u32[]{:S(2)}, u32[]{:S(2)}) collective-permute-start(bf16[64,2432]{1,0:T(8,128)(2,1)S(1)} %fusion.1.refs_0_), channel_id=1, source_target_pairs={{0,1},{1,0},{2,3},{3,2},{4,5},{5,4},{6,7},{7,6},{8,9},{9,8},{10,11... | collective-permute-start | bytes 933896 | tf_op jit(solution)/shard_map/ppermute | solution.py:32
  27.5 1.6 %collective-permute-start.9 = (bf16[64,2432]{1,0:T(8,128)(2,1)S(1)}, bf16[64,2432]{1,0:T(8,128)(2,1)S(1)}, u32[]{:S(2)}, u32[]{:S(2)}) collective-permute-start(bf16[64,2432]{1,0:T(8,128)(2,1)S(1)} %collective-permute-done.4.refs_1_), channel_id=1, source_target_pairs={{0,1},{1,0},{2,3},{3,2},{4,5},{5,4},{6,7},{7,6},{8,9},{9,8},{10,11... | collective-permute-start | bytes 933896 | tf_op jit(solution)/shard_map/ppermute | solution.py:32
  38.8 2.4 %collective-permute-start.13 = (bf16[128,2048]{1,0:T(8,128)(2,1)S(1)}, bf16[128,2048]{1,0:T(8,128)(2,1)S(1)}, u32[]{:S(2)}, u32[]{:S(2)}) collective-permute-start(bf16[128,2048]{1,0:T(8,128)(2,1)S(1)} %get-tuple-element.102), channel_id=1, source_target_pairs={{0,1},{1,0},{2,3},{3,2},{4,5},{5,4},{6,7},{7,6},{8,9},{9,8},{10,11... | collective-permute-start | bytes 1572872 | tf_op jit(solution)/shard_map/ppermute | solution.py:32
  41.1 2.0 %collective-permute-start.10 = (bf16[128,2048]{1,0:T(8,128)(2,1)S(1)}, bf16[128,2048]{1,0:T(8,128)(2,1)S(1)}, u32[]{:S(2)}, u32[]{:S(2)}) collective-permute-start(bf16[128,2048]{1,0:T(8,128)(2,1)S(1)} %get-tuple-element.100), channel_id=1, source_target_pairs={{0,1},{1,0},{2,3},{3,2},{4,5},{5,4},{6,7},{7,6},{8,9},{9,8},{10,11... | collective-permute-start | bytes 1572872 | tf_op jit(solution)/shard_map/ppermute | solution.py:32
  41.4 6.4 %collective-permute-start.14 = (bf16[64,2048]{1,0:T(8,128)(2,1)S(1)}, bf16[64,2048]{1,0:T(8,128)(2,1)S(1)}, u32[]{:S(2)}, u32[]{:S(2)}) collective-permute-start(bf16[64,2048]{1,0:T(8,128)(2,1)S(1)} %slice.159), channel_id=1, source_target_pairs={{0,4},{1,3},{2,6},{3,1},{4,0},{5,7},{6,2},{7,5},{8,12},{9,11},{10,... | collective-permute-start | bytes 786440 | tf_op jit(solution)/shard_map/ppermute | solution.py:32
  43.3 7.7 %collective-permute-start.11 = (bf16[64,2048]{1,0:T(8,128)(2,1)S(1)}, bf16[64,2048]{1,0:T(8,128)(2,1)S(1)}, u32[]{:S(2)}, u32[]{:S(2)}) collective-permute-start(bf16[64,2048]{1,0:T(8,128)(2,1)S(1)} %slice.160), channel_id=1, source_target_pairs={{0,4},{1,3},{2,6},{3,1},{4,0},{5,7},{6,2},{7,5},{8,12},{9,11},{10,... | collective-permute-start | bytes 786440 | tf_op jit(solution)/shard_map/ppermute | solution.py:32
  47.9 5.0 %collective-permute-start.15 = (bf16[32,2048]{1,0:T(8,128)(2,1)S(1)}, bf16[32,2048]{1,0:T(8,128)(2,1)S(1)}, u32[]{:S(2)}, u32[]{:S(2)}) collective-permute-start(bf16[32,2048]{1,0:T(8,128)(2,1)S(1)} %slice.161), channel_id=1, source_target_pairs={{0,2},{1,5},{2,0},{3,7},{4,6},{5,1},{6,4},{7,3},{8,10},{9,13},{10,... | collective-permute-start | bytes 393224 | tf_op jit(solution)/shard_map/ppermute | solution.py:32
  51.1 5.0 %collective-permute-start.12 = (bf16[32,2048]{1,0:T(8,128)(2,1)S(1)}, bf16[32,2048]{1,0:T(8,128)(2,1)S(1)}, u32[]{:S(2)}, u32[]{:S(2)}) collective-permute-start(bf16[32,2048]{1,0:T(8,128)(2,1)S(1)} %slice.162), channel_id=1, source_target_pairs={{0,2},{1,5},{2,0},{3,7},{4,6},{5,1},{6,4},{7,3},{8,10},{9,13},{10,... | collective-permute-start | bytes 393224 | tf_op jit(solution)/shard_map/ppermute | solution.py:32
  56.2 5.6 %collective-permute-start.16 = (bf16[8,4096]{1,0:T(8,128)(2,1)S(1)}, bf16[8,4096]{1,0:T(8,128)(2,1)S(1)}, u32[]{:S(2)}, u32[]{:S(2)}) collective-permute-start(bf16[8,4096]{1,0:T(8,128)(2,1)S(1)} %get-tuple-element.103), channel_id=1, source_target_pairs={{0,16},{8,24},{16,0},{24,8},{1,17},{9,25},{17,1},{25,9},{2,18},{10... | collective-permute-start | bytes 196616 | tf_op jit(solution)/shard_map/ppermute | solution.py:32
  57.1 6.2 %collective-permute-start.17 = (bf16[8,4096]{1,0:T(8,128)(2,1)S(1)}, bf16[8,4096]{1,0:T(8,128)(2,1)S(1)}, u32[]{:S(2)}, u32[]{:S(2)}) collective-permute-start(bf16[8,4096]{1,0:T(8,128)(2,1)S(1)} %get-tuple-element.105), channel_id=1, source_target_pairs={{0,8},{8,16},{16,24},{24,0},{1,9},{9,17},{17,25},{25,1},{2,10},{10... | collective-permute-start | bytes 196616 | tf_op jit(solution)/shard_map/ppermute | solution.py:32
  60.0 4.3 %collective-permute-start.18 = (bf16[8,4096]{1,0:T(8,128)(2,1)S(1)}, bf16[8,4096]{1,0:T(8,128)(2,1)S(1)}, u32[]{:S(2)}, u32[]{:S(2)}) collective-permute-start(bf16[8,4096]{1,0:T(8,128)(2,1)S(1)} %get-tuple-element.104), channel_id=1, source_target_pairs={{0,24},{8,0},{16,8},{24,16},{1,25},{9,1},{17,9},{25,17},{2,26},{10... | collective-permute-start | bytes 196616 | tf_op jit(solution)/shard_map/ppermute | solution.py:32
